TPU v7x, 512 devices: a whole 4x4x16 slice. The times are simulated.
512 devices in a mesh: rows: 32 (over z, core), tp: 4 (over x), attn: 4 (over y).
Axes of the slice: x: 4, y: 4, z: 16, core: 2. Of those that a mesh axis runs over, the one named last changes fastest.
Arguments:
- tokens: bfloat16 [65536, 4096], P(('rows', 'attn')), may hold values from -60 to 60, as said below
- norm_gain: bfloat16 [4096], replicated, may hold values from 0.099609375 to 1.8984375
- w_query: bfloat16 [4096, 2048], P('rows', 'tp'), may hold values from -1 to 1, as said below
- key_projection_weight: bfloat16 [4096, 512], P('rows', 'tp'), may hold values from -8 to 8, as said below
- value_projection_weight: bfloat16 [4096, 512], P('rows', 'tp'), may hold values from -0.09375 to 0.09375
- documents: int32 [32, 2048], P('rows'), may hold values from 0 to 5, never falling along the last dimension, each value on 1 to 1024 neighbouring positions
Outputs:
- attn_out: bfloat16 [65536, 2048], P(('rows', 'attn'), 'tp')
Inputs may be any that keep to these rules, and one draw needn't show every extreme that they name: `tokens`: activations of order one. `w_query`: entries of order 4096 ** -0.5. `key_projection_weight`: entries of order one or smaller. `documents`: along each window the document numbers never fall; every document spans 1 to 1024 tokens and some document of each window spans exactly 1024.
All inputs are finite; a program needn't handle non-finite values.
Results may differ from a plain program's by a relative error of at most 0.012.
The roundings to bfloat16 on the way count: a program that leaves them out, or rounds other values in their place, can miss the bound.
Values may be sent and summed in bfloat16 or wider, within the bound.
No kernel may reach another device: no remote copies, remote signals or barrier semaphores. Data moves between devices by JAX's collectives and lax.ppermute only.
A program may use at most 64 MiB of HBM per device.

v0:
```python
import math

import jax
import jax.numpy as jnp
from jax import lax
from jax.sharding import PartitionSpec as P

HEAD_SIZE = 128


def rotary(vectors, positions):
    head_dim = vectors.shape[-1]
    half_dim = head_dim // 2
    frequency = jnp.exp(
        jnp.arange(half_dim, dtype=jnp.float32) * (-2.0 * math.log(500000.0) / head_dim)
    )
    angles = positions.astype(jnp.float32)[:, None] * frequency[None, :]
    cosine_table = jnp.cos(angles)[:, None, :]
    sine_table = jnp.sin(angles)[:, None, :]
    first_half = vectors[..., :half_dim]
    second_half = vectors[..., half_dim:]
    return jnp.concatenate(
        [
            first_half * cosine_table - second_half * sine_table,
            second_half * cosine_table + first_half * sine_table,
        ],
        axis=-1,
    )


def attend(query_piece, first_row, keys_window, values_window, doc_ids, kv_heads, head_dim):
    piece_rows = query_piece.shape[0]
    group_width = query_piece.shape[1] // (kv_heads * head_dim)
    grouped_heads = query_piece.reshape(piece_rows, kv_heads, group_width, head_dim)
    query_docs = lax.dynamic_slice_in_dim(doc_ids, first_row, piece_rows)
    query_pos = first_row + jnp.arange(piece_rows, dtype=jnp.int32)
    doc_begin = jnp.sum((doc_ids < query_docs[0]).astype(jnp.int32))
    block_low = doc_begin // piece_rows
    block_high = first_row // piece_rows + 1
    score_scale = 1.0 / math.sqrt(head_dim)

    def visit_block(block_index, carry):
        run_max, run_sum, run_acc = carry
        block_start = block_index * piece_rows
        key_block = lax.dynamic_slice_in_dim(keys_window, block_start, piece_rows, 0).reshape(
            piece_rows, kv_heads, head_dim
        )
        value_block = lax.dynamic_slice_in_dim(values_window, block_start, piece_rows, 0).reshape(
            piece_rows, kv_heads, head_dim
        )
        key_docs = lax.dynamic_slice_in_dim(doc_ids, block_start, piece_rows)
        key_pos = block_start + jnp.arange(piece_rows, dtype=jnp.int32)
        visible = (query_docs[:, None] == key_docs[None, :]) & (
            query_pos[:, None] >= key_pos[None, :]
        )
        scores = (
            jnp.einsum(
                "pcgd,jcd->cgpj", grouped_heads, key_block, preferred_element_type=jnp.float32
            )
            * score_scale
        )
        scores = jnp.where(visible, scores, -1e30)
        new_max = jnp.maximum(run_max, jnp.max(scores, axis=-1))
        factor = jnp.exp(run_max - new_max)
        weights = jnp.where(visible, jnp.exp(scores - new_max[..., None]), 0.0)
        run_sum = run_sum * factor + jnp.sum(weights, axis=-1)
        run_acc = run_acc * factor[..., None] + jnp.einsum(
            "cgpj,jcd->cgpd",
            weights.astype(jnp.bfloat16),
            value_block,
            preferred_element_type=jnp.float32,
        )
        return (new_max, run_sum, run_acc)

    initial = (
        jnp.full((kv_heads, group_width, piece_rows), -1e30, jnp.float32),
        jnp.zeros((kv_heads, group_width, piece_rows), jnp.float32),
        jnp.zeros((kv_heads, group_width, piece_rows, head_dim), jnp.float32),
    )
    run_max, run_sum, run_acc = lax.fori_loop(block_low, block_high, visit_block, initial)
    mixed_out = run_acc / run_sum[..., None]
    return (
        jnp.transpose(mixed_out, (2, 0, 1, 3))
        .reshape(piece_rows, kv_heads * group_width * head_dim)
        .astype(jnp.bfloat16)
    )


def on_device(
    tokens, norm_gain, w_query, key_projection_weight, value_projection_weight, documents
):
    tok_rows = tokens.shape[0]
    query_width = w_query.shape[1]
    kv_width = key_projection_weight.shape[1]
    widened = tokens.astype(jnp.float32)
    mean_sq = jnp.mean(widened * widened, axis=-1, keepdims=True)
    normalized_input = (
        widened * lax.rsqrt(mean_sq + 1e-05) * norm_gain.astype(jnp.float32)
    ).astype(jnp.bfloat16)

    def add_rows(shard_block):
        return jnp.dot(normalized_input, shard_block, preferred_element_type=jnp.float32)

    my_index = lax.axis_index("attn")
    attn_size = lax.axis_size("attn")
    query_proj = add_rows(lax.all_gather(w_query, "rows", axis=0, tiled=True))
    key_projected = add_rows(lax.all_gather(key_projection_weight, "rows", axis=0, tiled=True))
    value_proj = add_rows(lax.all_gather(value_projection_weight, "rows", axis=0, tiled=True))
    positions = my_index * tok_rows + jnp.arange(tok_rows, dtype=jnp.int32)
    query_vectors_all = (
        rotary(query_proj.reshape(tok_rows, query_width // HEAD_SIZE, HEAD_SIZE), positions)
        .reshape(tok_rows, query_width)
        .astype(jnp.bfloat16)
    )
    keys_local = (
        rotary(key_projected.reshape(tok_rows, kv_width // HEAD_SIZE, HEAD_SIZE), positions)
        .reshape(tok_rows, kv_width)
        .astype(jnp.bfloat16)
    )
    values_local = value_proj.astype(jnp.bfloat16)
    keys_window, values_window = (
        lax.all_gather(keys_local, "attn", axis=0, tiled=True),
        lax.all_gather(values_local, "attn", axis=0, tiled=True),
    )
    doc_ids = documents[0]
    piece_rows = tok_rows // attn_size
    kv_heads = kv_width // HEAD_SIZE
    results = []
    for piece_index in range(attn_size):
        first_row = my_index * tok_rows + piece_index * piece_rows
        query_piece = query_vectors_all[piece_index * piece_rows : (piece_index + 1) * piece_rows]
        results.append(
            attend(query_piece, first_row, keys_window, values_window, doc_ids, kv_heads, HEAD_SIZE)
        )
    return jnp.concatenate(results, axis=0)


def solution(mesh):
    placed = (
        P(("rows", "attn"), None),
        P(),
        P("rows", "tp"),
        P("rows", "tp"),
        P("rows", "tp"),
        P("rows", None),
    )
    return jax.shard_map(
        on_device, mesh=mesh, in_specs=placed, out_specs=P(("rows", "attn"), "tp"), check_vma=False
    )
```

profile of v0, /device:TPU:179, one launch (start us, length us, event | category | flops | bytes accessed | tf_op | source)
XLA Modules:
  0.0 287.7 jit_solution(9726449319295346139)
XLA Ops:
  6.5 0.7 all-gather.5.cloned.1.call-update
  7.3 0.7 all-gather.9.cloned.1.call-update
  8.1 0.7 all-gather.7.cloned.1.call-update
  8.7 0.7 constant_dynamic-slice_fusion.2
  9.5 1.4 convert_reduce_fusion.3
  20.6 0.7 convert_element_type.88
  21.3 3.1 %fusion.84 = f32[512]{0:T(512)S(1)} fusion(bf16[512,4096]{1,0:T(8,128)(2,1)} %param.14), kind=kLoop, calls=%fused_computation.114 | loop fusion | flops 6290944 | bytes 4196352 | tf_op jit(solution)/shard_map/reduce_sum | solution.py:96
  24.4 1.8 multiply_cosine_fusion
  26.2 53.7 %all-gather.5.cloned.1.call-done = bf16[4096,128]{1,0:T(8,128)(2,1)} async-done(((bf16[128,128]{1,0:T(8,128)(2,1)}), bf16[4096,128]{1,0:T(8,128)(2,1)}) %all-gather.5.cloned.1.call-update) | async-done | bytes 1048592 | tf_op jit(solution)/shard_map/all_gather | solution.py:107
  79.9 4.1 %convolution_bitcast_fusion.4 = f32[512,1,128]{0,2,1:T(8,128)S(1)} fusion(bf16[4096,128]{1,0:T(8,128)(2,1)} %all-gather.5.cloned.1.call-done, bf16[512,4096]{1,0:T(8,128)(2,1)} %param.14, f32[4096]{0:T(1024)S(1)} %convert_element_type.88, f32[512]{0:T(512)S(1)} %add_rsqrt_fusion), kind=kOutput, calls=%fused_computation.117 | convolution fusion | flops 545259520 | bytes 5523456 | tf_op jit(solution)/shard_map/dot_general | solution.py:102
  84.0 0.6 fusion.92
  84.6 9.6 %all-gather = bf16[2048,1,128]{0,2,1:T(8,128)(2,1)S(1)} all-gather(bf16[512,1,128]{0,2,1:T(8,128)(2,1)S(1)} %pad_maximum_fusion.2), channel_id=2, replica_groups=mesh['rows'=32,'tp'=4,'attn'=4] {'attn'}, dimensions={0}, use_global_device_ids=true | all-gather | bytes 655360 | tf_op jit(solution)/shard_map/all_gather | solution.py:122
  94.4 55.4 %all-gather.9.cloned.1.call-done = bf16[4096,128]{1,0:T(8,128)(2,1)} async-done(((bf16[128,128]{1,0:T(8,128)(2,1)}), bf16[4096,128]{1,0:T(8,128)(2,1)}) %all-gather.9.cloned.1.call-update) | async-done | bytes 1048592 | tf_op jit(solution)/shard_map/all_gather | solution.py:108
  149.9 3.8 %convolution_convert_fusion = bf16[512,128]{1,0:T(8,128)(2,1)S(1)} fusion(bf16[4096,128]{1,0:T(8,128)(2,1)} %all-gather.9.cloned.1.call-done, bf16[512,4096]{1,0:T(8,128)(2,1)} %param.14, f32[4096]{0:T(1024)S(1)} %convert_element_type.88, f32[512]{0:T(512)S(1)} %add_rsqrt_fusion), kind=kOutput, calls=%fused_computation.118 | convolution fusion | flops 545325056 | bytes 5392384 | tf_op jit(solution)/shard_map/dot_general | solution.py:102
  153.6 9.5 %all_gather.19 = bf16[2048,128]{1,0:T(8,128)(2,1)S(1)} all-gather(bf16[512,128]{1,0:T(8,128)(2,1)S(1)} %convolution_convert_fusion), channel_id=1, replica_groups=mesh['rows'=32,'tp'=4,'attn'=4] {'attn'}, dimensions={0}, use_global_device_ids=true | all-gather | bytes 655360 | tf_op jit(solution)/shard_map/all_gather | solution.py:123
  163.2 60.2 %all-gather.7.cloned.1.call-done = bf16[4096,512]{1,0:T(8,128)(2,1)} async-done(((bf16[128,512]{1,0:T(8,128)(2,1)}), bf16[4096,512]{1,0:T(8,128)(2,1)}) %all-gather.7.cloned.1.call-update) | async-done | bytes 4194320 | tf_op jit(solution)/shard_map/all_gather | solution.py:106
  223.4 5.9 %fusion.107 = f32[512,512]{0,1:T(8,128)S(1)} fusion(bf16[4096,512]{1,0:T(8,128)(2,1)} %all-gather.7.cloned.1.call-done, bf16[512,4096]{1,0:T(8,128)(2,1)} %param.14, f32[4096]{0:T(1024)S(1)} %convert_element_type.88, f32[512]{0:T(512)S(1)} %add_rsqrt_fusion), kind=kOutput, calls=%fused_computation.172 | convolution fusion | flops 2155872256 | bytes 9455616 | tf_op jit(solution)/shard_map/dot_general | solution.py:102
  229.3 0.9 fusion.114
  230.2 0.3 copy.25
  230.5 1.4 copy.26
  231.9 1.2 subtract_convert_fusion
  233.2 0.3 fusion.98
  233.5 9.1 %while.60 = (s32[]{:T(128)}, f32[1,4,128]{2,1,0:T(4,128)S(1)}, f32[1,4,128]{2,1,0:T(4,128)S(1)}, f32[1,4,128,128]{3,2,1,0:T(8,128)S(1)}, s32[]{:T(128)}, /*index...) while((s32[]{:T(128)}, f32[1,4,128]{2,1,0:T(4,128)S(1)}, ...), condition=%wide.region_5.6_spmd.clone, body=%wide.region_2.5_spmd.clone.sunk | while | flops 34326276 | bytes 1609935 | solution.py:80
  233.5 0.8 dynamic_slice.134
  235.1 0.8 dynamic_slice.134
  236.2 0.3 fusion.147
  236.6 0.8 dynamic_slice.134
  238.1 0.8 dynamic_slice.134
  239.6 0.8 dynamic_slice.134
  240.7 0.3 fusion.147
  241.1 0.8 dynamic_slice.134
  242.9 10.6 %while.61 = (s32[]{:T(128)}, f32[1,4,128]{2,1,0:T(4,128)S(1)}, f32[1,4,128]{2,1,0:T(4,128)S(1)}, f32[1,4,128,128]{3,2,1,0:T(8,128)S(1)}, s32[]{:T(128)}, /*index...) while((s32[]{:T(128)}, f32[1,4,128]{2,1,0:T(4,128)S(1)}, ...), condition=%wide.region_10.11_spmd.clone, body=%wide.region_7.10_spmd.clone.sunk | while | flops 34326276 | bytes 1609935 | solution.py:80
  243.0 0.8 dynamic_slice.137
  244.1 0.3 fusion.153
  244.5 0.8 dynamic_slice.137
  246.0 0.8 dynamic_slice.137
  247.5 0.8 dynamic_slice.137
  248.6 0.3 fusion.153
  249.0 0.8 dynamic_slice.137
  250.6 0.8 dynamic_slice.137
  252.1 0.8 dynamic_slice.137
  253.9 12.2 %while.62 = (s32[]{:T(128)}, f32[1,4,128]{2,1,0:T(4,128)S(1)}, f32[1,4,128]{2,1,0:T(4,128)S(1)}, f32[1,4,128,128]{3,2,1,0:T(8,128)S(1)}, s32[]{:T(128)}, /*index...) while((s32[]{:T(128)}, f32[1,4,128]{2,1,0:T(4,128)S(1)}, ...), condition=%wide.region_15.16_spmd.clone, body=%wide.region_12.15_spmd.clone.sunk | while | flops 34326276 | bytes 1609935 | solution.py:80
  253.9 0.8 dynamic_slice.140
  255.4 0.8 dynamic_slice.140
  257.0 0.8 dynamic_slice.140
  258.1 0.3 fusion.159
  258.5 0.8 dynamic_slice.140
  260.0 0.8 dynamic_slice.140
  261.5 0.8 dynamic_slice.140
  263.0 0.8 dynamic_slice.140
  264.6 0.8 dynamic_slice.140
  266.4 13.7 %while.63 = (s32[]{:T(128)}, f32[1,4,128]{2,1,0:T(4,128)S(1)}, f32[1,4,128]{2,1,0:T(4,128)S(1)}, f32[1,4,128,128]{3,2,1,0:T(8,128)S(1)}, s32[]{:T(128)}, /*index...) while((s32[]{:T(128)}, f32[1,4,128]{2,1,0:T(4,128)S(1)}, ...), condition=%wide.region_20.21_spmd.clone, body=%wide.region_17.20_spmd.clone.sunk | while | flops 34326276 | bytes 1609935 | solution.py:80
  266.4 0.8 dynamic_slice.143
  267.9 0.8 dynamic_slice.143
  269.4 0.8 dynamic_slice.143
  270.9 0.8 dynamic_slice.143
  272.5 0.8 dynamic_slice.143
  273.6 0.3 fusion.165
  274.0 0.8 dynamic_slice.143
  275.5 0.8 dynamic_slice.143
  277.0 0.8 dynamic_slice.143
  278.5 0.8 dynamic_slice.143
  279.6 0.3 fusion.165
  280.4 0.8 pad_maximum_fusion
  (263 shorter events, 20.3 us)
Async XLA Ops:
  6.5 73.4 %all-gather.5.cloned.1.call-start = ((), (), s32[]{:S(2)}) async-start(), calls=%async_computation | async-start | bytes 1081344 | tf_op jit(solution)/shard_map/all_gather | solution.py:107
  7.3 142.6 %all-gather.9.cloned.1.call-start = ((), (), s32[]{:S(2)}) async-start(), calls=%async_computation.2 | async-start | bytes 1081344 | tf_op jit(solution)/shard_map/all_gather | solution.py:108
  8.0 215.4 %all-gather.7.cloned.1.call-start = ((), (), s32[]{:S(2)}) async-start(), calls=%async_computation.1 | async-start | bytes 4325376 | tf_op jit(solution)/shard_map/all_gather | solution.py:106
Sparse Core Ops, SparseCore 0:
  9.5 70.3 all-gather.4
  82.0 67.8 all-gather.8
  152.0 71.3 all-gather.6
where the time goes:
time: 289 us; the launch traced here: 288 us
  waiting for transfers between devices  171 us (59%)
  matrix products  28.6 us (10%)
  local copies, waits for them, and re-layouts  27.1 us (9%)
  between operations  23.1 us (8%)
  blocking collectives  19.1 us (7%)
  other arithmetic  16.4 us (6%)
    all_gather x1, waiting for transfers between devices, on_device(): query_proj = add_rows(lax.all_gather(w_query, 'rows', axis=0, tiled=True))  60.2 us
    all_gather x1, waiting for transfers between devices, on_device(): lax.all_gather(value_projection_weight, 'rows', axis=0, tiled=True)  55.4 us
    all_gather x1, waiting for transfers between devices, on_device(): lax.all_gather(key_projection_weight, 'rows', axis=0, tiled=True)  53.7 us
    dynamic_slice x30, local copies, waits for them, and re-layouts, visit_block(): key_docs = lax.dynamic_slice_in_dim(doc_ids, block_start, piece_rows)  22.9 us
    dot_general x3, matrix products, add_rows(): jnp.dot(normalized_input, shard_block, preferred_element_type=jnp.float32)  13.8 us
    all_gather x1, blocking collectives, on_device(): lax.all_gather(keys_local, 'attn', axis=0, tiled=True)  9.56 us
    all_gather x1, blocking collectives, on_device(): lax.all_gather(values_local, 'attn', axis=0, tiled=True)  9.54 us
    dot_general x30, matrix products, visit_block(): jnp.einsum('cgpj,jcd->cgpd', weights.astype(jnp.bfloat16), value_block, p...  8.53 us
  transfers between devices with their start and end apart: 3, of which 3 were waited for; matrix products, arithmetic and copies ran while one was open for 6% of the time, Pallas kernels for 0%

commit v1 on v0

v1 whole, which is shorter than its diff:
```python
import functools
import math

import jax
import jax.numpy as jnp
from jax import lax
from jax.experimental import pallas as pl
from jax.experimental.pallas import tpu as pltpu
from jax.sharding import PartitionSpec as P

HEAD_SIZE = 128
KEY_BLOCK = 256
QUERY_BLOCK = 128


def rotary_tables(positions):
    half_dim = HEAD_SIZE // 2
    frequency = jnp.exp(
        jnp.arange(half_dim, dtype=jnp.float32) * (-2.0 * math.log(500000.0) / HEAD_SIZE)
    )
    angles = positions.astype(jnp.float32)[:, None] * frequency[None, :]
    cosine, sine = jnp.cos(angles), jnp.sin(angles)
    return jnp.concatenate([cosine, cosine], 1), jnp.concatenate([-sine, sine], 1)


def project_kernel(rotated_heads, x_ref, w_ref, cos_ref, sin_ref, out_ref, acc_ref):
    step = pl.program_id(0)
    part = jnp.dot(x_ref[...], w_ref[...], preferred_element_type=jnp.float32)

    @pl.when(step == 0)
    def _():
        acc_ref[...] = part

    @pl.when(step > 0)
    def _():
        acc_ref[...] += part

    @pl.when(step == pl.num_programs(0) - 1)
    def _():
        for head in range(out_ref.shape[1] // HEAD_SIZE):
            lanes = slice(head * HEAD_SIZE, (head + 1) * HEAD_SIZE)
            u = acc_ref[:, lanes]
            if head < rotated_heads:
                u = u * cos_ref[...] + pltpu.roll(u, HEAD_SIZE // 2, 1) * sin_ref[...]
            out_ref[:, lanes] = u.astype(jnp.bfloat16)


def project(x, w, cosine, sine, rotated_heads, steps=4):
    rows, depth = x.shape
    width = w.shape[1]
    chunk = depth // steps
    return pl.pallas_call(
        functools.partial(project_kernel, rotated_heads),
        grid=(steps,),
        in_specs=[
            pl.BlockSpec((rows, chunk), lambda s: (0, s)),
            pl.BlockSpec((chunk, width), lambda s: (s, 0)),
            pl.BlockSpec((rows, HEAD_SIZE), lambda s: (0, 0)),
            pl.BlockSpec((rows, HEAD_SIZE), lambda s: (0, 0)),
        ],
        out_specs=pl.BlockSpec((rows, width), lambda s: (0, 0)),
        out_shape=jax.ShapeDtypeStruct((rows, width), jnp.bfloat16),
        scratch_shapes=[pltpu.VMEM((rows, width), jnp.float32)],
        compiler_params=pltpu.CompilerParams(vmem_limit_bytes=32 * 1024 * 1024),
        cost_estimate=pl.CostEstimate(
            flops=2 * rows * depth * width,
            bytes_accessed=2 * (rows * depth + depth * width + rows * width),
            transcendentals=0,
        ),
    )(x, w, cosine, sine)


def attend_kernel(first_ref, q_ref, low_ref, kv2_ref, kv1_ref, kv0_ref, out_ref, kv, sems):
    step = pl.program_id(0)
    rows = kv0_ref.shape[0]
    sources = (kv2_ref, kv1_ref, kv0_ref)

    @pl.when(step == 0)
    def _():
        copies = [
            pltpu.make_async_copy(src, kv.at[pl.ds(n * rows, rows)], sems.at[n])
            for n, src in enumerate(sources)
        ]
        for copy in copies:
            copy.start()
        for copy in copies:
            copy.wait()

    heads = q_ref.shape[1] // HEAD_SIZE
    block = q_ref.shape[0]
    q = jnp.concatenate(
        [q_ref[:, h * HEAD_SIZE : (h + 1) * HEAD_SIZE] for h in range(heads)], axis=0
    )
    low = low_ref[...]
    first_query = 2 * rows + step * block
    query_at = first_query + lax.broadcasted_iota(jnp.int32, (block, KEY_BLOCK), 0)
    lane = lax.broadcasted_iota(jnp.int32, (block, KEY_BLOCK), 1)
    to_log2 = math.log2(math.e) / math.sqrt(HEAD_SIZE)

    def visit(n, carry):
        run_max, run_sum, run_acc = carry
        start = pl.multiple_of(n * KEY_BLOCK, KEY_BLOCK)
        keys = kv[pl.ds(start, KEY_BLOCK), :HEAD_SIZE]
        values = kv[pl.ds(start, KEY_BLOCK), HEAD_SIZE:]
        scores = lax.dot_general(
            q, keys, (((1,), (1,)), ((), ())), preferred_element_type=jnp.float32
        )
        key_at = start + lane
        visible = (key_at >= low) & (key_at <= query_at)
        scores = jnp.where(visible[None], scores.reshape(heads, block, KEY_BLOCK), -1e30)
        scores = scores.reshape(heads * block, KEY_BLOCK)
        new_max = jnp.maximum(run_max, jnp.max(scores, axis=-1, keepdims=True))
        factor = jnp.exp2((run_max - new_max) * to_log2)
        weights = jnp.exp2((scores - new_max) * to_log2)
        run_sum = run_sum * factor + jnp.sum(weights, axis=-1, keepdims=True)
        run_acc = run_acc * factor + jnp.dot(
            weights.astype(jnp.bfloat16), values, preferred_element_type=jnp.float32
        )
        return new_max, run_sum, run_acc

    initial = (
        jnp.full((heads * block, 1), -1e30, jnp.float32),
        jnp.zeros((heads * block, 1), jnp.float32),
        jnp.zeros((heads * block, HEAD_SIZE), jnp.float32),
    )
    last = (first_query + block - 1) // KEY_BLOCK + 1
    _, run_sum, run_acc = lax.fori_loop(first_ref[step], last, visit, initial)
    mixed = (run_acc / run_sum).astype(jnp.bfloat16)
    for h in range(heads):
        out_ref[:, h * HEAD_SIZE : (h + 1) * HEAD_SIZE] = mixed[h * block : (h + 1) * block]


def attend(q, low, kv2, kv1, kv0):
    rows, width = q.shape
    first = low[:: QUERY_BLOCK, 0] // KEY_BLOCK
    spec = pltpu.PrefetchScalarGridSpec(
        num_scalar_prefetch=1,
        grid=(rows // QUERY_BLOCK,),
        in_specs=[
            pl.BlockSpec((QUERY_BLOCK, width), lambda s, first: (s, 0)),
            pl.BlockSpec((QUERY_BLOCK, 1), lambda s, first: (s, 0)),
            pl.BlockSpec(memory_space=pl.ANY),
            pl.BlockSpec(memory_space=pl.ANY),
            pl.BlockSpec(memory_space=pl.ANY),
        ],
        out_specs=pl.BlockSpec((QUERY_BLOCK, width), lambda s, first: (s, 0)),
        scratch_shapes=[
            pltpu.VMEM((3 * rows, 2 * HEAD_SIZE), jnp.bfloat16),
            pltpu.SemaphoreType.DMA((3,)),
        ],
    )
    return pl.pallas_call(
        attend_kernel,
        grid_spec=spec,
        out_shape=jax.ShapeDtypeStruct((rows, width), jnp.bfloat16),
        compiler_params=pltpu.CompilerParams(vmem_limit_bytes=32 * 1024 * 1024),
        cost_estimate=pl.CostEstimate(
            flops=4 * rows * rows * width * 2, bytes_accessed=2 * 6 * rows * width, transcendentals=0
        ),
    )(first, q, low, kv2, kv1, kv0)


def normalize(tokens, norm_gain):
    widened = tokens.astype(jnp.float32)
    mean_sq = jnp.mean(widened * widened, axis=-1, keepdims=True)
    return (widened * lax.rsqrt(mean_sq + 1e-05) * norm_gain.astype(jnp.float32)).astype(
        jnp.bfloat16
    )


def on_device(
    tokens, norm_gain, w_query, key_projection_weight, value_projection_weight, documents
):
    rows = tokens.shape[0]
    me = lax.axis_index("attn")
    mine = jnp.concatenate([key_projection_weight, value_projection_weight, w_query], 1)
    weights = lax.all_gather(mine, "rows", axis=0, tiled=True)

    normed = normalize(tokens, norm_gain)
    cosine, sine = rotary_tables(me * rows + jnp.arange(rows, dtype=jnp.int32))
    doc_ids = documents[0]
    my_docs = lax.dynamic_slice_in_dim(doc_ids, me * rows, rows)
    begin = jnp.sum((doc_ids[None, :] < my_docs[:, None]).astype(jnp.int32), axis=1, keepdims=True)
    low = jnp.maximum(begin - (me - 2) * rows, 0)

    kv = project(normed, weights[:, : 2 * HEAD_SIZE], cosine, sine, 1)
    kv1 = lax.ppermute(kv, "attn", [(0, 1), (1, 2), (2, 3)])
    kv2 = lax.ppermute(kv, "attn", [(0, 2), (1, 3)])
    q = project(normed, weights[:, 2 * HEAD_SIZE :], cosine, sine, 4)
    return attend(q, low, kv2, kv1, kv)


def solution(mesh):
    placed = (
        P(("rows", "attn"), None),
        P(),
        P("rows", "tp"),
        P("rows", "tp"),
        P("rows", "tp"),
        P("rows", None),
    )
    return jax.shard_map(
        on_device, mesh=mesh, in_specs=placed, out_specs=P(("rows", "attn"), "tp"), check_vma=False
    )
```

time: 289 us -> 127 us (0.44)
  the two profiles are of different devices: /device:TPU:179 before, /device:TPU:176 now
where the time goes in v1:
time: 127 us; the launch traced here: 126 us
  waiting for transfers between devices  71.3 us (56%)
  Pallas kernels  18.3 us (14%)
  between operations  13.5 us (11%)
  other arithmetic  11.7 us (9%)
  local copies, waits for them, and re-layouts  7.21 us (6%)
  starting transfers between devices  4.39 us (3%)
    all_gather x1, waiting for transfers between devices, on_device(): weights = lax.all_gather(mine, 'rows', axis=0, tiled=True)  67.3 us
    pallas_call x1, Pallas kernels, attend(): pl.pallas_call(attend_kernel, grid_spec=spec, out_shape=jax.ShapeDtypeStr...  12 us
    pallas_call x2, Pallas kernels, project(): pl.pallas_call(functools.partial(project_kernel, rotated_heads), grid=(st...  6.27 us
    ppermute x1, waiting for transfers between devices, on_device(): kv2 = lax.ppermute(kv, 'attn', [(0, 2), (1, 3)])  4.05 us
    convert_element_type x1, other arithmetic, normalize(): (widened * lax.rsqrt(mean_sq + 1e-05) * norm_gain.astype(jnp.float32)).as...  3.64 us
    ppermute x1, starting transfers between devices, on_device(): kv1 = lax.ppermute(kv, 'attn', [(0, 1), (1, 2), (2, 3)])  3.1 us
    reduce_sum x1, other arithmetic, normalize(): mean_sq = jnp.mean(widened * widened, axis=-1, keepdims=True)  3.08 us
    slice x1, local copies, waits for them, and re-layouts, on_device(): q = project(normed, weights[:, 2 * HEAD_SIZE:], cosine, sine, 4)  2.62 us
  transfers between devices with their start and end apart: 3, of which 2 were waited for; matrix products, arithmetic and copies ran while one was open for 11% of the time, Pallas kernels for 3%

profile of v1, /device:TPU:176, one launch (start us, length us, event | category | flops | bytes accessed | tf_op | source)
XLA Modules:
  0.0 126.4 jit_solution(3671214550857482258)
XLA Ops:
  6.5 0.0 all-gather.2.cloned.1.call-start
  6.5 1.6 %pad_maximum_fusion.2 = bf16[128,768]{1,0:T(8,128)(2,1)} fusion(bf16[128,512]{1,0:T(8,128)(2,1)} %param.8, bf16[128,128]{1,0:T(8,128)(2,1)} %param.10, bf16[128,128]{1,0:T(8,128)(2,1)} %param.9), kind=kLoop, calls=%fused_computation.10 | loop fusion | flops 589824 | bytes 393216 | tf_op jit(solution)/shard_map/concatenate | solution.py:176
  8.2 0.0 all-gather.2.cloned.1.call-update
  8.2 0.7 constant_dynamic-slice_fusion
  8.9 1.3 convert_reduce_fusion
  10.1 0.1 slice.9
  10.2 0.0 copy-start.2
  10.2 0.9 convert_element_type.21
  11.1 1.0 fusion.3
  12.1 0.2 pad_maximum_fusion
  12.3 3.1 %fusion = f32[512]{0:T(512)S(1)} fusion(bf16[512,4096]{1,0:T(8,128)(2,1)} %param.6), kind=kLoop, calls=%fused_computation.2 | loop fusion | flops 6290944 | bytes 4196352 | tf_op jit(solution)/shard_map/reduce_sum | solution.py:165
  15.4 0.0 copy-done.2
  15.4 3.6 %fusion.2.x_ref = bf16[512,4096]{1,0:T(8,128)(2,1)} fusion(bf16[512,4096]{1,0:T(8,128)(2,1)S(1)} %copy-done.2, f32[4096]{0:T(1024)S(1)} %convert_element_type.21, f32[512]{0:T(512)S(1)} %add_rsqrt_fusion), kind=kLoop, calls=%fused_computation.4 | loop fusion | flops 8388608 | bytes 8407040 | tf_op jit(solution)/shard_map/convert_element_type | solution.py:166
  19.1 67.3 %all-gather.2.cloned.1.call-done = bf16[4096,768]{1,0:T(8,128)(2,1)} async-done(((bf16[128,768]{1,0:T(8,128)(2,1)}), bf16[4096,768]{1,0:T(8,128)(2,1)}) %all-gather.2.cloned.1.call-update) | async-done | bytes 6291472 | tf_op jit(solution)/shard_map/all_gather | solution.py:177
  86.3 0.0 copy-start
  86.3 1.9 %slice.13.w_ref = bf16[4096,256]{1,0:T(8,128)(2,1)S(1)} slice(bf16[4096,768]{1,0:T(8,128)(2,1)} %all-gather.2.cloned.1.call-done), slice={[0:4096], [0:256]} | slice | bytes 4194304 | tf_op jit(solution)/shard_map/slice | solution.py:186
  88.2 1.0 copy-done
  89.2 2.4 %shard_map.65.kv0_ref = bf16[512,256]{1,0:T(8,128)(2,1)S(1)} custom-call(bf16[512,4096]{1,0:T(8,128)(2,1)S(1)} %copy-done, bf16[4096,256]{1,0:T(8,128)(2,1)S(1)} %slice.13.w_ref, f32[512,128]{1,0:T(8,128)S(1)} %get-tuple-element.8.cos_ref, f32[512,128]{1,0:T(8,128)S(1)} %get-tuple-element.9.sin_ref), custom_call_target="tpu_custom_call" | custom-call | flops 1073741824 | bytes 6553600 | tf_op jit(solution)/shard_map/pallas_call | solution.py:52
  91.6 3.1 %collective-permute-start.1 = (bf16[512,256]{1,0:T(8,128)(2,1)S(1)}, bf16[512,256]{1,0:T(8,128)(2,1)S(1)}, u32[]{:S(2)}, u32[]{:S(2)}) collective-permute-start(bf16[512,256]{1,0:T(8,128)(2,1)S(1)} %shard_map.65.kv0_ref), channel_id=1, source_target_pairs={{0,1},{1,2},{2,3},{4,5},{5,6},{6,7},{8,9},{9,10},{10,11},{12,13},{... | collective-permute-start | bytes 786440 | tf_op jit(solution)/shard_map/ppermute | solution.py:187
  94.7 1.3 %collective-permute-start = (bf16[512,256]{1,0:T(8,128)(2,1)S(1)}, bf16[512,256]{1,0:T(8,128)(2,1)S(1)}, u32[]{:S(2)}, u32[]{:S(2)}) collective-permute-start(bf16[512,256]{1,0:T(8,128)(2,1)S(1)} %shard_map.65.kv0_ref), channel_id=1, source_target_pairs={{0,2},{1,3},{4,6},{5,7},{8,10},{9,11},{12,14},{13,15},{16,18},{17,... | collective-permute-start | bytes 786440 | tf_op jit(solution)/shard_map/ppermute | solution.py:188
  96.0 0.1 copy.8.low_ref
  96.1 0.0 copy-start.1
  96.2 2.6 %slice.12.w_ref = bf16[4096,512]{1,0:T(8,128)(2,1)S(1)} slice(bf16[4096,768]{1,0:T(8,128)(2,1)} %all-gather.2.cloned.1.call-done), slice={[0:4096], [256:768]} | slice | bytes 8388608 | tf_op jit(solution)/shard_map/slice | solution.py:189
  98.8 0.8 copy-done.1
  99.6 3.9 %shard_map.64.q_ref = bf16[512,512]{1,0:T(8,128)(2,1)S(1)} custom-call(bf16[512,4096]{1,0:T(8,128)(2,1)S(1)} %copy-done.1, bf16[4096,512]{1,0:T(8,128)(2,1)S(1)} %slice.12.w_ref, f32[512,128]{1,0:T(8,128)S(1)} %get-tuple-element.8.cos_ref, f32[512,128]{1,0:T(8,128)S(1)} %get-tuple-element.9.sin_ref), custom_call_target="tpu_custom_call" | custom-call | flops 2147483648 | bytes 8912896 | tf_op jit(solution)/shard_map/pallas_call | solution.py:52
  103.5 0.0 collective-permute-done.1.kv1_ref
  103.5 4.0 %collective-permute-done.kv2_ref = bf16[512,256]{1,0:T(8,128)(2,1)S(1)} collective-permute-done((bf16[512,256]{1,0:T(8,128)(2,1)S(1)}, bf16[512,256]{1,0:T(8,128)(2,1)S(1)}, u32[]{:S(2)}, u32[]{:S(2)}) %collective-permute-start) | collective-permute-done | bytes 262176 | tf_op jit(solution)/shard_map/ppermute | solution.py:188
  107.5 12.0 %shard_map.66 = bf16[512,512]{1,0:T(8,128)(2,1)} custom-call(s32[4]{0:T(128)S(1)} %and_select_fusion.first_ref, bf16[512,512]{1,0:T(8,128)(2,1)S(1)} %shard_map.64.q_ref, s32[512,1]{1,0:T(8,128)S(1)} %copy.8.low_ref, bf16[512,256]{1,0:T(8,128)(2,1)S(1)} %collective-permute-done.kv2_ref, bf16[512,256]{1,0:T(8,128)(2,1)S(1)} %collective-permute-done.1.kv1_ref, ...), custom_call_target="tpu_custom_call" | custom-call | flops 1073741824 | bytes 3145728 | tf_op jit(solution)/shard_map/pallas_call | solution.py:152
  (5 shorter events, 0.0 us)
Async XLA Ops:
  6.5 79.8 %all-gather.2.cloned.1.call-start = ((), (), s32[]{:S(2)}) async-start(), calls=%async_computation | async-start | bytes 6488064 | tf_op jit(solution)/shard_map/all_gather | solution.py:177
  10.2 5.2 %copy-start.2 = (bf16[512,4096]{1,0:T(8,128)(2,1)S(1)}, bf16[512,4096]{1,0:T(8,128)(2,1)}, u32[]{:S(2)}) copy-start(bf16[512,4096]{1,0:T(8,128)(2,1)} %param.6) | copy-start | bytes 12582916
  86.3 2.8 %copy-start = (bf16[512,4096]{1,0:T(8,128)(2,1)S(1)}, bf16[512,4096]{1,0:T(8,128)(2,1)}, u32[]{:S(2)}) copy-start(bf16[512,4096]{1,0:T(8,128)(2,1)} %fusion.2.x_ref) | copy-start | bytes 12582916
  91.6 11.9 %collective-permute-start.1 = (bf16[512,256]{1,0:T(8,128)(2,1)S(1)}, bf16[512,256]{1,0:T(8,128)(2,1)S(1)}, u32[]{:S(2)}, u32[]{:S(2)}) collective-permute-start(bf16[512,256]{1,0:T(8,128)(2,1)S(1)} %shard_map.65.kv0_ref), channel_id=1, source_target_pairs={{0,1},{1,2},{2,3},{4,5},{5,6},{6,7},{8,9},{9,10},{10,11},{12,13},{... | collective-permute-start | bytes 786440 | tf_op jit(solution)/shard_map/ppermute | solution.py:187
  94.7 12.8 %collective-permute-start = (bf16[512,256]{1,0:T(8,128)(2,1)S(1)}, bf16[512,256]{1,0:T(8,128)(2,1)S(1)}, u32[]{:S(2)}, u32[]{:S(2)}) collective-permute-start(bf16[512,256]{1,0:T(8,128)(2,1)S(1)} %shard_map.65.kv0_ref), channel_id=1, source_target_pairs={{0,2},{1,3},{4,6},{5,7},{8,10},{9,11},{12,14},{13,15},{16,18},{17,... | collective-permute-start | bytes 786440 | tf_op jit(solution)/shard_map/ppermute | solution.py:188
  96.1 3.5 %copy-start.1 = (bf16[512,4096]{1,0:T(8,128)(2,1)S(1)}, bf16[512,4096]{1,0:T(8,128)(2,1)}, u32[]{:S(2)}) copy-start(bf16[512,4096]{1,0:T(8,128)(2,1)} %fusion.2.x_ref) | copy-start | bytes 12582916
Sparse Core Ops, SparseCore 0:
  9.5 76.7 all-gather.1

commit v2 on v1

--- a/solution.py
+++ b/solution.py
@@ -61,7 +61,7 @@
         out_specs=pl.BlockSpec((rows, width), lambda s: (0, 0)),
         out_shape=jax.ShapeDtypeStruct((rows, width), jnp.bfloat16),
         scratch_shapes=[pltpu.VMEM((rows, width), jnp.float32)],
-        compiler_params=pltpu.CompilerParams(vmem_limit_bytes=32 * 1024 * 1024),
+        compiler_params=pltpu.CompilerParams(vmem_limit_bytes=60 * 1024 * 1024),
         cost_estimate=pl.CostEstimate(
             flops=2 * rows * depth * width,
             bytes_accessed=2 * (rows * depth + depth * width + rows * width),
@@ -168,13 +168,35 @@
     )
 
 
+def gather_key_value(mine):
+    me = lax.axis_index("attn")
+    parts = lax.axis_size("attn")
+    devices = lax.axis_size("rows")
+    rows, width = mine.shape
+    quarter = rows // parts
+    own = lax.dynamic_slice_in_dim(mine, me * quarter, quarter, 0)
+    chips = devices // 2
+    same_core = [[2 * z + c for z in range(chips)] for c in range(2)]
+    column = lax.all_gather(own, "rows", axis=0, tiled=True, axis_index_groups=same_core)
+    spread = jnp.broadcast_to(column[None], (parts, chips * quarter, width))
+    half = lax.all_to_all(spread, "attn", 0, 0, tiled=True)
+    half = half.reshape(parts, chips, quarter, width).transpose(1, 0, 2, 3)
+    half = half.reshape(chips, rows, width)
+    other = lax.ppermute(half, "rows", [(i, i ^ 1) for i in range(devices)])
+    first = lax.axis_index("rows") % 2 == 0
+    both = jnp.stack([jnp.where(first, half, other), jnp.where(first, other, half)], 1)
+    return both.reshape(devices * rows, width)
+
+
 def on_device(
     tokens, norm_gain, w_query, key_projection_weight, value_projection_weight, documents
 ):
     rows = tokens.shape[0]
     me = lax.axis_index("attn")
-    mine = jnp.concatenate([key_projection_weight, value_projection_weight, w_query], 1)
-    weights = lax.all_gather(mine, "rows", axis=0, tiled=True)
+    query_weights = lax.all_gather(w_query, "rows", axis=0, tiled=True)
+    kv_weights = gather_key_value(
+        jnp.concatenate([key_projection_weight, value_projection_weight], 1)
+    )
 
     normed = normalize(tokens, norm_gain)
     cosine, sine = rotary_tables(me * rows + jnp.arange(rows, dtype=jnp.int32))
@@ -183,10 +205,10 @@
     begin = jnp.sum((doc_ids[None, :] < my_docs[:, None]).astype(jnp.int32), axis=1, keepdims=True)
     low = jnp.maximum(begin - (me - 2) * rows, 0)
 
-    kv = project(normed, weights[:, : 2 * HEAD_SIZE], cosine, sine, 1)
+    kv = project(normed, kv_weights, cosine, sine, 1)
     kv1 = lax.ppermute(kv, "attn", [(0, 1), (1, 2), (2, 3)])
     kv2 = lax.ppermute(kv, "attn", [(0, 2), (1, 3)])
-    q = project(normed, weights[:, 2 * HEAD_SIZE :], cosine, sine, 4)
+    q = project(normed, query_weights, cosine, sine, 4)
     return attend(q, low, kv2, kv1, kv)
 
 

time: 127 us -> 114 us (0.90)
  the two profiles are of different devices: /device:TPU:176 before, /device:TPU:17 now
where the time goes in v2:
time: 114 us; the launch traced here: 113 us
  blocking collectives  29.8 us (26%)
  Pallas kernels  22.1 us (19%)
  starting transfers between devices  20.2 us (18%)
  between operations  13.5 us (12%)
  other arithmetic  13.4 us (12%)
  waiting for transfers between devices  9.56 us (8%)
  local copies, waits for them, and re-layouts  4.59 us (4%)
    all_gather x1, blocking collectives, gather_key_value(): lax.all_gather(own, 'rows', axis=0, tiled=True, axis_index_groups=same_core)  29.8 us
    pallas_call x2, Pallas kernels, project(): pl.pallas_call(functools.partial(project_kernel, rotated_heads), grid=(st...  12.3 us
    ppermute x1, starting transfers between devices, gather_key_value(): other = lax.ppermute(half, 'rows', [(i, i ^ 1) for i in range(devices)])  10.9 us
    pallas_call x1, Pallas kernels, attend(): pl.pallas_call(attend_kernel, grid_spec=spec, out_shape=jax.ShapeDtypeStr...  9.78 us
    all_gather x1, waiting for transfers between devices, on_device(): query_weights = lax.all_gather(w_query, 'rows', axis=0, tiled=True)  8.63 us
    convert_element_type x1, other arithmetic, normalize(): (widened * lax.rsqrt(mean_sq + 1e-05) * norm_gain.astype(jnp.float32)).as...  5.83 us
    all_to_all x1, starting transfers between devices, gather_key_value(): half = lax.all_to_all(spread, 'attn', 0, 0, tiled=True)  4.24 us
    ppermute x1, starting transfers between devices, on_device(): kv1 = lax.ppermute(kv, 'attn', [(0, 1), (1, 2), (2, 3)])  3.72 us
  transfers between devices with their start and end apart: 5, of which 2 were waited for; matrix products, arithmetic and copies ran while one was open for 15% of the time, Pallas kernels for 11%

profile of v2, /device:TPU:17, one launch (start us, length us, event | category | flops | bytes accessed | tf_op | source)
XLA Modules:
  0.0 113.1 jit_solution(5435409259793102362)
XLA Ops:
  6.5 0.0 copy-start.2
  6.5 0.0 all-gather.2.cloned.1.call-start
  6.5 0.7 all-gather.2.cloned.1.call-update
  7.3 0.7 fusion.4
  8.0 29.8 %all_gather.7 = bf16[512,256]{1,0:T(8,128)(2,1)S(1)} all-gather(bf16[32,256]{1,0:T(8,128)(2,1)S(1)} %fusion.4), channel_id=1, replica_groups={{0,32,64,96,128,160,192,224,256,288,320,352,384,416,448,480},{16,48,80,..., dimensions={0}, use_global_device_ids=true | all-gather | bytes 278528 | tf_op jit(solution)/shard_map/all_gather | solution.py:180
  37.8 1.0 broadcast_in_dim.2
  38.8 4.2 %all-to-all-start = ((bf16[4,512,256]{2,1,0:T(8,128)(2,1)}), bf16[4,512,256]{2,1,0:T(8,128)(2,1)S(1)}, u32[]{:S(2)}, u32[]{:S(2)}) async-start(bf16[4,512,256]{2,1,0:T(8,128)(2,1)} %broadcast_in_dim.2), calls=%async_computation | async-start | bytes 2097152 | tf_op jit(solution)/shard_map/all_to_all | solution.py:182
  43.1 0.7 constant_dynamic-slice_fusion
  43.8 1.3 %convert_reduce_fusion = s32[512]{0:T(512)S(1)} fusion(s32[2048]{0:T(1024)} %bitcast.25, s32[512]{0:T(512)S(1)} %bitcast.28), kind=kLoop, calls=%fused_computation.5 | loop fusion | flops 3145216 | bytes 12288 | tf_op jit(solution)/shard_map/reduce_sum | solution.py:205
  45.0 1.0 fusion.3
  46.0 0.1 slice.3
  46.1 0.0 copy-done.2
  46.1 1.0 pad_maximum_fusion.1
  47.2 3.1 %fusion = f32[512]{0:T(512)S(1)} fusion(bf16[512,4096]{1,0:T(8,128)(2,1)} %param.6), kind=kLoop, calls=%fused_computation.2 | loop fusion | flops 6290944 | bytes 4196352 | tf_op jit(solution)/shard_map/reduce_sum | solution.py:165
  50.3 0.2 all-to-all-done
  50.5 0.1 copy.13
  50.6 10.9 %collective-permute-start = (bf16[16,128,256]{2,1,0:T(8,128)(2,1)S(1)}, bf16[16,128,256]{2,1,0:T(8,128)(2,1)S(1)}, u32[]{:S(2)}, u32[]{:S(2)}) collective-permute-start(bf16[16,128,256]{2,1,0:T(8,128)(2,1)S(1)} %bitcast.23), channel_id=1, source_target_pairs={{0,16},{16,0},{32,48},{48,32},{64,80},{80,64},{96,112},{112,96},{1... | collective-permute-start | bytes 3145736 | tf_op jit(solution)/shard_map/ppermute | solution.py:185
  61.6 5.8 %fusion.2.x_ref = bf16[512,4096]{1,0:T(8,128)(2,1)} fusion(bf16[512,4096]{1,0:T(8,128)(2,1)} %param.6, f32[4096]{0:T(1024)S(1)} %convert_element_type.21, f32[512]{0:T(512)S(1)} %add_rsqrt_fusion), kind=kLoop, calls=%fused_computation.4 | loop fusion | flops 8388608 | bytes 8407040 | tf_op jit(solution)/shard_map/convert_element_type | solution.py:166
  67.4 0.0 collective-permute-done
  67.4 0.2 select_bitcast_fusion.1
  67.6 0.2 pad_maximum_fusion
  67.8 1.5 %copy.14 = bf16[16,2,128,256]{3,2,1,0:T(8,128)(2,1)} copy(bf16[16,2,128,256]{3,2,0,1:T(8,128)(2,1)S(1)} %pad_maximum_fusion) | data formatting | bytes 4194304 | tf_op jit(solution)/shard_map/stack | solution.py:187
  69.3 5.4 %shard_map.65.kv0_ref = bf16[512,256]{1,0:T(8,128)(2,1)} custom-call(bf16[512,4096]{1,0:T(8,128)(2,1)} %fusion.2.x_ref, bf16[4096,256]{1,0:T(8,128)(2,1)} %bitcast.22, f32[512,128]{1,0:T(8,128)} %get-tuple-element.10.cos_ref, f32[512,128]{1,0:T(8,128)} %get-tuple-element.11.sin_ref), custom_call_target="tpu_custom_call" | custom-call | flops 1073741824 | bytes 6553600 | tf_op jit(solution)/shard_map/pallas_call | solution.py:52
  74.7 1.3 %collective-permute-start.1 = (bf16[512,256]{1,0:T(8,128)(2,1)}, bf16[512,256]{1,0:T(8,128)(2,1)S(1)}, u32[]{:S(2)}, u32[]{:S(2)}) collective-permute-start(bf16[512,256]{1,0:T(8,128)(2,1)} %shard_map.65.kv0_ref), channel_id=1, source_target_pairs={{0,2},{1,3},{4,6},{5,7},{8,10},{9,11},{12,14},{13,15},{16,18},{17,... | collective-permute-start | bytes 786440 | tf_op jit(solution)/shard_map/ppermute | solution.py:210
  76.0 3.7 %collective-permute-start.2 = (bf16[512,256]{1,0:T(8,128)(2,1)}, bf16[512,256]{1,0:T(8,128)(2,1)S(1)}, u32[]{:S(2)}, u32[]{:S(2)}) collective-permute-start(bf16[512,256]{1,0:T(8,128)(2,1)} %shard_map.65.kv0_ref), channel_id=1, source_target_pairs={{0,1},{1,2},{2,3},{4,5},{5,6},{6,7},{8,9},{9,10},{10,11},{12,13},{... | collective-permute-start | bytes 786440 | tf_op jit(solution)/shard_map/ppermute | solution.py:209
  79.7 0.1 copy.15.low_ref
  79.9 0.0 copy-start.1
  79.9 8.6 %all-gather.2.cloned.1.call-done.w_ref = bf16[4096,512]{1,0:T(8,128)(2,1)} async-done(((bf16[128,512]{1,0:T(8,128)(2,1)}), bf16[4096,512]{1,0:T(8,128)(2,1)}) %all-gather.2.cloned.1.call-update) | async-done | bytes 4194320 | tf_op jit(solution)/shard_map/all_gather | solution.py:196
  88.5 6.9 %shard_map.64.q_ref = bf16[512,512]{1,0:T(8,128)(2,1)} custom-call(bf16[512,4096]{1,0:T(8,128)(2,1)} %fusion.2.x_ref, bf16[4096,512]{1,0:T(8,128)(2,1)} %all-gather.2.cloned.1.call-done.w_ref, f32[512,128]{1,0:T(8,128)} %get-tuple-element.10.cos_ref, f32[512,128]{1,0:T(8,128)} %get-tuple-element.11.sin_ref), custom_call_target="tpu_custom_call" | custom-call | flops 2147483648 | bytes 8912896 | tf_op jit(solution)/shard_map/pallas_call | solution.py:52
  95.4 0.0 collective-permute-done.1.kv2_ref
  95.4 0.0 collective-permute-done.2.kv1_ref
  95.4 0.0 copy-done.1
  95.4 0.0 copy-start
  95.4 1.0 copy-done
  96.5 9.8 %shard_map.66 = bf16[512,512]{1,0:T(8,128)(2,1)} custom-call(s32[4]{0:T(128)S(1)} %and_select_fusion.first_ref, bf16[512,512]{1,0:T(8,128)(2,1)S(1)} %copy-done, s32[512,1]{1,0:T(8,128)S(1)} %copy.15.low_ref, bf16[512,256]{1,0:T(8,128)(2,1)S(1)} %collective-permute-done.1.kv2_ref, bf16[512,256]{1,0:T(8,128)(2,1)S(1)} %collective-permute-done.2.kv1_ref, ...), custom_call_target="tpu_custom_call" | custom-call | flops 1073741824 | bytes 3145728 | tf_op jit(solution)/shard_map/pallas_call | solution.py:152
  (6 shorter events, 0.0 us)
Async XLA Ops:
  6.5 39.6 %copy-start.2 = (bf16[4096]{0:T(1024)(128)(2,1)S(1)}, bf16[4096]{0:T(1024)(128)(2,1)}, u32[]{:S(2)}) copy-start(bf16[4096]{0:T(1024)(128)(2,1)} %param.7) | copy-start | bytes 24580
  6.5 82.0 %all-gather.2.cloned.1.call-start = ((), (), s32[]{:S(2)}) async-start(), calls=%async_computation.1 | async-start | bytes 4325376 | tf_op jit(solution)/shard_map/all_gather | solution.py:196
  38.8 11.7 %all-to-all-start = ((bf16[4,512,256]{2,1,0:T(8,128)(2,1)}), bf16[4,512,256]{2,1,0:T(8,128)(2,1)S(1)}, u32[]{:S(2)}, u32[]{:S(2)}) async-start(bf16[4,512,256]{2,1,0:T(8,128)(2,1)} %broadcast_in_dim.2), calls=%async_computation | async-start | bytes 2097152 | tf_op jit(solution)/shard_map/all_to_all | solution.py:182
  50.6 16.8 %collective-permute-start = (bf16[16,128,256]{2,1,0:T(8,128)(2,1)S(1)}, bf16[16,128,256]{2,1,0:T(8,128)(2,1)S(1)}, u32[]{:S(2)}, u32[]{:S(2)}) collective-permute-start(bf16[16,128,256]{2,1,0:T(8,128)(2,1)S(1)} %bitcast.23), channel_id=1, source_target_pairs={{0,16},{16,0},{32,48},{48,32},{64,80},{80,64},{96,112},{112,96},{1... | collective-permute-start | bytes 3145736 | tf_op jit(solution)/shard_map/ppermute | solution.py:185
  74.7 20.7 %collective-permute-start.1 = (bf16[512,256]{1,0:T(8,128)(2,1)}, bf16[512,256]{1,0:T(8,128)(2,1)S(1)}, u32[]{:S(2)}, u32[]{:S(2)}) collective-permute-start(bf16[512,256]{1,0:T(8,128)(2,1)} %shard_map.65.kv0_ref), channel_id=1, source_target_pairs={{0,2},{1,3},{4,6},{5,7},{8,10},{9,11},{12,14},{13,15},{16,18},{17,... | collective-permute-start | bytes 786440 | tf_op jit(solution)/shard_map/ppermute | solution.py:210
  76.0 19.5 %collective-permute-start.2 = (bf16[512,256]{1,0:T(8,128)(2,1)}, bf16[512,256]{1,0:T(8,128)(2,1)S(1)}, u32[]{:S(2)}, u32[]{:S(2)}) collective-permute-start(bf16[512,256]{1,0:T(8,128)(2,1)} %shard_map.65.kv0_ref), channel_id=1, source_target_pairs={{0,1},{1,2},{2,3},{4,5},{5,6},{6,7},{8,9},{9,10},{10,11},{12,13},{... | collective-permute-start | bytes 786440 | tf_op jit(solution)/shard_map/ppermute | solution.py:209
  79.9 15.6 %copy-start.1 = (bf16[512,256]{1,0:T(8,128)(2,1)S(1)}, bf16[512,256]{1,0:T(8,128)(2,1)}, u32[]{:S(2)}) copy-start(bf16[512,256]{1,0:T(8,128)(2,1)} %shard_map.65.kv0_ref) | copy-start | bytes 786436
  95.4 1.0 copy-start
Sparse Core Ops, SparseCore 0:
  9.5 78.9 all-gather.1

commit v3 on v1

--- a/solution.py
+++ b/solution.py
@@ -23,9 +23,17 @@
     return jnp.concatenate([cosine, cosine], 1), jnp.concatenate([-sine, sine], 1)
 
 
-def project_kernel(rotated_heads, x_ref, w_ref, cos_ref, sin_ref, out_ref, acc_ref):
+def project_kernel(rotated_heads, core_ref, x_ref, wa_ref, wb_ref, cos_ref, sin_ref, out_ref, acc_ref):
     step = pl.program_id(0)
-    part = jnp.dot(x_ref[...], w_ref[...], preferred_element_type=jnp.float32)
+    first = core_ref[0] == 0
+    wa, wb = wa_ref[...], wb_ref[...]
+    evens, odds = jnp.where(first, wa, wb), jnp.where(first, wb, wa)
+    blocks = []
+    for n in range(0, wa.shape[0], 128):
+        blocks += [evens[n : n + 128], odds[n : n + 128]]
+    part = jnp.dot(
+        x_ref[...], jnp.concatenate(blocks, axis=0), preferred_element_type=jnp.float32
+    )
 
     @pl.when(step == 0)
     def _():
@@ -45,29 +53,33 @@
             out_ref[:, lanes] = u.astype(jnp.bfloat16)
 
 
-def project(x, w, cosine, sine, rotated_heads, steps=4):
+def project(core, x, w, cosine, sine, rotated_heads, steps=4):
     rows, depth = x.shape
-    width = w.shape[1]
+    width = w[0].shape[1]
     chunk = depth // steps
+    w_spec = pl.BlockSpec((chunk // 2, width), lambda s: (s, 0))
+    table = pl.BlockSpec((rows, HEAD_SIZE), lambda s: (0, 0))
     return pl.pallas_call(
         functools.partial(project_kernel, rotated_heads),
         grid=(steps,),
         in_specs=[
+            pl.BlockSpec(memory_space=pltpu.SMEM),
             pl.BlockSpec((rows, chunk), lambda s: (0, s)),
-            pl.BlockSpec((chunk, width), lambda s: (s, 0)),
-            pl.BlockSpec((rows, HEAD_SIZE), lambda s: (0, 0)),
-            pl.BlockSpec((rows, HEAD_SIZE), lambda s: (0, 0)),
+            w_spec,
+            w_spec,
+            table,
+            table,
         ],
         out_specs=pl.BlockSpec((rows, width), lambda s: (0, 0)),
         out_shape=jax.ShapeDtypeStruct((rows, width), jnp.bfloat16),
         scratch_shapes=[pltpu.VMEM((rows, width), jnp.float32)],
-        compiler_params=pltpu.CompilerParams(vmem_limit_bytes=32 * 1024 * 1024),
+        compiler_params=pltpu.CompilerParams(vmem_limit_bytes=20 * 1024 * 1024),
         cost_estimate=pl.CostEstimate(
             flops=2 * rows * depth * width,
             bytes_accessed=2 * (rows * depth + depth * width + rows * width),
             transcendentals=0,
         ),
-    )(x, w, cosine, sine)
+    )(core, x, *w, cosine, sine)
 
 
 def attend_kernel(first_ref, q_ref, low_ref, kv2_ref, kv1_ref, kv0_ref, out_ref, kv, sems):
@@ -153,7 +165,7 @@
         attend_kernel,
         grid_spec=spec,
         out_shape=jax.ShapeDtypeStruct((rows, width), jnp.bfloat16),
-        compiler_params=pltpu.CompilerParams(vmem_limit_bytes=32 * 1024 * 1024),
+        compiler_params=pltpu.CompilerParams(vmem_limit_bytes=16 * 1024 * 1024),
         cost_estimate=pl.CostEstimate(
             flops=4 * rows * rows * width * 2, bytes_accessed=2 * 6 * rows * width, transcendentals=0
         ),
@@ -168,25 +180,132 @@
     )
 
 
+def chip_shift(x, steps):
+    n = lax.axis_size("rows") // 2
+    pairs = [(2 * z + c, 2 * ((z + steps(z)) % n) + c) for z in range(n) for c in range(2)]
+    return lax.ppermute(x, "rows", pairs)
+
+
+def neighbours(x):
+    return [
+        x,
+        chip_shift(x, lambda z: 1),
+        chip_shift(x, lambda z: -1),
+        chip_shift(x, lambda z: 2 if z % 2 == 0 else -2),
+    ]
+
+
+def round_attn(spread):
+    return lax.all_to_all(spread, "attn", 0, 0, tiled=True)
+
+
+def columns_kernel(first, here_ref, there_ref, *refs):
+    spread_ref, far_ref = refs[-2:]
+    take = pl.ds(first, far_ref.shape[-1])
+    for n in range(spread_ref.shape[0]):
+        spread_ref[n] = here_ref[..., take]
+    far_ref[...] = there_ref[..., take]
+
+
+def columns(here, there, first, width, after):
+    whole = pl.BlockSpec(memory_space=pltpu.VMEM)
+    one = jax.ShapeDtypeStruct((*here.shape[:-1], width), here.dtype)
+    return pl.pallas_call(
+        functools.partial(columns_kernel, first),
+        in_specs=[whole, whole] + [pl.BlockSpec(memory_space=pl.ANY)] * len(after),
+        out_specs=[whole, whole],
+        out_shape=[jax.ShapeDtypeStruct((4, *one.shape), one.dtype), one],
+        compiler_params=pltpu.CompilerParams(vmem_limit_bytes=8 * 1024 * 1024),
+        cost_estimate=pl.CostEstimate(flops=0, bytes_accessed=14 * one.size, transcendentals=0),
+    )(here, there, *after)
+
+
+def order_kernel(place_ref, near_ref, r0_ref, r1_ref, r2_ref, r3_ref, after_ref, out_ref, sems):
+    copies = []
+    for k in range(4):
+        for r in range(4):
+            copies.append((near_ref.at[k, r], out_ref.at[:, r, k, 0]))
+        for d, ref in enumerate((r0_ref, r1_ref, r2_ref, r3_ref)):
+            copies.append((ref.at[k], out_ref.at[:, place_ref[d], k, 1]))
+    copies = [
+        pltpu.make_async_copy(src, dst, sems.at[n]) for n, (src, dst) in enumerate(copies)
+    ]
+    for copy in copies:
+        copy.start()
+    for copy in copies:
+        copy.wait()
+
+
+def in_order(place, near, far, after):
+    block, width = near.shape[-2:]
+    out = pl.pallas_call(
+        order_kernel,
+        in_specs=[pl.BlockSpec(memory_space=pltpu.SMEM)] + [pl.BlockSpec(memory_space=pl.ANY)] * 6,
+        out_specs=pl.BlockSpec(memory_space=pl.ANY),
+        out_shape=jax.ShapeDtypeStruct((4, 4, 4, 2, block, width), jnp.bfloat16),
+        scratch_shapes=[pltpu.SemaphoreType.DMA((32,))],
+        compiler_params=pltpu.CompilerParams(vmem_limit_bytes=2 * 1024 * 1024),
+        cost_estimate=pl.CostEstimate(flops=0, bytes_accessed=4 * near.size * 2, transcendentals=0),
+    )(place, near, *far, after)
+    return out.reshape(128 * block, width)
+
+
+def gather_first(mine):
+    me = lax.axis_index("attn")
+    rows = mine.shape[0]
+    quarter = rows // 4
+    own = lax.dynamic_slice_in_dim(mine, me * quarter, quarter, 0)
+    apart = [[2 * (4 * q + r) + c for q in range(4)] for r in range(4) for c in range(2)]
+    close = [[2 * (4 * q + r) + c for r in range(4)] for q in range(4) for c in range(2)]
+    far = lax.all_gather(own, "rows", axis=0, tiled=False, axis_index_groups=apart)
+    there = round_attn(jnp.broadcast_to(far[None, :, quarter // 2 :], (4, 4, quarter // 2, mine.shape[1])))
+    here = lax.all_gather(
+        far[:, : quarter // 2], "rows", axis=0, tiled=False, axis_index_groups=close
+    )
+    return here, there
+
+
+def swap_cores(own):
+    devices = lax.axis_size("rows")
+    return own, lax.ppermute(own, "rows", [(i, i ^ 1) for i in range(devices)])
+
+
+def gather_second(here, there, first, width, after):
+    spread, far = columns(here, there, first, width, after)
+    return round_attn(spread), neighbours(far)
+
+
 def on_device(
     tokens, norm_gain, w_query, key_projection_weight, value_projection_weight, documents
 ):
     rows = tokens.shape[0]
     me = lax.axis_index("attn")
+    chip, core = lax.axis_index("rows") // 2, lax.axis_index("rows") % 2
+    split = 2 * key_projection_weight.shape[1]
     mine = jnp.concatenate([key_projection_weight, value_projection_weight, w_query], 1)
-    weights = lax.all_gather(mine, "rows", axis=0, tiled=True)
-
-    normed = normalize(tokens, norm_gain)
+    here, there = gather_first(mine)
+    across = jnp.where(chip % 2 == 0, -2, 2)
+    place = (chip + jnp.stack([0 * across, across * 0 - 1, across * 0 + 1, across])) % 4
+    place = place.astype(jnp.int32)
+
+    x = normalize(tokens, norm_gain)
     cosine, sine = rotary_tables(me * rows + jnp.arange(rows, dtype=jnp.int32))
     doc_ids = documents[0]
     my_docs = lax.dynamic_slice_in_dim(doc_ids, me * rows, rows)
     begin = jnp.sum((doc_ids[None, :] < my_docs[:, None]).astype(jnp.int32), axis=1, keepdims=True)
     low = jnp.maximum(begin - (me - 2) * rows, 0)
 
-    kv = project(normed, weights[:, : 2 * HEAD_SIZE], cosine, sine, 1)
+    core = core.reshape(1).astype(jnp.int32)
+    near, far = gather_second(here, there, 0, split, [])
+    near_q, far_q = gather_second(
+        here, there, split, w_query.shape[1], [near, *far[1:], x]
+    )
+    kv_weights = swap_cores(in_order(place, near, far, x))
+    kv = project(core, x, kv_weights, cosine, sine, 1)
     kv1 = lax.ppermute(kv, "attn", [(0, 1), (1, 2), (2, 3)])
     kv2 = lax.ppermute(kv, "attn", [(0, 2), (1, 3)])
-    q = project(normed, weights[:, 2 * HEAD_SIZE :], cosine, sine, 4)
+    query_weights = swap_cores(in_order(place, near_q, far_q, kv))
+    q = project(core, x, query_weights, cosine, sine, 4)
     return attend(q, low, kv2, kv1, kv)
 
 

time: 127 us -> 143 us (1.13)
  the two profiles are of different devices: /device:TPU:176 before, /device:TPU:82 now
where the time goes in v3:
time: 143 us; the launch traced here: 142 us
  starting transfers between devices  44.2 us (31%)
  blocking collectives  38.3 us (27%)
  Pallas kernels  24.9 us (17%)
  local copies, waits for them, and re-layouts  15.6 us (11%)
  other arithmetic  13.7 us (10%)
  waiting for transfers between devices  4.47 us (3%)
    all_gather x1, blocking collectives, gather_first(): lax.all_gather(own, 'rows', axis=0, tiled=False, axis_index_groups=apart)  25 us
    ppermute x6, starting transfers between devices, chip_shift(): return lax.ppermute(x, 'rows', pairs)  20.7 us
    all_to_all x3, starting transfers between devices, round_attn(): return lax.all_to_all(spread, 'attn', 0, 0, tiled=True)  15.2 us
    unnamed x38, local copies, waits for them, and re-layouts  13.8 us
    all_gather x1, blocking collectives, gather_first(): lax.all_gather(far[:, :quarter // 2], 'rows', axis=0, tiled=False, axis_i...  13.3 us
    pallas_call x1, Pallas kernels, attend(): pl.pallas_call(attend_kernel, grid_spec=spec, out_shape=jax.ShapeDtypeStr...  13 us
    pallas_call x2, Pallas kernels, project(): pl.pallas_call(functools.partial(project_kernel, rotated_heads), grid=(st...  7.61 us
    convert_element_type x1, other arithmetic, normalize(): (widened * lax.rsqrt(mean_sq + 1e-05) * norm_gain.astype(jnp.float32)).as...  5.78 us
  transfers between devices with their start and end apart: 13, of which 1 were waited for; matrix products, arithmetic and copies ran while one was open for 10% of the time, Pallas kernels for 5%

profile of v3, /device:TPU:82, one launch (start us, length us, event | category | flops | bytes accessed | tf_op | source)
XLA Modules:
  0.0 141.6 jit_solution(3919274484759023812)
XLA Ops:
  0.0 0.8 fusion.5
  0.8 25.0 %all-gather = bf16[128,768]{1,0:T(8,128)(2,1)S(1)} all-gather(bf16[32,768]{1,0:T(8,128)(2,1)S(1)} %fusion.5), channel_id=2, replica_groups={{0,128,256,384},{16,144,272,400},{32,160,288,416},{48,176,304,432},{64,..., dimensions={0}, use_global_device_ids=true | all-gather | bytes 245760 | tf_op jit(solution)/shard_map/all_gather | solution.py:260
  25.8 0.8 broadcast_in_dim.2
  26.6 4.8 %all-to-all-start = ((bf16[4,4,16,768]{3,2,1,0:T(8,128)(2,1)}), bf16[4,4,16,768]{3,2,1,0:T(8,128)(2,1)S(1)}, u32[]{:S(2)}, u32[]{:S(2)}) async-start(bf16[4,4,16,768]{3,2,1,0:T(8,128)(2,1)} %broadcast_in_dim.2), calls=%async_computation | async-start | bytes 786432 | tf_op jit(solution)/shard_map/all_to_all | solution.py:199
  31.4 3.1 %fusion = f32[512]{0:T(512)S(1)} fusion(bf16[512,4096]{1,0:T(8,128)(2,1)} %param.6), kind=kLoop, calls=%fused_computation.2 | loop fusion | flops 6290944 | bytes 4196352 | tf_op jit(solution)/shard_map/reduce_sum | solution.py:177
  34.5 13.3 %all-gather.1 = bf16[16,16,768]{2,1,0:T(8,128)(2,1)S(1)} all-gather(bf16[4,16,768]{2,1,0:T(8,128)(2,1)S(1)} %get-tuple-element.14), channel_id=3, replica_groups={{0,32,64,96},{16,48,80,112},{128,160,192,224},{144,176,208,240},{256,28..., dimensions={0}, use_global_device_ids=true | all-gather | bytes 491520 | tf_op jit(solution)/shard_map/all_gather | solution.py:262
  47.8 0.0 copy-done.18
  47.8 0.0 all-to-all-done.there_ref
  47.8 0.8 shard_map.64
  48.7 4.8 %collective-permute-start = (bf16[4,4,16,256]{3,2,1,0:T(8,128)(2,1)S(1)}, bf16[4,4,16,256]{3,2,1,0:T(8,128)(2,1)S(1)}, u32[]{:S(2)}, u32[]{:S(2)}) collective-permute-start(bf16[4,4,16,256]{3,2,1,0:T(8,128)(2,1)S(1)} %get-tuple-element.10.r0_ref), channel_id=1, source_target_pairs={{0,32},{16,48},{32,64},{48,80},{64,96},{80,112},{96,128},{112,144}... | collective-permute-start | bytes 393224 | tf_op jit(solution)/shard_map/ppermute | solution.py:186
  53.5 1.9 %collective-permute-start.1 = (bf16[4,4,16,256]{3,2,1,0:T(8,128)(2,1)S(1)}, bf16[4,4,16,256]{3,2,1,0:T(8,128)(2,1)S(1)}, u32[]{:S(2)}, u32[]{:S(2)}) collective-permute-start(bf16[4,4,16,256]{3,2,1,0:T(8,128)(2,1)S(1)} %get-tuple-element.10.r0_ref), channel_id=1, source_target_pairs={{0,480},{16,496},{32,0},{48,16},{64,32},{80,48},{96,64},{112,80},{... | collective-permute-start | bytes 393224 | tf_op jit(solution)/shard_map/ppermute | solution.py:186
  55.4 4.6 %collective-permute-start.2 = (bf16[4,4,16,256]{3,2,1,0:T(8,128)(2,1)S(1)}, bf16[4,4,16,256]{3,2,1,0:T(8,128)(2,1)S(1)}, u32[]{:S(2)}, u32[]{:S(2)}) collective-permute-start(bf16[4,4,16,256]{3,2,1,0:T(8,128)(2,1)S(1)} %get-tuple-element.10.r0_ref), channel_id=1, source_target_pairs={{0,64},{16,80},{32,480},{48,496},{64,128},{80,144},{96,32},{112,48... | collective-permute-start | bytes 393224 | tf_op jit(solution)/shard_map/ppermute | solution.py:186
  60.0 4.8 %all-to-all-start.1 = ((bf16[4,4,4,16,256]{4,3,2,1,0:T(8,128)(2,1)}), bf16[4,4,4,16,256]{4,3,2,1,0:T(8,128)(2,1)S(1)}, u32[]{:S(2)}, u32[]{:S(2)}) async-start(bf16[4,4,4,16,256]{4,3,2,1,0:T(8,128)(2,1)} %get-tuple-element.9), calls=%async_computation.1 | async-start | bytes 1048576 | tf_op jit(solution)/shard_map/all_to_all | solution.py:199
  64.8 5.8 %fusion.2.refs_4_.after_ref.x_ref = bf16[512,4096]{1,0:T(8,128)(2,1)} fusion(bf16[512,4096]{1,0:T(8,128)(2,1)} %param.6, f32[4096]{0:T(1024)S(1)} %convert_element_type.21, f32[512]{0:T(512)S(1)} %add_rsqrt_fusion), kind=kLoop, calls=%fused_computation.4 | loop fusion | flops 8388608 | bytes 8407040 | tf_op jit(solution)/shard_map/convert_element_type | solution.py:178
  70.6 0.1 and_select_fusion.place_ref
  70.7 0.0 collective-permute-done.refs_1_.r1_ref
  70.7 0.0 collective-permute-done.1.refs_2_.r2_ref
  70.7 0.0 copy-start.10
  70.7 0.0 collective-permute-done.2.refs_3_.r3_ref
  70.7 0.0 copy-start.12
  70.8 0.0 all-to-all-done.1.refs_0_.near_ref
  70.8 0.0 copy-start
  70.8 2.3 %copy-done = bf16[512,4096]{1,0:T(8,128)(2,1)S(1)} copy-done((bf16[512,4096]{1,0:T(8,128)(2,1)S(1)}, bf16[512,4096]{1,0:T(8,128)(2,1)}, u32[]{:S(2)}) %copy-start) | copy-done | bytes 4194328
  73.0 1.2 shard_map.66
  74.2 0.0 copy-done.10
  74.3 0.0 copy-done.12
  74.3 2.1 %collective-permute-start.6 = (bf16[2048,256]{1,0:T(8,128)(2,1)S(1)}, bf16[2048,256]{1,0:T(8,128)(2,1)S(1)}, u32[]{:S(2)}, u32[]{:S(2)}) collective-permute-start(bf16[2048,256]{1,0:T(8,128)(2,1)S(1)} %bitcast.19), channel_id=1, source_target_pairs={{0,16},{16,0},{32,48},{48,32},{64,80},{80,64},{96,112},{112,96},{1... | collective-permute-start | bytes 3145736 | tf_op jit(solution)/shard_map/ppermute | solution.py:270
  76.3 0.9 copy-done.11
  77.2 0.9 copy-done.13
  78.2 0.1 shard_map.65
  78.2 0.0 copy-start.9
  78.2 1.0 copy-done.9
  79.3 0.7 copy-done.14
  80.0 5.6 %all-to-all-start.2 = ((bf16[4,4,4,16,512]{4,3,2,1,0:T(8,128)(2,1)}), bf16[4,4,4,16,512]{4,3,2,1,0:T(8,128)(2,1)S(1)}, u32[]{:S(2)}, u32[]{:S(2)}) async-start(bf16[4,4,4,16,512]{4,3,2,1,0:T(8,128)(2,1)} %copy-done.9), calls=%async_computation.2 | async-start | bytes 2097152 | tf_op jit(solution)/shard_map/all_to_all | solution.py:199
  85.6 1.9 %collective-permute-start.3 = (bf16[4,4,16,512]{3,2,1,0:T(8,128)(2,1)}, bf16[4,4,16,512]{3,2,1,0:T(8,128)(2,1)}, u32[]{:S(2)}, u32[]{:S(2)}) collective-permute-start(bf16[4,4,16,512]{3,2,1,0:T(8,128)(2,1)} %copy-done.14), channel_id=1, source_target_pairs={{0,32},{16,48},{32,64},{48,80},{64,96},{80,112},{96,128},{112,144}... | collective-permute-start | bytes 786440 | tf_op jit(solution)/shard_map/ppermute | solution.py:186
  87.5 3.9 %collective-permute-start.4 = (bf16[4,4,16,512]{3,2,1,0:T(8,128)(2,1)}, bf16[4,4,16,512]{3,2,1,0:T(8,128)(2,1)}, u32[]{:S(2)}, u32[]{:S(2)}) collective-permute-start(bf16[4,4,16,512]{3,2,1,0:T(8,128)(2,1)} %copy-done.14), channel_id=1, source_target_pairs={{0,480},{16,496},{32,0},{48,16},{64,32},{80,48},{96,64},{112,80},{... | collective-permute-start | bytes 786440 | tf_op jit(solution)/shard_map/ppermute | solution.py:186
  91.4 3.6 %collective-permute-start.5 = (bf16[4,4,16,512]{3,2,1,0:T(8,128)(2,1)}, bf16[4,4,16,512]{3,2,1,0:T(8,128)(2,1)}, u32[]{:S(2)}, u32[]{:S(2)}) collective-permute-start(bf16[4,4,16,512]{3,2,1,0:T(8,128)(2,1)} %copy-done.14), channel_id=1, source_target_pairs={{0,64},{16,80},{32,480},{48,496},{64,128},{80,144},{96,32},{112,48... | collective-permute-start | bytes 786440 | tf_op jit(solution)/shard_map/ppermute | solution.py:186
  95.0 1.9 %fusion.3 = (f32[512,64]{1,0:T(8,128)}, f32[512,64]{1,0:T(8,128)}, f32[512,64]{1,0:T(8,128)}) fusion(f32[64]{0:T(128)S(1)} %multiply_exponential_fusion, f32[512]{0:T(512)S(1)} %add_convert_fusion), kind=kLoop, calls=%fused_computation.13 | loop fusion | flops 65536 | bytes 395520 | tf_op jit(solution)/shard_map/neg | solution.py:23
  96.9 1.4 pad_maximum_fusion
  98.3 0.0 collective-permute-done.6.wb_ref
  98.3 2.3 %copy-done.2 = bf16[512,4096]{1,0:T(8,128)(2,1)S(1)} copy-done((bf16[512,4096]{1,0:T(8,128)(2,1)S(1)}, bf16[512,4096]{1,0:T(8,128)(2,1)}, u32[]{:S(2)}) %copy-start.2) | copy-done | bytes 4194328
  100.6 2.4 %shard_map.67.after_ref.kv0_ref = bf16[512,256]{1,0:T(8,128)(2,1)S(1)} custom-call(s32[1]{0:T(128)} %bitcast.4.core_ref, bf16[512,4096]{1,0:T(8,128)(2,1)S(1)} %copy-done.2, bf16[2048,256]{1,0:T(8,128)(2,1)S(1)} %bitcast.20, bf16[2048,256]{1,0:T(8,128)(2,1)S(1)} %collective-permute-done.6.wb_ref, f32[512,128]{1,0:T(8,128)S(1)} %get-tuple-element.18.cos_ref, ...), custom_call_target="tpu_custom_call" | custom-call | flops 1073741824 | bytes 6553600 | tf_op jit(solution)/shard_map/pallas_call | solution.py:62
  103.0 0.7 copy-done.6
  103.7 0.0 collective-permute-done.3.r1_ref
  103.7 0.0 collective-permute-done.4.r2_ref
  103.7 0.0 collective-permute-done.5.r3_ref
  103.8 0.0 all-to-all-done.2.near_ref
  103.8 0.9 copy-done.7
  104.7 0.9 copy-done.15
  105.7 2.2 %shard_map.68 = bf16[4,4,4,2,16,512]{5,4,3,2,1,0:T(8,128)(2,1)S(1)} custom-call(s32[4]{0:T(128)S(1)} %and_select_fusion.place_ref, bf16[4,4,4,16,512]{4,3,2,1,0:T(8,128)(2,1)S(1)} %all-to-all-done.2.near_ref, bf16[4,4,16,512]{3,2,1,0:T(8,128)(2,1)S(1)} %copy-done.15, bf16[4,4,16,512]{3,2,1,0:T(8,128)(2,1)} %collective-permute-done.3.r1_ref, ...), custom_call_target="tpu_custom_call" | custom-call | bytes 4194304 | tf_op jit(solution)/shard_map/pallas_call | solution.py:241
  107.9 1.9 %collective-permute-start.7 = (bf16[2048,512]{1,0:T(8,128)(2,1)S(1)}, bf16[2048,512]{1,0:T(8,128)(2,1)}, u32[]{:S(2)}, u32[]{:S(2)}) collective-permute-start(bf16[2048,512]{1,0:T(8,128)(2,1)S(1)} %bitcast.17), channel_id=1, source_target_pairs={{0,16},{16,0},{32,48},{48,32},{64,80},{80,64},{96,112},{112,96},{1... | collective-permute-start | bytes 6291464 | tf_op jit(solution)/shard_map/ppermute | solution.py:270
  109.8 0.0 copy-done.17
  109.8 0.6 convert_reduce_fusion
  110.4 0.1 slice.9
  110.5 1.3 collective-permute-start.8
  111.8 3.1 %collective-permute-start.9 = (bf16[512,256]{1,0:T(8,128)(2,1)}, bf16[512,256]{1,0:T(8,128)(2,1)}, u32[]{:S(2)}, u32[]{:S(2)}) collective-permute-start(bf16[512,256]{1,0:T(8,128)(2,1)} %copy-done.6), channel_id=1, source_target_pairs={{0,1},{1,2},{2,3},{4,5},{5,6},{6,7},{8,9},{9,10},{10,11},{12,13},{... | collective-permute-start | bytes 786440 | tf_op jit(solution)/shard_map/ppermute | solution.py:305
  114.9 0.9 copy.9.low_ref
  115.8 0.0 collective-permute-done.7.wb_ref
  115.8 2.2 %copy-done.3 = bf16[512,4096]{1,0:T(8,128)(2,1)S(1)} copy-done((bf16[512,4096]{1,0:T(8,128)(2,1)S(1)}, bf16[512,4096]{1,0:T(8,128)(2,1)}, u32[]{:S(2)}) %copy-start.3) | copy-done | bytes 4194328
  118.0 0.9 copy-done.5
  118.9 5.2 %shard_map.69.q_ref = bf16[512,512]{1,0:T(8,128)(2,1)S(1)} custom-call(s32[1]{0:T(128)} %bitcast.4.core_ref, bf16[512,4096]{1,0:T(8,128)(2,1)S(1)} %copy-done.3, bf16[2048,512]{1,0:T(8,128)(2,1)S(1)} %bitcast.18, bf16[2048,512]{1,0:T(8,128)(2,1)} %collective-permute-done.7.wb_ref, f32[512,128]{1,0:T(8,128)S(1)} %get-tuple-element.18.cos_ref, ...), custom_call_target="tpu_custom_call" | custom-call | flops 2147483648 | bytes 8912896 | tf_op jit(solution)/shard_map/pallas_call | solution.py:62
  124.1 0.0 collective-permute-done.8.kv2_ref
  124.1 4.4 %collective-permute-done.9.kv1_ref = bf16[512,256]{1,0:T(8,128)(2,1)} collective-permute-done((bf16[512,256]{1,0:T(8,128)(2,1)}, bf16[512,256]{1,0:T(8,128)(2,1)}, u32[]{:S(2)}, u32[]{:S(2)}) %collective-permute-start.9) | collective-permute-done | bytes 262176 | tf_op jit(solution)/shard_map/ppermute | solution.py:305
  128.6 13.0 %shard_map.70 = bf16[512,512]{1,0:T(8,128)(2,1)} custom-call(s32[4]{0:T(128)S(1)} %and_select_fusion.1.first_ref, bf16[512,512]{1,0:T(8,128)(2,1)S(1)} %shard_map.69.q_ref, s32[512,1]{1,0:T(8,128)S(1)} %copy-done.16, bf16[512,256]{1,0:T(8,128)(2,1)} %collective-permute-done.8.kv2_ref, bf16[512,256]{1,0:T(8,128)(2,1)} %collective-permute-done.9.kv1_ref, ...), custom_call_target="tpu_custom_call" | custom-call | flops 1073741824 | bytes 3145728 | tf_op jit(solution)/shard_map/pallas_call | solution.py:164
  (27 shorter events, 0.1 us)
Async XLA Ops:
  0.0 47.8 %copy-start.18 = (bf16[4096]{0:T(1024)(128)(2,1)S(1)}, bf16[4096]{0:T(1024)(128)(2,1)}, u32[]{:S(2)}) copy-start(bf16[4096]{0:T(1024)(128)(2,1)} %param.7) | copy-start | bytes 24580
  26.6 21.2 %all-to-all-start = ((bf16[4,4,16,768]{3,2,1,0:T(8,128)(2,1)}), bf16[4,4,16,768]{3,2,1,0:T(8,128)(2,1)S(1)}, u32[]{:S(2)}, u32[]{:S(2)}) async-start(bf16[4,4,16,768]{3,2,1,0:T(8,128)(2,1)} %broadcast_in_dim.2), calls=%async_computation | async-start | bytes 786432 | tf_op jit(solution)/shard_map/all_to_all | solution.py:199
  48.7 22.0 %collective-permute-start = (bf16[4,4,16,256]{3,2,1,0:T(8,128)(2,1)S(1)}, bf16[4,4,16,256]{3,2,1,0:T(8,128)(2,1)S(1)}, u32[]{:S(2)}, u32[]{:S(2)}) collective-permute-start(bf16[4,4,16,256]{3,2,1,0:T(8,128)(2,1)S(1)} %get-tuple-element.10.r0_ref), channel_id=1, source_target_pairs={{0,32},{16,48},{32,64},{48,80},{64,96},{80,112},{96,128},{112,144}... | collective-permute-start | bytes 393224 | tf_op jit(solution)/shard_map/ppermute | solution.py:186
  53.5 17.3 %collective-permute-start.1 = (bf16[4,4,16,256]{3,2,1,0:T(8,128)(2,1)S(1)}, bf16[4,4,16,256]{3,2,1,0:T(8,128)(2,1)S(1)}, u32[]{:S(2)}, u32[]{:S(2)}) collective-permute-start(bf16[4,4,16,256]{3,2,1,0:T(8,128)(2,1)S(1)} %get-tuple-element.10.r0_ref), channel_id=1, source_target_pairs={{0,480},{16,496},{32,0},{48,16},{64,32},{80,48},{96,64},{112,80},{... | collective-permute-start | bytes 393224 | tf_op jit(solution)/shard_map/ppermute | solution.py:186
  55.4 15.3 %collective-permute-start.2 = (bf16[4,4,16,256]{3,2,1,0:T(8,128)(2,1)S(1)}, bf16[4,4,16,256]{3,2,1,0:T(8,128)(2,1)S(1)}, u32[]{:S(2)}, u32[]{:S(2)}) collective-permute-start(bf16[4,4,16,256]{3,2,1,0:T(8,128)(2,1)S(1)} %get-tuple-element.10.r0_ref), channel_id=1, source_target_pairs={{0,64},{16,80},{32,480},{48,496},{64,128},{80,144},{96,32},{112,48... | collective-permute-start | bytes 393224 | tf_op jit(solution)/shard_map/ppermute | solution.py:186
  60.0 10.7 %all-to-all-start.1 = ((bf16[4,4,4,16,256]{4,3,2,1,0:T(8,128)(2,1)}), bf16[4,4,4,16,256]{4,3,2,1,0:T(8,128)(2,1)S(1)}, u32[]{:S(2)}, u32[]{:S(2)}) async-start(bf16[4,4,4,16,256]{4,3,2,1,0:T(8,128)(2,1)} %get-tuple-element.9), calls=%async_computation.1 | async-start | bytes 1048576 | tf_op jit(solution)/shard_map/all_to_all | solution.py:199
  70.7 3.5 %copy-start.10 = (bf16[4,4,16,256]{3,2,1,0:T(8,128)(2,1)}, bf16[4,4,16,256]{3,2,1,0:T(8,128)(2,1)S(1)}, u32[]{:S(2)}) copy-start(bf16[4,4,16,256]{3,2,1,0:T(8,128)(2,1)S(1)} %collective-permute-done.1.refs_2_.r2_ref) | copy-start | bytes 393220
  70.7 3.5 %copy-start.12 = (bf16[4,4,16,256]{3,2,1,0:T(8,128)(2,1)}, bf16[4,4,16,256]{3,2,1,0:T(8,128)(2,1)S(1)}, u32[]{:S(2)}) copy-start(bf16[4,4,16,256]{3,2,1,0:T(8,128)(2,1)S(1)} %collective-permute-done.2.refs_3_.r3_ref) | copy-start | bytes 393220
  70.8 2.3 %copy-start = (bf16[512,4096]{1,0:T(8,128)(2,1)S(1)}, bf16[512,4096]{1,0:T(8,128)(2,1)}, u32[]{:S(2)}) copy-start(bf16[512,4096]{1,0:T(8,128)(2,1)} %fusion.2.refs_4_.after_ref.x_ref) | copy-start | bytes 12582916
  73.0 3.3 %copy-start.1 = (bf16[512,4096]{1,0:T(8,128)(2,1)S(1)}, bf16[512,4096]{1,0:T(8,128)(2,1)}, u32[]{:S(2)}) copy-start(bf16[512,4096]{1,0:T(8,128)(2,1)} %fusion.2.refs_4_.after_ref.x_ref) | copy-start | bytes 12582916
  74.3 24.0 %collective-permute-start.6 = (bf16[2048,256]{1,0:T(8,128)(2,1)S(1)}, bf16[2048,256]{1,0:T(8,128)(2,1)S(1)}, u32[]{:S(2)}, u32[]{:S(2)}) collective-permute-start(bf16[2048,256]{1,0:T(8,128)(2,1)S(1)} %bitcast.19), channel_id=1, source_target_pairs={{0,16},{16,0},{32,48},{48,32},{64,80},{80,64},{96,112},{112,96},{1... | collective-permute-start | bytes 3145736 | tf_op jit(solution)/shard_map/ppermute | solution.py:270
  76.3 0.9 copy-start.11
  77.2 0.9 copy-start.13
  78.2 1.0 copy-start.9
  79.3 0.7 copy-start.14
  80.0 23.8 %all-to-all-start.2 = ((bf16[4,4,4,16,512]{4,3,2,1,0:T(8,128)(2,1)}), bf16[4,4,4,16,512]{4,3,2,1,0:T(8,128)(2,1)S(1)}, u32[]{:S(2)}, u32[]{:S(2)}) async-start(bf16[4,4,4,16,512]{4,3,2,1,0:T(8,128)(2,1)} %copy-done.9), calls=%async_computation.2 | async-start | bytes 2097152 | tf_op jit(solution)/shard_map/all_to_all | solution.py:199
  85.6 18.2 %collective-permute-start.3 = (bf16[4,4,16,512]{3,2,1,0:T(8,128)(2,1)}, bf16[4,4,16,512]{3,2,1,0:T(8,128)(2,1)}, u32[]{:S(2)}, u32[]{:S(2)}) collective-permute-start(bf16[4,4,16,512]{3,2,1,0:T(8,128)(2,1)} %copy-done.14), channel_id=1, source_target_pairs={{0,32},{16,48},{32,64},{48,80},{64,96},{80,112},{96,128},{112,144}... | collective-permute-start | bytes 786440 | tf_op jit(solution)/shard_map/ppermute | solution.py:186
  87.5 16.2 %collective-permute-start.4 = (bf16[4,4,16,512]{3,2,1,0:T(8,128)(2,1)}, bf16[4,4,16,512]{3,2,1,0:T(8,128)(2,1)}, u32[]{:S(2)}, u32[]{:S(2)}) collective-permute-start(bf16[4,4,16,512]{3,2,1,0:T(8,128)(2,1)} %copy-done.14), channel_id=1, source_target_pairs={{0,480},{16,496},{32,0},{48,16},{64,32},{80,48},{96,64},{112,80},{... | collective-permute-start | bytes 786440 | tf_op jit(solution)/shard_map/ppermute | solution.py:186
  91.4 12.3 %collective-permute-start.5 = (bf16[4,4,16,512]{3,2,1,0:T(8,128)(2,1)}, bf16[4,4,16,512]{3,2,1,0:T(8,128)(2,1)}, u32[]{:S(2)}, u32[]{:S(2)}) collective-permute-start(bf16[4,4,16,512]{3,2,1,0:T(8,128)(2,1)} %copy-done.14), channel_id=1, source_target_pairs={{0,64},{16,80},{32,480},{48,496},{64,128},{80,144},{96,32},{112,48... | collective-permute-start | bytes 786440 | tf_op jit(solution)/shard_map/ppermute | solution.py:186
  98.3 5.5 %copy-start.4 = (f32[512,128]{1,0:T(8,128)}, f32[512,128]{1,0:T(8,128)S(1)}, u32[]{:S(2)}) copy-start(f32[512,128]{1,0:T(8,128)S(1)} %get-tuple-element.19.sin_ref) | copy-start | bytes 786436
  98.3 2.3 %copy-start.2 = (bf16[512,4096]{1,0:T(8,128)(2,1)S(1)}, bf16[512,4096]{1,0:T(8,128)(2,1)}, u32[]{:S(2)}) copy-start(bf16[512,4096]{1,0:T(8,128)(2,1)} %fusion.2.refs_4_.after_ref.x_ref) | copy-start | bytes 12582916
  100.6 9.2 %copy-start.17 = (s32[1,2048]{1,0:T(1,128)S(1)}, s32[1,2048]{1,0:T(1,128)}, u32[]{:S(2)}) copy-start(s32[1,2048]{1,0:T(1,128)} %param.11) | copy-start | bytes 24580
  103.0 0.7 copy-start.6
  103.8 1.0 copy-start.7
  104.7 0.9 copy-start.15
  107.9 7.9 %collective-permute-start.7 = (bf16[2048,512]{1,0:T(8,128)(2,1)S(1)}, bf16[2048,512]{1,0:T(8,128)(2,1)}, u32[]{:S(2)}, u32[]{:S(2)}) collective-permute-start(bf16[2048,512]{1,0:T(8,128)(2,1)S(1)} %bitcast.17), channel_id=1, source_target_pairs={{0,16},{16,0},{32,48},{48,32},{64,80},{80,64},{96,112},{112,96},{1... | collective-permute-start | bytes 6291464 | tf_op jit(solution)/shard_map/ppermute | solution.py:270
  110.5 13.6 %collective-permute-start.8 = (bf16[512,256]{1,0:T(8,128)(2,1)}, bf16[512,256]{1,0:T(8,128)(2,1)}, u32[]{:S(2)}, u32[]{:S(2)}) collective-permute-start(bf16[512,256]{1,0:T(8,128)(2,1)} %copy-done.6), channel_id=1, source_target_pairs={{0,2},{1,3},{4,6},{5,7},{8,10},{9,11},{12,14},{13,15},{16,18},{17,... | collective-permute-start | bytes 786440 | tf_op jit(solution)/shard_map/ppermute | solution.py:306
  111.8 16.7 %collective-permute-start.9 = (bf16[512,256]{1,0:T(8,128)(2,1)}, bf16[512,256]{1,0:T(8,128)(2,1)}, u32[]{:S(2)}, u32[]{:S(2)}) collective-permute-start(bf16[512,256]{1,0:T(8,128)(2,1)} %copy-done.6), channel_id=1, source_target_pairs={{0,1},{1,2},{2,3},{4,5},{5,6},{6,7},{8,9},{9,10},{10,11},{12,13},{... | collective-permute-start | bytes 786440 | tf_op jit(solution)/shard_map/ppermute | solution.py:305
  115.8 2.2 %copy-start.3 = (bf16[512,4096]{1,0:T(8,128)(2,1)S(1)}, bf16[512,4096]{1,0:T(8,128)(2,1)}, u32[]{:S(2)}) copy-start(bf16[512,4096]{1,0:T(8,128)(2,1)} %fusion.2.refs_4_.after_ref.x_ref) | copy-start | bytes 12582916
  118.0 0.9 copy-start.5
  118.9 9.6 %copy-start.8 = (bf16[512,256]{1,0:T(8,128)(2,1)S(1)}, bf16[512,256]{1,0:T(8,128)(2,1)}, u32[]{:S(2)}) copy-start(bf16[512,256]{1,0:T(8,128)(2,1)} %copy-done.6) | copy-start | bytes 786436
  118.9 9.6 %copy-start.16 = (s32[512,1]{1,0:T(8,128)S(1)}, s32[512,1]{1,0:T(8,128)}, u32[]{:S(2)}) copy-start(s32[512,1]{1,0:T(8,128)} %copy.9.low_ref) | copy-start | bytes 6148

commit v4 on v2

v4 whole, which is shorter than its diff:
```python
import functools
import math

import jax
import jax.numpy as jnp
from jax import lax
from jax.experimental import pallas as pl
from jax.experimental.pallas import tpu as pltpu
from jax.sharding import PartitionSpec as P

HEAD_SIZE = 128
KEY_BLOCK = 256
QUERY_BLOCK = 128


def rotary_tables(positions):
    half_dim = HEAD_SIZE // 2
    frequency = jnp.exp(
        jnp.arange(half_dim, dtype=jnp.float32) * (-2.0 * math.log(500000.0) / HEAD_SIZE)
    )
    angles = positions.astype(jnp.float32)[:, None] * frequency[None, :]
    cosine, sine = jnp.cos(angles), jnp.sin(angles)
    return jnp.concatenate([cosine, cosine], 1), jnp.concatenate([-sine, sine], 1)


def rotate(u, cosine, sine):
    return u * cosine + pltpu.roll(u, HEAD_SIZE // 2, 1) * sine


def kv_kernel(core_ref, x_ref, wa_ref, wb_ref, cos_ref, sin_ref, out_ref, acc_ref):
    step = pl.program_id(0)
    first = core_ref[0] == 0
    rows = []
    for chip in range(wa_ref.shape[1]):
        own = jnp.concatenate([wa_ref[k, chip] for k in range(wa_ref.shape[0])], axis=0)
        other = jnp.concatenate([wb_ref[k, chip] for k in range(wb_ref.shape[0])], axis=0)
        rows += [jnp.where(first, own, other), jnp.where(first, other, own)]
    part = jnp.dot(x_ref[...], jnp.concatenate(rows, axis=0), preferred_element_type=jnp.float32)

    @pl.when(step == 0)
    def _():
        acc_ref[...] = part

    @pl.when(step > 0)
    def _():
        acc_ref[...] += part

    @pl.when(step == pl.num_programs(0) - 1)
    def _():
        keys = rotate(acc_ref[:, :HEAD_SIZE], cos_ref[...], sin_ref[...])
        out_ref[:, :HEAD_SIZE] = keys.astype(jnp.bfloat16)
        out_ref[:, HEAD_SIZE:] = acc_ref[:, HEAD_SIZE:].astype(jnp.bfloat16)


def project_kv(core, x, wa, wb, cosine, sine, steps=4):
    rows, depth = x.shape
    quarters, chips, part, width = wa.shape
    w_spec = pl.BlockSpec((quarters, chips // steps, part, width), lambda s: (0, s, 0, 0))
    table = pl.BlockSpec((rows, HEAD_SIZE), lambda s: (0, 0))
    return pl.pallas_call(
        kv_kernel,
        grid=(steps,),
        in_specs=[
            pl.BlockSpec(memory_space=pltpu.SMEM),
            pl.BlockSpec((rows, depth // steps), lambda s: (0, s)),
            w_spec,
            w_spec,
            table,
            table,
        ],
        out_specs=pl.BlockSpec((rows, width), lambda s: (0, 0)),
        out_shape=jax.ShapeDtypeStruct((rows, width), jnp.bfloat16),
        scratch_shapes=[pltpu.VMEM((rows, width), jnp.float32)],
        compiler_params=pltpu.CompilerParams(vmem_limit_bytes=20 * 1024 * 1024),
        cost_estimate=pl.CostEstimate(
            flops=2 * rows * depth * width,
            bytes_accessed=2 * (rows * depth + depth * width + rows * width),
            transcendentals=0,
        ),
    )(core, x, wa, wb, cosine, sine)


def attend_kernel(
    first_ref, low_ref, x_ref, cos_ref, sin_ref, kv2_ref, kv1_ref, kv0_ref, w_ref,
    out_ref, x, w, q, keys, values, sums, acc, sems,
):
    rows, depth = x_ref.shape
    width = out_ref.shape[1]
    heads = width // HEAD_SIZE
    pieces = sems.shape[1]
    piece = depth // pieces
    copies = []
    for n in range(pieces):
        take = pl.ds(n * piece, piece)
        copies.append(pltpu.make_async_copy(w_ref.at[take], w.at[take], sems.at[0, n]))
        copies[-1].start()
        copies.append(pltpu.make_async_copy(x_ref.at[:, take], x.at[:, take], sems.at[1, n]))
        copies[-1].start()

    for n, ref in enumerate((kv2_ref, kv1_ref, kv0_ref)):
        keys[n * rows : (n + 1) * rows] = ref[:, :HEAD_SIZE]
        values[:, n * rows : (n + 1) * rows] = ref[:, HEAD_SIZE:].T

    for n in range(pieces):
        copies[2 * n].wait()
        copies[2 * n + 1].wait()
        take = slice(n * piece, (n + 1) * piece)
        part = jnp.dot(x[:, take], w[take], preferred_element_type=jnp.float32)
        if n == 0:
            sums[...] = part
        else:
            sums[...] += part
    for h in range(heads):
        lanes = slice(h * HEAD_SIZE, (h + 1) * HEAD_SIZE)
        q[:, lanes] = rotate(sums[:, lanes], cos_ref[...], sin_ref[...]).astype(jnp.bfloat16)

    key_lane = lax.broadcasted_iota(jnp.int32, (KEY_BLOCK, QUERY_BLOCK), 0)
    query_lane = lax.broadcasted_iota(jnp.int32, (KEY_BLOCK, QUERY_BLOCK), 1)
    to_log2 = math.log2(math.e) / math.sqrt(HEAD_SIZE)
    for step in range(rows // QUERY_BLOCK):
        block = slice(step * QUERY_BLOCK, (step + 1) * QUERY_BLOCK)
        queries = jnp.concatenate(
            [q[block, h * HEAD_SIZE : (h + 1) * HEAD_SIZE] for h in range(heads)], axis=0
        )
        low = low_ref[step : step + 1, :]
        first_query = 2 * rows + step * QUERY_BLOCK
        acc[...] = jnp.zeros_like(acc)

        def visit(n, carry):
            run_max, run_sum = carry
            start = pl.multiple_of(n * KEY_BLOCK, KEY_BLOCK)
            scores = lax.dot_general(
                keys[pl.ds(start, KEY_BLOCK)],
                queries,
                (((1,), (1,)), ((), ())),
                preferred_element_type=jnp.float32,
            )
            visible = (start + key_lane >= low) & (start + key_lane <= first_query + query_lane)
            visible = jnp.concatenate([visible] * heads, axis=1)
            scores = jnp.where(visible, scores, -1e30)
            new_max = jnp.maximum(run_max, jnp.max(scores, axis=0, keepdims=True))
            factor = jnp.exp2((run_max - new_max) * to_log2)
            weights = jnp.exp2((scores - new_max) * to_log2)
            run_sum = run_sum * factor + jnp.sum(weights, axis=0, keepdims=True)
            acc[...] = acc[...] * factor + jnp.dot(
                values[:, pl.ds(start, KEY_BLOCK)],
                weights.astype(jnp.bfloat16),
                preferred_element_type=jnp.float32,
            )
            return new_max, run_sum

        initial = (
            jnp.full((1, width), -1e30, jnp.float32),
            jnp.zeros((1, width), jnp.float32),
        )
        last = (first_query + QUERY_BLOCK - 1) // KEY_BLOCK + 1
        _, run_sum = lax.fori_loop(first_ref[step], last, visit, initial)
        mixed = acc[...] / run_sum
        for h in range(heads):
            lanes = slice(h * HEAD_SIZE, (h + 1) * HEAD_SIZE)
            out_ref[block, lanes] = mixed[:, lanes].T.astype(jnp.bfloat16)


def attend(first, low, x, cosine, sine, kv2, kv1, kv0, w, pieces=4):
    rows, depth = x.shape
    width = w.shape[1]
    whole = pl.BlockSpec(memory_space=pltpu.VMEM)
    return pl.pallas_call(
        attend_kernel,
        in_specs=[pl.BlockSpec(memory_space=pltpu.SMEM)]
        + [whole, pl.BlockSpec(memory_space=pl.ANY)]
        + [whole] * 5
        + [pl.BlockSpec(memory_space=pl.ANY)],
        out_specs=whole,
        out_shape=jax.ShapeDtypeStruct((rows, width), jnp.bfloat16),
        scratch_shapes=[
            pltpu.VMEM((rows, depth), jnp.bfloat16),
            pltpu.VMEM((depth, width), jnp.bfloat16),
            pltpu.VMEM((rows, width), jnp.bfloat16),
            pltpu.VMEM((3 * rows, HEAD_SIZE), jnp.bfloat16),
            pltpu.VMEM((HEAD_SIZE, 3 * rows), jnp.bfloat16),
            pltpu.VMEM((rows, width), jnp.float32),
            pltpu.VMEM((HEAD_SIZE, width), jnp.float32),
            pltpu.SemaphoreType.DMA((2, pieces)),
        ],
        compiler_params=pltpu.CompilerParams(vmem_limit_bytes=60 * 1024 * 1024),
        cost_estimate=pl.CostEstimate(
            flops=2 * rows * depth * width + 8 * rows * rows * width,
            bytes_accessed=2 * (rows * depth + depth * width),
            transcendentals=0,
        ),
    )(first, low, x, cosine, sine, kv2, kv1, kv0, w)


def normalize(tokens, norm_gain):
    widened = tokens.astype(jnp.float32)
    mean_sq = jnp.mean(widened * widened, axis=-1, keepdims=True)
    return (widened * lax.rsqrt(mean_sq + 1e-05) * norm_gain.astype(jnp.float32)).astype(
        jnp.bfloat16
    )


def gather_key_value(mine):
    me = lax.axis_index("attn")
    parts = lax.axis_size("attn")
    devices = lax.axis_size("rows")
    rows, width = mine.shape
    quarter = rows // parts
    own = lax.dynamic_slice_in_dim(mine, me * quarter, quarter, 0)
    chips = devices // 2
    same_core = [[2 * z + c for z in range(chips)] for c in range(2)]
    column = lax.all_gather(own, "rows", axis=0, tiled=True, axis_index_groups=same_core)
    spread = jnp.broadcast_to(column[None], (parts, chips * quarter, width))
    half = lax.all_to_all(spread, "attn", 0, 0, tiled=True)
    half = half.reshape(parts, chips, quarter, width)
    return half, lax.ppermute(half, "rows", [(i, i ^ 1) for i in range(devices)])


def on_device(
    tokens, norm_gain, w_query, key_projection_weight, value_projection_weight, documents
):
    rows = tokens.shape[0]
    me = lax.axis_index("attn")
    query_weights = lax.all_gather(w_query, "rows", axis=0, tiled=True)
    kv_weights = gather_key_value(
        jnp.concatenate([key_projection_weight, value_projection_weight], 1)
    )

    normed = normalize(tokens, norm_gain)
    cosine, sine = rotary_tables(me * rows + jnp.arange(rows, dtype=jnp.int32))
    doc_ids = documents[0]
    my_docs = lax.dynamic_slice_in_dim(doc_ids, me * rows, rows)
    begin = jnp.sum((doc_ids[None, :] < my_docs[:, None]).astype(jnp.int32), axis=1)
    low = jnp.maximum(begin - (me - 2) * rows, 0).reshape(-1, QUERY_BLOCK)
    first = low[:, 0] // KEY_BLOCK

    core = (lax.axis_index("rows") % 2).astype(jnp.int32).reshape(1)
    kv = project_kv(core, normed, *kv_weights, cosine, sine)
    kv1 = lax.ppermute(kv, "attn", [(0, 1), (1, 2), (2, 3)])
    kv2 = lax.ppermute(kv, "attn", [(0, 2), (1, 3)])
    return attend(first, low, normed, cosine, sine, kv2, kv1, kv, query_weights)


def solution(mesh):
    placed = (
        P(("rows", "attn"), None),
        P(),
        P("rows", "tp"),
        P("rows", "tp"),
        P("rows", "tp"),
        P("rows", None),
    )
    return jax.shard_map(
        on_device, mesh=mesh, in_specs=placed, out_specs=P(("rows", "attn"), "tp"), check_vma=False
    )
```

time: 114 us -> 110 us (0.965)
  the two profiles are of different devices: /device:TPU:17 before, /device:TPU:11 now
where the time goes in v4:
time: 110 us
  blocking collectives  29.7 us (27%)
  starting transfers between devices  20.8 us (19%)
  Pallas kernels  16.6 us (15%)
  waiting for transfers between devices  14.5 us (13%)
  between operations  13.6 us (12%)
  other arithmetic  10.8 us (10%)
  local copies, waits for them, and re-layouts  3.83 us (3%)
    all_gather x1, blocking collectives, gather_key_value(): lax.all_gather(own, 'rows', axis=0, tiled=True, axis_index_groups=same_core)  29.7 us
    pallas_call x1, Pallas kernels, attend(): pl.pallas_call(attend_kernel, in_specs=[pl.BlockSpec(memory_space=pltpu.S...  14 us
    ppermute x1, starting transfers between devices, gather_key_value(): lax.ppermute(half, 'rows', [(i, i ^ 1) for i in range(devices)])  11.3 us
    ppermute x1, waiting for transfers between devices, on_device(): kv1 = lax.ppermute(kv, 'attn', [(0, 1), (1, 2), (2, 3)])  6.69 us
    all_to_all x1, starting transfers between devices, gather_key_value(): half = lax.all_to_all(spread, 'attn', 0, 0, tiled=True)  4.47 us
    convert_element_type x1, other arithmetic, normalize(): (widened * lax.rsqrt(mean_sq + 1e-05) * norm_gain.astype(jnp.float32)).as...  3.87 us
    reduce_sum x1, other arithmetic, normalize(): mean_sq = jnp.mean(widened * widened, axis=-1, keepdims=True)  3.13 us
    ppermute x1, starting transfers between devices, on_device(): kv2 = lax.ppermute(kv, 'attn', [(0, 2), (1, 3)])  3.1 us
  transfers between devices with their start and end apart: 5, of which 4 were waited for; matrix products, arithmetic and copies ran while one was open for 12% of the time, Pallas kernels for 2%

profile of v4, /device:TPU:11, one launch (start us, length us, event | category | flops | bytes accessed | tf_op | source)
XLA Modules:
  0.0 109.7 jit_solution(4139918361552671916)
XLA Ops:
  6.5 0.0 copy-start.4
  6.5 0.0 all-gather.2.cloned.1.call-start
  6.5 0.7 all-gather.2.cloned.1.call-update
  7.3 0.7 fusion.4
  8.0 29.7 %all_gather.6 = bf16[512,256]{1,0:T(8,128)(2,1)S(1)} all-gather(bf16[32,256]{1,0:T(8,128)(2,1)S(1)} %fusion.4), channel_id=1, replica_groups={{0,32,64,96,128,160,192,224,256,288,320,352,384,416,448,480},{16,48,80,..., dimensions={0}, use_global_device_ids=true | all-gather | bytes 278528 | tf_op jit(solution)/shard_map/all_gather | solution.py:212
  37.6 1.0 broadcast_in_dim.2
  38.7 4.5 %all-to-all-start = ((bf16[4,512,256]{2,1,0:T(8,128)(2,1)}), bf16[4,512,256]{2,1,0:T(8,128)(2,1)S(1)}, u32[]{:S(2)}, u32[]{:S(2)}) async-start(bf16[4,512,256]{2,1,0:T(8,128)(2,1)} %broadcast_in_dim.2), calls=%async_computation | async-start | bytes 2097152 | tf_op jit(solution)/shard_map/all_to_all | solution.py:214
  43.2 0.7 convert_element_type.21
  43.9 0.7 constant_dynamic-slice_fusion
  44.6 1.0 fusion.3
  45.6 0.2 pad_maximum_fusion
  45.8 0.0 copy-start.1
  45.8 0.0 copy-start.2
  45.8 0.0 copy-done.4
  45.8 0.6 convert_reduce_fusion
  46.4 3.1 %fusion = f32[512]{0:T(512)S(1)} fusion(bf16[512,4096]{1,0:T(8,128)(2,1)} %param.6), kind=kLoop, calls=%fused_computation.2 | loop fusion | flops 6290944 | bytes 4196352 | tf_op jit(solution)/shard_map/reduce_sum | solution.py:197
  49.5 0.0 copy-start.5
  49.6 2.2 %all-to-all-done = bf16[4,512,256]{2,1,0:T(8,128)(2,1)S(1)} async-done(((bf16[4,512,256]{2,1,0:T(8,128)(2,1)}), bf16[4,512,256]{2,1,0:T(8,128)(2,1)S(1)}, u32[]{:S(2)}, u32[]{:S(2)}) %all-to-all-start) | async-done | bytes 1048608 | tf_op jit(solution)/shard_map/all_to_all | solution.py:214
  51.7 11.3 %collective-permute-start = (bf16[4,16,32,256]{3,2,1,0:T(8,128)(2,1)S(1)}, bf16[4,16,32,256]{3,2,1,0:T(8,128)(2,1)S(1)}, u32[]{:S(2)}, u32[]{:S(2)}) collective-permute-start(bf16[4,16,32,256]{3,2,1,0:T(8,128)(2,1)S(1)} %bitcast.6), channel_id=1, source_target_pairs={{0,16},{16,0},{32,48},{48,32},{64,80},{80,64},{96,112},{112,96},{1... | collective-permute-start | bytes 3145736 | tf_op jit(solution)/shard_map/ppermute | solution.py:216
  63.1 3.9 %fusion.2.x_ref = bf16[512,4096]{1,0:T(8,128)(2,1)S(1)} fusion(bf16[512,4096]{1,0:T(8,128)(2,1)} %param.6, f32[4096]{0:T(1024)S(1)} %convert_element_type.21, f32[512]{0:T(512)S(1)} %add_rsqrt_fusion), kind=kLoop, calls=%fused_computation.4 | loop fusion | flops 8388608 | bytes 8407040 | tf_op jit(solution)/shard_map/convert_element_type | solution.py:198
  66.9 0.0 collective-permute-done.wb_ref
  67.0 0.0 copy-done.1
  67.0 0.0 copy-done.2
  67.0 2.6 %shard_map.64.kv0_ref = bf16[512,256]{1,0:T(8,128)(2,1)S(1)} custom-call(s32[1]{0:T(128)} %bitcast.3.core_ref, bf16[512,4096]{1,0:T(8,128)(2,1)S(1)} %fusion.2.x_ref, bf16[4,16,32,256]{3,2,1,0:T(8,128)(2,1)S(1)} %bitcast.7, bf16[4,16,32,256]{3,2,1,0:T(8,128)(2,1)S(1)} %collective-permute-done.wb_ref, f32[512,128]{1,0:T(8,128)S(1)} %get-tuple-element.8.cos_ref, ...), custom_call_target="tpu_custom_call" | custom-call | flops 1073741824 | bytes 6553600 | tf_op jit(solution)/shard_map/pallas_call | solution.py:60
  69.6 0.0 copy-start
  69.6 2.0 %copy-done = bf16[512,4096]{1,0:T(8,128)(2,1)} copy-done((bf16[512,4096]{1,0:T(8,128)(2,1)}, bf16[512,4096]{1,0:T(8,128)(2,1)S(1)}, u32[]{:S(2)}) %copy-start) | copy-done | bytes 4194328
  71.6 0.0 copy-start.3
  71.6 3.1 %collective-permute-start.1 = (bf16[512,256]{1,0:T(8,128)(2,1)S(1)}, bf16[512,256]{1,0:T(8,128)(2,1)S(1)}, u32[]{:S(2)}, u32[]{:S(2)}) collective-permute-start(bf16[512,256]{1,0:T(8,128)(2,1)S(1)} %shard_map.64.kv0_ref), channel_id=1, source_target_pairs={{0,2},{1,3},{4,6},{5,7},{8,10},{9,11},{12,14},{13,15},{16,18},{17,... | collective-permute-start | bytes 786440 | tf_op jit(solution)/shard_map/ppermute | solution.py:240
  74.7 1.9 %collective-permute-start.2 = (bf16[512,256]{1,0:T(8,128)(2,1)S(1)}, bf16[512,256]{1,0:T(8,128)(2,1)S(1)}, u32[]{:S(2)}, u32[]{:S(2)}) collective-permute-start(bf16[512,256]{1,0:T(8,128)(2,1)S(1)} %shard_map.64.kv0_ref), channel_id=1, source_target_pairs={{0,1},{1,2},{2,3},{4,5},{5,6},{6,7},{8,9},{9,10},{10,11},{12,13},{... | collective-permute-start | bytes 786440 | tf_op jit(solution)/shard_map/ppermute | solution.py:239
  76.6 0.0 copy-done.5
  76.6 0.1 slice_reduce_fusion
  76.7 0.6 and_select_fusion.first_ref
  77.3 3.1 %collective-permute-done.1.kv2_ref = bf16[512,256]{1,0:T(8,128)(2,1)S(1)} collective-permute-done((bf16[512,256]{1,0:T(8,128)(2,1)S(1)}, bf16[512,256]{1,0:T(8,128)(2,1)S(1)}, u32[]{:S(2)}, u32[]{:S(2)}) %collective-permute-start.1) | collective-permute-done | bytes 262176 | tf_op jit(solution)/shard_map/ppermute | solution.py:240
  80.4 0.0 copy-start.6
  80.4 6.7 %collective-permute-done.2.kv1_ref = bf16[512,256]{1,0:T(8,128)(2,1)S(1)} collective-permute-done((bf16[512,256]{1,0:T(8,128)(2,1)S(1)}, bf16[512,256]{1,0:T(8,128)(2,1)S(1)}, u32[]{:S(2)}, u32[]{:S(2)}) %collective-permute-start.2) | collective-permute-done | bytes 262176 | tf_op jit(solution)/shard_map/ppermute | solution.py:239
  87.1 0.0 copy-start.7
  87.1 1.8 %all-gather.2.cloned.1.call-done.w_ref = bf16[4096,512]{1,0:T(8,128)(2,1)} async-done(((bf16[128,512]{1,0:T(8,128)(2,1)}), bf16[4096,512]{1,0:T(8,128)(2,1)}) %all-gather.2.cloned.1.call-update) | async-done | bytes 4194320 | tf_op jit(solution)/shard_map/all_gather | solution.py:224
  88.9 0.0 copy-done.3
  88.9 0.0 copy-done.6
  88.9 0.0 copy-done.7
  88.9 14.0 %shard_map.65 = bf16[512,512]{1,0:T(8,128)(2,1)} custom-call(s32[4]{0:T(128)} %and_select_fusion.first_ref, s32[4,128]{1,0:T(4,128)} %copy-done.5, bf16[512,4096]{1,0:T(8,128)(2,1)} %copy-done, f32[512,128]{1,0:T(8,128)} %copy-done.1, f32[512,128]{1,0:T(8,128)} %copy-done.2, bf16[512,256]{1,0:T(8,128)(2,1)} %copy-done.6, bf16[512,256]{1,0:T(8,128)(2,1)} %copy-done.7, ...), custom_call_target="tpu_custom_call" | custom-call | flops 3221225472 | bytes 8388608 | tf_op jit(solution)/shard_map/pallas_call | solution.py:168
  (4 shorter events, 0.0 us)
Async XLA Ops:
  6.5 39.3 %copy-start.4 = (s32[1,2048]{1,0:T(1,128)S(1)}, s32[1,2048]{1,0:T(1,128)}, u32[]{:S(2)}) copy-start(s32[1,2048]{1,0:T(1,128)} %param.11) | copy-start | bytes 24580
  6.5 82.4 %all-gather.2.cloned.1.call-start = ((), (), s32[]{:S(2)}) async-start(), calls=%async_computation.1 | async-start | bytes 4325376 | tf_op jit(solution)/shard_map/all_gather | solution.py:224
  38.7 13.0 %all-to-all-start = ((bf16[4,512,256]{2,1,0:T(8,128)(2,1)}), bf16[4,512,256]{2,1,0:T(8,128)(2,1)S(1)}, u32[]{:S(2)}, u32[]{:S(2)}) async-start(bf16[4,512,256]{2,1,0:T(8,128)(2,1)} %broadcast_in_dim.2), calls=%async_computation | async-start | bytes 2097152 | tf_op jit(solution)/shard_map/all_to_all | solution.py:214
  45.8 21.2 %copy-start.1 = (f32[512,128]{1,0:T(8,128)}, f32[512,128]{1,0:T(8,128)S(1)}, u32[]{:S(2)}) copy-start(f32[512,128]{1,0:T(8,128)S(1)} %get-tuple-element.8.cos_ref) | copy-start | bytes 786436
  45.8 21.2 %copy-start.2 = (f32[512,128]{1,0:T(8,128)}, f32[512,128]{1,0:T(8,128)S(1)}, u32[]{:S(2)}) copy-start(f32[512,128]{1,0:T(8,128)S(1)} %get-tuple-element.9.sin_ref) | copy-start | bytes 786436
  49.5 27.1 %copy-start.5 = (s32[4,128]{1,0:T(4,128)}, s32[4,128]{1,0:T(4,128)S(1)}, u32[]{:S(2)}) copy-start(s32[4,128]{1,0:T(4,128)S(1)} %maximum_bitcast_fusion.low_ref) | copy-start | bytes 6148
  51.7 15.2 %collective-permute-start = (bf16[4,16,32,256]{3,2,1,0:T(8,128)(2,1)S(1)}, bf16[4,16,32,256]{3,2,1,0:T(8,128)(2,1)S(1)}, u32[]{:S(2)}, u32[]{:S(2)}) collective-permute-start(bf16[4,16,32,256]{3,2,1,0:T(8,128)(2,1)S(1)} %bitcast.6), channel_id=1, source_target_pairs={{0,16},{16,0},{32,48},{48,32},{64,80},{80,64},{96,112},{112,96},{1... | collective-permute-start | bytes 3145736 | tf_op jit(solution)/shard_map/ppermute | solution.py:216
  69.6 2.0 %copy-start = (bf16[512,4096]{1,0:T(8,128)(2,1)}, bf16[512,4096]{1,0:T(8,128)(2,1)S(1)}, u32[]{:S(2)}) copy-start(bf16[512,4096]{1,0:T(8,128)(2,1)S(1)} %fusion.2.x_ref) | copy-start | bytes 12582916
  71.6 17.4 %copy-start.3 = (bf16[512,256]{1,0:T(8,128)(2,1)}, bf16[512,256]{1,0:T(8,128)(2,1)S(1)}, u32[]{:S(2)}) copy-start(bf16[512,256]{1,0:T(8,128)(2,1)S(1)} %shard_map.64.kv0_ref) | copy-start | bytes 786436
  71.6 8.8 %collective-permute-start.1 = (bf16[512,256]{1,0:T(8,128)(2,1)S(1)}, bf16[512,256]{1,0:T(8,128)(2,1)S(1)}, u32[]{:S(2)}, u32[]{:S(2)}) collective-permute-start(bf16[512,256]{1,0:T(8,128)(2,1)S(1)} %shard_map.64.kv0_ref), channel_id=1, source_target_pairs={{0,2},{1,3},{4,6},{5,7},{8,10},{9,11},{12,14},{13,15},{16,18},{17,... | collective-permute-start | bytes 786440 | tf_op jit(solution)/shard_map/ppermute | solution.py:240
  74.7 12.4 %collective-permute-start.2 = (bf16[512,256]{1,0:T(8,128)(2,1)S(1)}, bf16[512,256]{1,0:T(8,128)(2,1)S(1)}, u32[]{:S(2)}, u32[]{:S(2)}) collective-permute-start(bf16[512,256]{1,0:T(8,128)(2,1)S(1)} %shard_map.64.kv0_ref), channel_id=1, source_target_pairs={{0,1},{1,2},{2,3},{4,5},{5,6},{6,7},{8,9},{9,10},{10,11},{12,13},{... | collective-permute-start | bytes 786440 | tf_op jit(solution)/shard_map/ppermute | solution.py:239
  80.4 8.5 %copy-start.6 = (bf16[512,256]{1,0:T(8,128)(2,1)}, bf16[512,256]{1,0:T(8,128)(2,1)S(1)}, u32[]{:S(2)}) copy-start(bf16[512,256]{1,0:T(8,128)(2,1)S(1)} %collective-permute-done.1.kv2_ref) | copy-start | bytes 786436
  87.1 1.8 %copy-start.7 = (bf16[512,256]{1,0:T(8,128)(2,1)}, bf16[512,256]{1,0:T(8,128)(2,1)S(1)}, u32[]{:S(2)}) copy-start(bf16[512,256]{1,0:T(8,128)(2,1)S(1)} %collective-permute-done.2.kv1_ref) | copy-start | bytes 786436
Sparse Core Ops, SparseCore 0:
  9.5 79.3 all-gather.1

commit v5 on v4

--- a/solution.py
+++ b/solution.py
@@ -9,7 +9,7 @@
 from jax.sharding import PartitionSpec as P
 
 HEAD_SIZE = 128
-KEY_BLOCK = 256
+KEY_BLOCK = 512
 QUERY_BLOCK = 128
 
 
@@ -82,24 +82,32 @@
 
 def attend_kernel(
     first_ref, low_ref, x_ref, cos_ref, sin_ref, kv2_ref, kv1_ref, kv0_ref, w_ref,
-    out_ref, x, w, q, keys, values, sums, acc, sems,
+    out_ref, x, w, cos, sin, q, keys, plain, values, sums, acc, sems,
 ):
     rows, depth = x_ref.shape
     width = out_ref.shape[1]
     heads = width // HEAD_SIZE
-    pieces = sems.shape[1]
+    pieces = (sems.shape[0] - 8) // 2
     piece = depth // pieces
     copies = []
+
+    def bring(src, dst):
+        copies.append(pltpu.make_async_copy(src, dst, sems.at[len(copies)]))
+        copies[-1].start()
+
     for n in range(pieces):
         take = pl.ds(n * piece, piece)
-        copies.append(pltpu.make_async_copy(w_ref.at[take], w.at[take], sems.at[0, n]))
-        copies[-1].start()
-        copies.append(pltpu.make_async_copy(x_ref.at[:, take], x.at[:, take], sems.at[1, n]))
-        copies[-1].start()
-
-    for n, ref in enumerate((kv2_ref, kv1_ref, kv0_ref)):
-        keys[n * rows : (n + 1) * rows] = ref[:, :HEAD_SIZE]
-        values[:, n * rows : (n + 1) * rows] = ref[:, HEAD_SIZE:].T
+        bring(w_ref.at[take], w.at[take])
+        bring(x_ref.at[:, take], x.at[:, take])
+        if n == 0:
+            for at, ref in enumerate((kv2_ref, kv1_ref, kv0_ref)):
+                part = pl.ds(at * rows, rows)
+                bring(ref.at[:, :HEAD_SIZE], keys.at[part])
+                bring(ref.at[:, HEAD_SIZE:], plain.at[part])
+            bring(cos_ref, cos)
+            bring(sin_ref, sin)
+    others = copies[2:10]
+    copies = copies[:2] + copies[10:]
 
     for n in range(pieces):
         copies[2 * n].wait()
@@ -110,9 +118,14 @@
             sums[...] = part
         else:
             sums[...] += part
+        if n == 0:
+            for copy in others:
+                copy.wait()
+            for at in range(0, 3 * rows, rows):
+                values[:, at : at + rows] = plain[at : at + rows].T
     for h in range(heads):
         lanes = slice(h * HEAD_SIZE, (h + 1) * HEAD_SIZE)
-        q[:, lanes] = rotate(sums[:, lanes], cos_ref[...], sin_ref[...]).astype(jnp.bfloat16)
+        q[h] = rotate(sums[:, lanes], cos[...], sin[...]).T.astype(jnp.bfloat16)
 
     key_lane = lax.broadcasted_iota(jnp.int32, (KEY_BLOCK, QUERY_BLOCK), 0)
     query_lane = lax.broadcasted_iota(jnp.int32, (KEY_BLOCK, QUERY_BLOCK), 1)
@@ -120,7 +133,7 @@
     for step in range(rows // QUERY_BLOCK):
         block = slice(step * QUERY_BLOCK, (step + 1) * QUERY_BLOCK)
         queries = jnp.concatenate(
-            [q[block, h * HEAD_SIZE : (h + 1) * HEAD_SIZE] for h in range(heads)], axis=0
+            [q[h, :, block] for h in range(heads)], axis=1
         )
         low = low_ref[step : step + 1, :]
         first_query = 2 * rows + step * QUERY_BLOCK
@@ -129,11 +142,8 @@
         def visit(n, carry):
             run_max, run_sum = carry
             start = pl.multiple_of(n * KEY_BLOCK, KEY_BLOCK)
-            scores = lax.dot_general(
-                keys[pl.ds(start, KEY_BLOCK)],
-                queries,
-                (((1,), (1,)), ((), ())),
-                preferred_element_type=jnp.float32,
+            scores = jnp.dot(
+                keys[pl.ds(start, KEY_BLOCK)], queries, preferred_element_type=jnp.float32
             )
             visible = (start + key_lane >= low) & (start + key_lane <= first_query + query_lane)
             visible = jnp.concatenate([visible] * heads, axis=1)
@@ -161,27 +171,29 @@
             out_ref[block, lanes] = mixed[:, lanes].T.astype(jnp.bfloat16)
 
 
-def attend(first, low, x, cosine, sine, kv2, kv1, kv0, w, pieces=4):
+def attend(first, low, x, cosine, sine, kv2, kv1, kv0, w, pieces=8):
     rows, depth = x.shape
     width = w.shape[1]
     whole = pl.BlockSpec(memory_space=pltpu.VMEM)
     return pl.pallas_call(
         attend_kernel,
         in_specs=[pl.BlockSpec(memory_space=pltpu.SMEM)]
-        + [whole, pl.BlockSpec(memory_space=pl.ANY)]
-        + [whole] * 5
-        + [pl.BlockSpec(memory_space=pl.ANY)],
+        + [whole]
+        + [pl.BlockSpec(memory_space=pl.ANY)] * 7,
         out_specs=whole,
         out_shape=jax.ShapeDtypeStruct((rows, width), jnp.bfloat16),
         scratch_shapes=[
             pltpu.VMEM((rows, depth), jnp.bfloat16),
             pltpu.VMEM((depth, width), jnp.bfloat16),
-            pltpu.VMEM((rows, width), jnp.bfloat16),
+            pltpu.VMEM((rows, HEAD_SIZE), jnp.float32),
+            pltpu.VMEM((rows, HEAD_SIZE), jnp.float32),
+            pltpu.VMEM((width // HEAD_SIZE, HEAD_SIZE, rows), jnp.bfloat16),
+            pltpu.VMEM((3 * rows, HEAD_SIZE), jnp.bfloat16),
             pltpu.VMEM((3 * rows, HEAD_SIZE), jnp.bfloat16),
             pltpu.VMEM((HEAD_SIZE, 3 * rows), jnp.bfloat16),
             pltpu.VMEM((rows, width), jnp.float32),
             pltpu.VMEM((HEAD_SIZE, width), jnp.float32),
-            pltpu.SemaphoreType.DMA((2, pieces)),
+            pltpu.SemaphoreType.DMA((2 * pieces + 8,)),
         ],
         compiler_params=pltpu.CompilerParams(vmem_limit_bytes=60 * 1024 * 1024),
         cost_estimate=pl.CostEstimate(

time: 110 us -> 110 us (level)
  the two profiles are of different devices: /device:TPU:11 before, /device:TPU:61 now
where the time goes in v5:
time: 110 us
  blocking collectives  28.7 us (26%)
  waiting for transfers between devices  18.4 us (17%)
  Pallas kernels  17.4 us (16%)
  starting transfers between devices  16.9 us (15%)
  between operations  13.6 us (12%)
  other arithmetic  10.8 us (10%)
  local copies, waits for them, and re-layouts  3.83 us (3%)
    all_gather x1, blocking collectives, gather_key_value(): lax.all_gather(own, 'rows', axis=0, tiled=True, axis_index_groups=same_core)  28.7 us
    pallas_call x1, Pallas kernels, attend(): pl.pallas_call(attend_kernel, in_specs=[pl.BlockSpec(memory_space=pltpu.S...  14.8 us
    ppermute x1, starting transfers between devices, gather_key_value(): lax.ppermute(half, 'rows', [(i, i ^ 1) for i in range(devices)])  10.3 us
    all_gather x1, waiting for transfers between devices, on_device(): query_weights = lax.all_gather(w_query, 'rows', axis=0, tiled=True)  8.17 us
    ppermute x1, waiting for transfers between devices, on_device(): kv2 = lax.ppermute(kv, 'attn', [(0, 2), (1, 3)])  7.99 us
    all_to_all x1, starting transfers between devices, gather_key_value(): half = lax.all_to_all(spread, 'attn', 0, 0, tiled=True)  3.94 us
    convert_element_type x1, other arithmetic, normalize(): (widened * lax.rsqrt(mean_sq + 1e-05) * norm_gain.astype(jnp.float32)).as...  3.87 us
    reduce_sum x1, other arithmetic, normalize(): mean_sq = jnp.mean(widened * widened, axis=-1, keepdims=True)  3.15 us
  transfers between devices with their start and end apart: 5, of which 3 were waited for; matrix products, arithmetic and copies ran while one was open for 12% of the time, Pallas kernels for 2%

profile of v5, /device:TPU:61, one launch (start us, length us, event | category | flops | bytes accessed | tf_op | source)
XLA Modules:
  0.0 109.6 jit_solution(14338830155370709821)
XLA Ops:
  6.5 0.0 copy-start.4
  6.5 0.0 all-gather.2.cloned.1.call-start
  6.5 0.7 all-gather.2.cloned.1.call-update
  7.3 0.7 fusion.4
  8.0 28.7 %all_gather.6 = bf16[512,256]{1,0:T(8,128)(2,1)S(1)} all-gather(bf16[32,256]{1,0:T(8,128)(2,1)S(1)} %fusion.4), channel_id=1, replica_groups={{0,32,64,96,128,160,192,224,256,288,320,352,384,416,448,480},{16,48,80,..., dimensions={0}, use_global_device_ids=true | all-gather | bytes 278528 | tf_op jit(solution)/shard_map/all_gather | solution.py:224
  36.7 1.0 broadcast_in_dim.2
  37.7 3.9 %all-to-all-start = ((bf16[4,512,256]{2,1,0:T(8,128)(2,1)}), bf16[4,512,256]{2,1,0:T(8,128)(2,1)S(1)}, u32[]{:S(2)}, u32[]{:S(2)}) async-start(bf16[4,512,256]{2,1,0:T(8,128)(2,1)} %broadcast_in_dim.2), calls=%async_computation | async-start | bytes 2097152 | tf_op jit(solution)/shard_map/all_to_all | solution.py:226
  41.7 0.7 convert_element_type.21
  42.4 0.7 constant_dynamic-slice_fusion
  43.1 1.0 fusion.3
  44.1 0.2 pad_maximum_fusion
  44.3 0.0 copy-start.1
  44.3 0.0 copy-start.2
  44.3 0.0 copy-done.4
  44.3 0.6 convert_reduce_fusion
  44.9 3.1 %fusion = f32[512]{0:T(512)S(1)} fusion(bf16[512,4096]{1,0:T(8,128)(2,1)} %param.6), kind=kLoop, calls=%fused_computation.2 | loop fusion | flops 6290944 | bytes 4196352 | tf_op jit(solution)/shard_map/reduce_sum | solution.py:209
  48.1 0.0 copy-start.5
  48.1 1.5 %all-to-all-done = bf16[4,512,256]{2,1,0:T(8,128)(2,1)S(1)} async-done(((bf16[4,512,256]{2,1,0:T(8,128)(2,1)}), bf16[4,512,256]{2,1,0:T(8,128)(2,1)S(1)}, u32[]{:S(2)}, u32[]{:S(2)}) %all-to-all-start) | async-done | bytes 1048608 | tf_op jit(solution)/shard_map/all_to_all | solution.py:226
  49.6 10.3 %collective-permute-start = (bf16[4,16,32,256]{3,2,1,0:T(8,128)(2,1)S(1)}, bf16[4,16,32,256]{3,2,1,0:T(8,128)(2,1)S(1)}, u32[]{:S(2)}, u32[]{:S(2)}) collective-permute-start(bf16[4,16,32,256]{3,2,1,0:T(8,128)(2,1)S(1)} %bitcast.6), channel_id=1, source_target_pairs={{0,16},{16,0},{32,48},{48,32},{64,80},{80,64},{96,112},{112,96},{1... | collective-permute-start | bytes 3145736 | tf_op jit(solution)/shard_map/ppermute | solution.py:228
  60.0 3.9 %fusion.2.x_ref = bf16[512,4096]{1,0:T(8,128)(2,1)S(1)} fusion(bf16[512,4096]{1,0:T(8,128)(2,1)} %param.6, f32[4096]{0:T(1024)S(1)} %convert_element_type.21, f32[512]{0:T(512)S(1)} %add_rsqrt_fusion), kind=kLoop, calls=%fused_computation.4 | loop fusion | flops 8388608 | bytes 8407040 | tf_op jit(solution)/shard_map/convert_element_type | solution.py:210
  63.8 0.0 collective-permute-done.wb_ref
  63.8 0.0 copy-done.1
  63.8 0.0 copy-done.2
  63.9 2.6 %shard_map.64.kv0_ref = bf16[512,256]{1,0:T(8,128)(2,1)S(1)} custom-call(s32[1]{0:T(128)} %bitcast.3.core_ref, bf16[512,4096]{1,0:T(8,128)(2,1)S(1)} %fusion.2.x_ref, bf16[4,16,32,256]{3,2,1,0:T(8,128)(2,1)S(1)} %bitcast.7, bf16[4,16,32,256]{3,2,1,0:T(8,128)(2,1)S(1)} %collective-permute-done.wb_ref, f32[512,128]{1,0:T(8,128)S(1)} %get-tuple-element.8.cos_ref, ...), custom_call_target="tpu_custom_call" | custom-call | flops 1073741824 | bytes 6553600 | tf_op jit(solution)/shard_map/pallas_call | solution.py:60
  66.5 0.0 copy-start
  66.5 2.0 %copy-done = bf16[512,4096]{1,0:T(8,128)(2,1)} copy-done((bf16[512,4096]{1,0:T(8,128)(2,1)}, bf16[512,4096]{1,0:T(8,128)(2,1)S(1)}, u32[]{:S(2)}) %copy-start) | copy-done | bytes 4194328
  68.4 0.0 copy-start.3
  68.4 1.3 %collective-permute-start.1 = (bf16[512,256]{1,0:T(8,128)(2,1)S(1)}, bf16[512,256]{1,0:T(8,128)(2,1)S(1)}, u32[]{:S(2)}, u32[]{:S(2)}) collective-permute-start(bf16[512,256]{1,0:T(8,128)(2,1)S(1)} %shard_map.64.kv0_ref), channel_id=1, source_target_pairs={{0,2},{1,3},{4,6},{5,7},{8,10},{9,11},{12,14},{13,15},{16,18},{17,... | collective-permute-start | bytes 786440 | tf_op jit(solution)/shard_map/ppermute | solution.py:252
  69.7 1.3 %collective-permute-start.2 = (bf16[512,256]{1,0:T(8,128)(2,1)S(1)}, bf16[512,256]{1,0:T(8,128)(2,1)S(1)}, u32[]{:S(2)}, u32[]{:S(2)}) collective-permute-start(bf16[512,256]{1,0:T(8,128)(2,1)S(1)} %shard_map.64.kv0_ref), channel_id=1, source_target_pairs={{0,1},{1,2},{2,3},{4,5},{5,6},{6,7},{8,9},{9,10},{10,11},{12,13},{... | collective-permute-start | bytes 786440 | tf_op jit(solution)/shard_map/ppermute | solution.py:251
  71.0 0.0 copy-done.5
  71.0 0.1 slice_reduce_fusion
  71.2 0.6 and_select_fusion.first_ref
  71.8 8.0 %collective-permute-done.1.kv2_ref = bf16[512,256]{1,0:T(8,128)(2,1)S(1)} collective-permute-done((bf16[512,256]{1,0:T(8,128)(2,1)S(1)}, bf16[512,256]{1,0:T(8,128)(2,1)S(1)}, u32[]{:S(2)}, u32[]{:S(2)}) %collective-permute-start.1) | collective-permute-done | bytes 262176 | tf_op jit(solution)/shard_map/ppermute | solution.py:252
  79.8 0.0 copy-start.6
  79.8 0.0 collective-permute-done.2.kv1_ref
  79.8 0.0 copy-start.7
  79.8 8.2 %all-gather.2.cloned.1.call-done.w_ref = bf16[4096,512]{1,0:T(8,128)(2,1)} async-done(((bf16[128,512]{1,0:T(8,128)(2,1)}), bf16[4096,512]{1,0:T(8,128)(2,1)}) %all-gather.2.cloned.1.call-update) | async-done | bytes 4194320 | tf_op jit(solution)/shard_map/all_gather | solution.py:236
  87.9 0.0 copy-done.3
  87.9 0.0 copy-done.6
  87.9 0.0 copy-done.7
  87.9 14.8 %shard_map.65 = bf16[512,512]{1,0:T(8,128)(2,1)} custom-call(s32[4]{0:T(128)} %and_select_fusion.first_ref, s32[4,128]{1,0:T(4,128)} %copy-done.5, bf16[512,4096]{1,0:T(8,128)(2,1)} %copy-done, f32[512,128]{1,0:T(8,128)} %copy-done.1, f32[512,128]{1,0:T(8,128)} %copy-done.2, bf16[512,256]{1,0:T(8,128)(2,1)} %copy-done.6, bf16[512,256]{1,0:T(8,128)(2,1)} %copy-done.7, ...), custom_call_target="tpu_custom_call" | custom-call | flops 3221225472 | bytes 8388608 | tf_op jit(solution)/shard_map/pallas_call | solution.py:178
  (4 shorter events, 0.0 us)
Async XLA Ops:
  6.5 37.8 %copy-start.4 = (s32[1,2048]{1,0:T(1,128)S(1)}, s32[1,2048]{1,0:T(1,128)}, u32[]{:S(2)}) copy-start(s32[1,2048]{1,0:T(1,128)} %param.11) | copy-start | bytes 24580
  6.5 81.4 %all-gather.2.cloned.1.call-start = ((), (), s32[]{:S(2)}) async-start(), calls=%async_computation.1 | async-start | bytes 4325376 | tf_op jit(solution)/shard_map/all_gather | solution.py:236
  37.7 11.9 %all-to-all-start = ((bf16[4,512,256]{2,1,0:T(8,128)(2,1)}), bf16[4,512,256]{2,1,0:T(8,128)(2,1)S(1)}, u32[]{:S(2)}, u32[]{:S(2)}) async-start(bf16[4,512,256]{2,1,0:T(8,128)(2,1)} %broadcast_in_dim.2), calls=%async_computation | async-start | bytes 2097152 | tf_op jit(solution)/shard_map/all_to_all | solution.py:226
  44.3 19.6 %copy-start.1 = (f32[512,128]{1,0:T(8,128)}, f32[512,128]{1,0:T(8,128)S(1)}, u32[]{:S(2)}) copy-start(f32[512,128]{1,0:T(8,128)S(1)} %get-tuple-element.8.cos_ref) | copy-start | bytes 786436
  44.3 19.6 %copy-start.2 = (f32[512,128]{1,0:T(8,128)}, f32[512,128]{1,0:T(8,128)S(1)}, u32[]{:S(2)}) copy-start(f32[512,128]{1,0:T(8,128)S(1)} %get-tuple-element.9.sin_ref) | copy-start | bytes 786436
  48.1 23.0 %copy-start.5 = (s32[4,128]{1,0:T(4,128)}, s32[4,128]{1,0:T(4,128)S(1)}, u32[]{:S(2)}) copy-start(s32[4,128]{1,0:T(4,128)S(1)} %maximum_bitcast_fusion.low_ref) | copy-start | bytes 6148
  49.6 14.2 %collective-permute-start = (bf16[4,16,32,256]{3,2,1,0:T(8,128)(2,1)S(1)}, bf16[4,16,32,256]{3,2,1,0:T(8,128)(2,1)S(1)}, u32[]{:S(2)}, u32[]{:S(2)}) collective-permute-start(bf16[4,16,32,256]{3,2,1,0:T(8,128)(2,1)S(1)} %bitcast.6), channel_id=1, source_target_pairs={{0,16},{16,0},{32,48},{48,32},{64,80},{80,64},{96,112},{112,96},{1... | collective-permute-start | bytes 3145736 | tf_op jit(solution)/shard_map/ppermute | solution.py:228
  66.5 2.0 %copy-start = (bf16[512,4096]{1,0:T(8,128)(2,1)}, bf16[512,4096]{1,0:T(8,128)(2,1)S(1)}, u32[]{:S(2)}) copy-start(bf16[512,4096]{1,0:T(8,128)(2,1)S(1)} %fusion.2.x_ref) | copy-start | bytes 12582916
  68.4 19.5 %copy-start.3 = (bf16[512,256]{1,0:T(8,128)(2,1)}, bf16[512,256]{1,0:T(8,128)(2,1)S(1)}, u32[]{:S(2)}) copy-start(bf16[512,256]{1,0:T(8,128)(2,1)S(1)} %shard_map.64.kv0_ref) | copy-start | bytes 786436
  68.4 11.3 %collective-permute-start.1 = (bf16[512,256]{1,0:T(8,128)(2,1)S(1)}, bf16[512,256]{1,0:T(8,128)(2,1)S(1)}, u32[]{:S(2)}, u32[]{:S(2)}) collective-permute-start(bf16[512,256]{1,0:T(8,128)(2,1)S(1)} %shard_map.64.kv0_ref), channel_id=1, source_target_pairs={{0,2},{1,3},{4,6},{5,7},{8,10},{9,11},{12,14},{13,15},{16,18},{17,... | collective-permute-start | bytes 786440 | tf_op jit(solution)/shard_map/ppermute | solution.py:252
  69.7 10.0 %collective-permute-start.2 = (bf16[512,256]{1,0:T(8,128)(2,1)S(1)}, bf16[512,256]{1,0:T(8,128)(2,1)S(1)}, u32[]{:S(2)}, u32[]{:S(2)}) collective-permute-start(bf16[512,256]{1,0:T(8,128)(2,1)S(1)} %shard_map.64.kv0_ref), channel_id=1, source_target_pairs={{0,1},{1,2},{2,3},{4,5},{5,6},{6,7},{8,9},{9,10},{10,11},{12,13},{... | collective-permute-start | bytes 786440 | tf_op jit(solution)/shard_map/ppermute | solution.py:251
  79.8 8.2 %copy-start.6 = (bf16[512,256]{1,0:T(8,128)(2,1)}, bf16[512,256]{1,0:T(8,128)(2,1)S(1)}, u32[]{:S(2)}) copy-start(bf16[512,256]{1,0:T(8,128)(2,1)S(1)} %collective-permute-done.1.kv2_ref) | copy-start | bytes 786436
  79.8 8.2 %copy-start.7 = (bf16[512,256]{1,0:T(8,128)(2,1)}, bf16[512,256]{1,0:T(8,128)(2,1)S(1)}, u32[]{:S(2)}) copy-start(bf16[512,256]{1,0:T(8,128)(2,1)S(1)} %collective-permute-done.2.kv1_ref) | copy-start | bytes 786436
Sparse Core Ops, SparseCore 0:
  9.5 78.4 all-gather.1

commit v6 on v5

--- a/solution.py
+++ b/solution.py
@@ -81,13 +81,15 @@
 
 
 def attend_kernel(
-    first_ref, low_ref, x_ref, cos_ref, sin_ref, kv2_ref, kv1_ref, kv0_ref, w_ref,
+    core_ref, first_ref, low_ref, x_ref, cos_ref, sin_ref, kv2_ref, kv1_ref, kv0_ref, wa_ref, wb_ref,
     out_ref, x, w, cos, sin, q, keys, plain, values, sums, acc, sems,
 ):
     rows, depth = x_ref.shape
     width = out_ref.shape[1]
     heads = width // HEAD_SIZE
-    pieces = (sems.shape[0] - 8) // 2
+    pieces = 4
+    quarters, chips = wa_ref.shape[:2]
+    count = chips // pieces
     piece = depth // pieces
     copies = []
 
@@ -95,34 +97,41 @@
         copies.append(pltpu.make_async_copy(src, dst, sems.at[len(copies)]))
         copies[-1].start()
 
+    ready = []
     for n in range(pieces):
+        begin = len(copies)
+        some = pl.ds(n * count, count)
+        for k in range(quarters):
+            bring(wa_ref.at[k, some], w.at[some, core_ref[0], k])
+            bring(wb_ref.at[k, some], w.at[some, 1 - core_ref[0], k])
         take = pl.ds(n * piece, piece)
-        bring(w_ref.at[take], w.at[take])
         bring(x_ref.at[:, take], x.at[:, take])
+        ready.append(copies[begin:])
         if n == 0:
+            begin = len(copies)
             for at, ref in enumerate((kv2_ref, kv1_ref, kv0_ref)):
                 part = pl.ds(at * rows, rows)
                 bring(ref.at[:, :HEAD_SIZE], keys.at[part])
                 bring(ref.at[:, HEAD_SIZE:], plain.at[part])
             bring(cos_ref, cos)
             bring(sin_ref, sin)
-    others = copies[2:10]
-    copies = copies[:2] + copies[10:]
+            others = copies[begin:]
 
     for n in range(pieces):
-        copies[2 * n].wait()
-        copies[2 * n + 1].wait()
-        take = slice(n * piece, (n + 1) * piece)
-        part = jnp.dot(x[:, take], w[take], preferred_element_type=jnp.float32)
+        for copy in ready[n]:
+            copy.wait()
+        weights = w[n * count : (n + 1) * count].reshape(piece, width)
+        part = jnp.dot(
+            x[:, n * piece : (n + 1) * piece], weights, preferred_element_type=jnp.float32
+        )
         if n == 0:
             sums[...] = part
-        else:
-            sums[...] += part
-        if n == 0:
             for copy in others:
                 copy.wait()
             for at in range(0, 3 * rows, rows):
                 values[:, at : at + rows] = plain[at : at + rows].T
+        else:
+            sums[...] += part
     for h in range(heads):
         lanes = slice(h * HEAD_SIZE, (h + 1) * HEAD_SIZE)
         q[h] = rotate(sums[:, lanes], cos[...], sin[...]).T.astype(jnp.bfloat16)
@@ -171,20 +180,20 @@
             out_ref[block, lanes] = mixed[:, lanes].T.astype(jnp.bfloat16)
 
 
-def attend(first, low, x, cosine, sine, kv2, kv1, kv0, w, pieces=8):
+def attend(core, first, low, x, cosine, sine, kv2, kv1, kv0, wa, wb):
     rows, depth = x.shape
-    width = w.shape[1]
+    quarters, chips, part, width = wa.shape
     whole = pl.BlockSpec(memory_space=pltpu.VMEM)
     return pl.pallas_call(
         attend_kernel,
-        in_specs=[pl.BlockSpec(memory_space=pltpu.SMEM)]
+        in_specs=[pl.BlockSpec(memory_space=pltpu.SMEM)] * 2
         + [whole]
-        + [pl.BlockSpec(memory_space=pl.ANY)] * 7,
+        + [pl.BlockSpec(memory_space=pl.ANY)] * 8,
         out_specs=whole,
         out_shape=jax.ShapeDtypeStruct((rows, width), jnp.bfloat16),
         scratch_shapes=[
             pltpu.VMEM((rows, depth), jnp.bfloat16),
-            pltpu.VMEM((depth, width), jnp.bfloat16),
+            pltpu.VMEM((chips, 2, quarters, part, width), jnp.bfloat16),
             pltpu.VMEM((rows, HEAD_SIZE), jnp.float32),
             pltpu.VMEM((rows, HEAD_SIZE), jnp.float32),
             pltpu.VMEM((width // HEAD_SIZE, HEAD_SIZE, rows), jnp.bfloat16),
@@ -193,7 +202,7 @@
             pltpu.VMEM((HEAD_SIZE, 3 * rows), jnp.bfloat16),
             pltpu.VMEM((rows, width), jnp.float32),
             pltpu.VMEM((HEAD_SIZE, width), jnp.float32),
-            pltpu.SemaphoreType.DMA((2 * pieces + 8,)),
+            pltpu.SemaphoreType.DMA((4 * (2 * quarters + 1) + 8,)),
         ],
         compiler_params=pltpu.CompilerParams(vmem_limit_bytes=60 * 1024 * 1024),
         cost_estimate=pl.CostEstimate(
@@ -201,7 +210,7 @@
             bytes_accessed=2 * (rows * depth + depth * width),
             transcendentals=0,
         ),
-    )(first, low, x, cosine, sine, kv2, kv1, kv0, w)
+    )(core, first, low, x, cosine, sine, kv2, kv1, kv0, wa, wb)
 
 
 def normalize(tokens, norm_gain):
@@ -212,20 +221,53 @@
     )
 
 
-def gather_key_value(mine):
-    me = lax.axis_index("attn")
+def gather_column(mine):
+    quarter = mine.shape[0] // lax.axis_size("attn")
+    own = lax.dynamic_slice_in_dim(mine, lax.axis_index("attn") * quarter, quarter, 0)
+    chips = lax.axis_size("rows") // 2
+    same_core = [[2 * z + c for z in range(chips)] for c in range(2)]
+    return lax.all_gather(own, "rows", axis=0, tiled=False, axis_index_groups=same_core)
+
+
+def nothing_kernel(*refs):
+    del refs
+
+
+def after(x, *others):
+    anywhere = pl.BlockSpec(memory_space=pl.ANY)
+    return pl.pallas_call(
+        nothing_kernel,
+        in_specs=[anywhere] * (1 + len(others)),
+        out_specs=anywhere,
+        out_shape=jax.ShapeDtypeStruct(x.shape, x.dtype),
+        input_output_aliases={0: 0},
+        compiler_params=pltpu.CompilerParams(vmem_limit_bytes=1024 * 1024),
+        cost_estimate=pl.CostEstimate(flops=0, bytes_accessed=0, transcendentals=0),
+    )(x, *others)
+
+
+def columns_kernel(first, x_ref, out_ref):
+    for n in range(out_ref.shape[0]):
+        out_ref[n] = x_ref[..., first : first + out_ref.shape[-1]]
+
+
+def spread_attn(x, first, width):
     parts = lax.axis_size("attn")
-    devices = lax.axis_size("rows")
-    rows, width = mine.shape
-    quarter = rows // parts
-    own = lax.dynamic_slice_in_dim(mine, me * quarter, quarter, 0)
-    chips = devices // 2
-    same_core = [[2 * z + c for z in range(chips)] for c in range(2)]
-    column = lax.all_gather(own, "rows", axis=0, tiled=True, axis_index_groups=same_core)
-    spread = jnp.broadcast_to(column[None], (parts, chips * quarter, width))
-    half = lax.all_to_all(spread, "attn", 0, 0, tiled=True)
-    half = half.reshape(parts, chips, quarter, width)
-    return half, lax.ppermute(half, "rows", [(i, i ^ 1) for i in range(devices)])
+    whole = pl.BlockSpec(memory_space=pltpu.VMEM)
+    out = jax.ShapeDtypeStruct((parts, *x.shape[:-1], width), x.dtype)
+    spread = pl.pallas_call(
+        functools.partial(columns_kernel, first),
+        in_specs=[whole],
+        out_specs=whole,
+        out_shape=out,
+        compiler_params=pltpu.CompilerParams(vmem_limit_bytes=8 * 1024 * 1024),
+        cost_estimate=pl.CostEstimate(flops=0, bytes_accessed=3 * out.size, transcendentals=0),
+    )(x)
+    return lax.all_to_all(spread, "attn", 0, 0, tiled=True)
+
+
+def swap_cores(half):
+    return lax.ppermute(half, "rows", [(i, i ^ 1) for i in range(lax.axis_size("rows"))])
 
 
 def on_device(
@@ -233,12 +275,13 @@
 ):
     rows = tokens.shape[0]
     me = lax.axis_index("attn")
-    query_weights = lax.all_gather(w_query, "rows", axis=0, tiled=True)
-    kv_weights = gather_key_value(
-        jnp.concatenate([key_projection_weight, value_projection_weight], 1)
-    )
-
+    split = 2 * HEAD_SIZE
+    column = gather_column(
+        jnp.concatenate([key_projection_weight, value_projection_weight, w_query], 1)
+    )
     normed = normalize(tokens, norm_gain)
+    kv_half = spread_attn(column, 0, split)
+    query_half = spread_attn(after(column, normed[:16, :HEAD_SIZE], kv_half), split, w_query.shape[1])
     cosine, sine = rotary_tables(me * rows + jnp.arange(rows, dtype=jnp.int32))
     doc_ids = documents[0]
     my_docs = lax.dynamic_slice_in_dim(doc_ids, me * rows, rows)
@@ -247,10 +290,12 @@
     first = low[:, 0] // KEY_BLOCK
 
     core = (lax.axis_index("rows") % 2).astype(jnp.int32).reshape(1)
-    kv = project_kv(core, normed, *kv_weights, cosine, sine)
+    kv = project_kv(core, normed, kv_half, swap_cores(kv_half), cosine, sine)
     kv1 = lax.ppermute(kv, "attn", [(0, 1), (1, 2), (2, 3)])
     kv2 = lax.ppermute(kv, "attn", [(0, 2), (1, 3)])
-    return attend(first, low, normed, cosine, sine, kv2, kv1, kv, query_weights)
+    query_half = after(query_half, kv1, kv2)
+    other = swap_cores(query_half)
+    return attend(core, first, low, normed, cosine, sine, kv2, kv1, kv, query_half, other)
 
 
 def solution(mesh):

time: 110 us -> 110 us (level)
  the two profiles are of different devices: /device:TPU:61 before, /device:TPU:51 now
where the time goes in v6:
time: 110 us
  blocking collectives  30.8 us (28%)
  starting transfers between devices  30.2 us (27%)
  Pallas kernels  19 us (17%)
  waiting for transfers between devices  15.7 us (14%)
  other arithmetic  8 us (7%)
  local copies, waits for them, and re-layouts  5.8 us (5%)
    all_gather x1, blocking collectives, gather_column(): lax.all_gather(own, 'rows', axis=0, tiled=False, axis_index_groups=same_c...  30.8 us
    pallas_call x1, Pallas kernels, attend(): pl.pallas_call(attend_kernel, in_specs=[pl.BlockSpec(memory_space=pltpu.S...  15.3 us
    ppermute x2, starting transfers between devices, swap_cores(): lax.ppermute(half, 'rows', [(i, i ^ 1) for i in range(lax.axis_size('rows...  14.8 us
    all_to_all x2, starting transfers between devices, spread_attn(): return lax.all_to_all(spread, 'attn', 0, 0, tiled=True)  11.3 us
    ppermute x1, waiting for transfers between devices, on_device(): kv1 = lax.ppermute(kv, 'attn', [(0, 1), (1, 2), (2, 3)])  8.57 us
    unnamed x24, local copies, waits for them, and re-layouts  5.67 us
    ppermute x2, waiting for transfers between devices, swap_cores(): lax.ppermute(half, 'rows', [(i, i ^ 1) for i in range(lax.axis_size('rows...  3.85 us
    ppermute x1, waiting for transfers between devices, on_device(): kv2 = lax.ppermute(kv, 'attn', [(0, 2), (1, 3)])  3.28 us
  transfers between devices with their start and end apart: 6, of which 4 were waited for; matrix products, arithmetic and copies ran while one was open for 7% of the time, Pallas kernels for 2%

profile of v6, /device:TPU:51, one launch (start us, length us, event | category | flops | bytes accessed | tf_op | source)
XLA Modules:
  0.0 109.8 jit_solution(7931903712534082117)
XLA Ops:
  0.0 0.8 fusion.5
  0.8 30.8 %all-gather = bf16[512,768]{1,0:T(8,128)(2,1)S(1)} all-gather(bf16[32,768]{1,0:T(8,128)(2,1)S(1)} %fusion.5), channel_id=2, replica_groups={{0,32,64,96,128,160,192,224,256,288,320,352,384,416,448,480},{16,48,80,..., dimensions={0}, use_global_device_ids=true | all-gather | bytes 835584 | tf_op jit(solution)/shard_map/all_gather | solution.py:229
  31.6 0.0 copy-start.10
  31.6 1.0 shard_map.64
  32.7 4.2 %all-to-all-start = ((bf16[4,16,32,256]{3,2,1,0:T(8,128)(2,1)}), bf16[4,16,32,256]{3,2,1,0:T(8,128)(2,1)S(1)}, u32[]{:S(2)}, u32[]{:S(2)}) async-start(bf16[4,16,32,256]{3,2,1,0:T(8,128)(2,1)} %shard_map.64), calls=%async_computation | async-start | bytes 2097152 | tf_op jit(solution)/shard_map/all_to_all | solution.py:266
  36.9 0.0 copy-start.8
  36.9 3.2 %fusion = f32[512]{0:T(512)S(1)} fusion(bf16[512,4096]{1,0:T(8,128)(2,1)} %param.6), kind=kLoop, calls=%fused_computation.2 | loop fusion | flops 6290944 | bytes 4196352 | tf_op jit(solution)/shard_map/reduce_sum | solution.py:218
  40.2 0.0 copy-done.10
  40.2 0.2 copy-done.8
  40.4 1.7 %fusion.2.x_ref = bf16[512,4096]{1,0:T(8,128)(2,1)S(1)} fusion(bf16[512,4096]{1,0:T(8,128)(2,1)S(1)} %copy-done.8, f32[4096]{0:T(1024)S(1)} %convert_element_type.21, f32[512]{0:T(512)S(1)} %add_rsqrt_fusion), kind=kLoop, calls=%fused_computation.4 | loop fusion | flops 8388608 | bytes 8407040 | tf_op jit(solution)/shard_map/convert_element_type | solution.py:219
  42.0 0.0 copy-start
  42.0 1.9 %copy-done = bf16[512,4096]{1,0:T(8,128)(2,1)} copy-done((bf16[512,4096]{1,0:T(8,128)(2,1)}, bf16[512,4096]{1,0:T(8,128)(2,1)S(1)}, u32[]{:S(2)}) %copy-start) | copy-done | bytes 4194328
  44.0 0.0 all-to-all-done.wa_ref.refs_2_
  44.0 0.1 shard_map.67
  44.1 0.0 copy-start.2
  44.1 1.3 %copy-done.2 = bf16[4,16,32,512]{3,2,1,0:T(8,128)(2,1)} copy-done((bf16[4,16,32,512]{3,2,1,0:T(8,128)(2,1)}, bf16[4,16,32,512]{3,2,1,0:T(8,128)(2,1)S(1)}, u32[]{:S(2)}) %copy-start.2) | copy-done | bytes 2097176
  45.5 7.1 %all-to-all-start.1 = ((bf16[4,16,32,512]{3,2,1,0:T(8,128)(2,1)}), bf16[4,16,32,512]{3,2,1,0:T(8,128)(2,1)}, u32[]{:S(2)}, u32[]{:S(2)}) async-start(bf16[4,16,32,512]{3,2,1,0:T(8,128)(2,1)} %copy-done.2), calls=%async_computation.1 | async-start | bytes 4194304 | tf_op jit(solution)/shard_map/all_to_all | solution.py:266
  52.5 11.1 %collective-permute-start = (bf16[4,16,32,256]{3,2,1,0:T(8,128)(2,1)S(1)}, bf16[4,16,32,256]{3,2,1,0:T(8,128)(2,1)S(1)}, u32[]{:S(2)}, u32[]{:S(2)}) collective-permute-start(bf16[4,16,32,256]{3,2,1,0:T(8,128)(2,1)S(1)} %all-to-all-done.wa_ref.refs_2_), channel_id=1, source_target_pairs={{0,16},{16,0},{32,48},{48,32},{64,80},{80,64},{96,112},{112,96},{1... | collective-permute-start | bytes 3145736 | tf_op jit(solution)/shard_map/ppermute | solution.py:270
  63.7 1.0 fusion.3
  64.7 0.2 pad_maximum_fusion
  64.9 0.0 copy-start.3
  64.9 0.0 copy-start.4
  64.9 1.0 collective-permute-done.wb_ref
  65.9 0.0 copy-start.1
  65.9 2.2 %copy-done.1 = bf16[512,4096]{1,0:T(8,128)(2,1)S(1)} copy-done((bf16[512,4096]{1,0:T(8,128)(2,1)S(1)}, bf16[512,4096]{1,0:T(8,128)(2,1)}, u32[]{:S(2)}) %copy-start.1) | copy-done | bytes 4194328
  68.1 0.0 copy-start.9
  68.1 2.6 %shard_map.65.kv0_ref = bf16[512,256]{1,0:T(8,128)(2,1)S(1)} custom-call(s32[1]{0:T(128)} %bitcast.core_ref, bf16[512,4096]{1,0:T(8,128)(2,1)S(1)} %copy-done.1, bf16[4,16,32,256]{3,2,1,0:T(8,128)(2,1)S(1)} %all-to-all-done.wa_ref.refs_2_, bf16[4,16,32,256]{3,2,1,0:T(8,128)(2,1)S(1)} %collective-permute-done.wb_ref, ...), custom_call_target="tpu_custom_call" | custom-call | flops 1073741824 | bytes 6553600 | tf_op jit(solution)/shard_map/pallas_call | solution.py:60
  70.7 0.0 copy-start.5
  70.7 2.8 %collective-permute-start.2 = (bf16[512,256]{1,0:T(8,128)(2,1)S(1)}, bf16[512,256]{1,0:T(8,128)(2,1)S(1)}, u32[]{:S(2)}, u32[]{:S(2)}) collective-permute-start(bf16[512,256]{1,0:T(8,128)(2,1)S(1)} %shard_map.65.kv0_ref), channel_id=1, source_target_pairs={{0,1},{1,2},{2,3},{4,5},{5,6},{6,7},{8,9},{9,10},{10,11},{12,13},{... | collective-permute-start | bytes 786440 | tf_op jit(solution)/shard_map/ppermute | solution.py:294
  73.5 1.3 %collective-permute-start.1 = (bf16[512,256]{1,0:T(8,128)(2,1)S(1)}, bf16[512,256]{1,0:T(8,128)(2,1)S(1)}, u32[]{:S(2)}, u32[]{:S(2)}) collective-permute-start(bf16[512,256]{1,0:T(8,128)(2,1)S(1)} %shard_map.65.kv0_ref), channel_id=1, source_target_pairs={{0,2},{1,3},{4,6},{5,7},{8,10},{9,11},{12,14},{13,15},{16,18},{17,... | collective-permute-start | bytes 786440 | tf_op jit(solution)/shard_map/ppermute | solution.py:295
  74.8 8.6 %collective-permute-done.2.refs_1_.kv1_ref = bf16[512,256]{1,0:T(8,128)(2,1)S(1)} collective-permute-done((bf16[512,256]{1,0:T(8,128)(2,1)S(1)}, bf16[512,256]{1,0:T(8,128)(2,1)S(1)}, u32[]{:S(2)}, u32[]{:S(2)}) %collective-permute-start.2) | collective-permute-done | bytes 262176 | tf_op jit(solution)/shard_map/ppermute | solution.py:294
  83.4 0.0 copy-start.6
  83.4 3.3 %collective-permute-done.1.refs_2_.kv2_ref = bf16[512,256]{1,0:T(8,128)(2,1)S(1)} collective-permute-done((bf16[512,256]{1,0:T(8,128)(2,1)S(1)}, bf16[512,256]{1,0:T(8,128)(2,1)S(1)}, u32[]{:S(2)}, u32[]{:S(2)}) %collective-permute-start.1) | collective-permute-done | bytes 262176 | tf_op jit(solution)/shard_map/ppermute | solution.py:295
  86.7 0.0 copy-start.7
  86.7 0.0 all-to-all-done.1.refs_0_
  86.7 0.0 copy-done.3
  86.7 0.0 copy-done.4
  86.7 3.7 %collective-permute-start.3 = (bf16[4,16,32,512]{3,2,1,0:T(8,128)(2,1)}, bf16[4,16,32,512]{3,2,1,0:T(8,128)(2,1)}, u32[]{:S(2)}, u32[]{:S(2)}) collective-permute-start(bf16[4,16,32,512]{3,2,1,0:T(8,128)(2,1)} %shard_map.68.wa_ref), channel_id=1, source_target_pairs={{0,16},{16,0},{32,48},{48,32},{64,80},{80,64},{96,112},{112,96},{1... | collective-permute-start | bytes 6291464 | tf_op jit(solution)/shard_map/ppermute | solution.py:270
  90.4 0.0 copy-done.9
  90.4 0.6 convert_reduce_fusion
  91.0 0.0 copy-start.11
  91.0 0.1 slice_reduce_fusion
  91.1 0.5 and_select_fusion.first_ref
  91.6 2.9 %collective-permute-done.3.wb_ref = bf16[4,16,32,512]{3,2,1,0:T(8,128)(2,1)} collective-permute-done((bf16[4,16,32,512]{3,2,1,0:T(8,128)(2,1)}, bf16[4,16,32,512]{3,2,1,0:T(8,128)(2,1)}, u32[]{:S(2)}, u32[]{:S(2)}) %collective-permute-start.3) | collective-permute-done | bytes 2097184 | tf_op jit(solution)/shard_map/ppermute | solution.py:270
  94.5 0.0 copy-done.5
  94.5 0.0 copy-done.6
  94.5 0.0 copy-done.7
  94.5 0.0 copy-done.11
  94.5 15.3 %shard_map.69 = bf16[512,512]{1,0:T(8,128)(2,1)} custom-call(s32[1]{0:T(128)} %bitcast.core_ref, s32[4]{0:T(128)} %and_select_fusion.first_ref, s32[4,128]{1,0:T(4,128)} %copy-done.11, bf16[512,4096]{1,0:T(8,128)(2,1)} %copy-done, f32[512,128]{1,0:T(8,128)} %copy-done.3, f32[512,128]{1,0:T(8,128)} %copy-done.4, bf16[512,256]{1,0:T(8,128)(2,1)} %copy-done.7, ...), custom_call_target="tpu_custom_call" | custom-call | flops 3221225472 | bytes 8388608 | tf_op jit(solution)/shard_map/pallas_call | solution.py:187
  (9 shorter events, 0.1 us)
Async XLA Ops:
  31.6 8.5 %copy-start.10 = (bf16[4096]{0:T(1024)(128)(2,1)S(1)}, bf16[4096]{0:T(1024)(128)(2,1)}, u32[]{:S(2)}) copy-start(bf16[4096]{0:T(1024)(128)(2,1)} %param.7) | copy-start | bytes 24580
  32.7 11.3 %all-to-all-start = ((bf16[4,16,32,256]{3,2,1,0:T(8,128)(2,1)}), bf16[4,16,32,256]{3,2,1,0:T(8,128)(2,1)S(1)}, u32[]{:S(2)}, u32[]{:S(2)}) async-start(bf16[4,16,32,256]{3,2,1,0:T(8,128)(2,1)} %shard_map.64), calls=%async_computation | async-start | bytes 2097152 | tf_op jit(solution)/shard_map/all_to_all | solution.py:266
  36.9 3.4 %copy-start.8 = (bf16[512,4096]{1,0:T(8,128)(2,1)S(1)}, bf16[512,4096]{1,0:T(8,128)(2,1)}, u32[]{:S(2)}) copy-start(bf16[512,4096]{1,0:T(8,128)(2,1)} %param.6) | copy-start | bytes 12582916
  42.0 1.9 %copy-start = (bf16[512,4096]{1,0:T(8,128)(2,1)}, bf16[512,4096]{1,0:T(8,128)(2,1)S(1)}, u32[]{:S(2)}) copy-start(bf16[512,4096]{1,0:T(8,128)(2,1)S(1)} %fusion.2.x_ref) | copy-start | bytes 12582916
  44.1 1.3 %copy-start.2 = (bf16[4,16,32,512]{3,2,1,0:T(8,128)(2,1)}, bf16[4,16,32,512]{3,2,1,0:T(8,128)(2,1)S(1)}, u32[]{:S(2)}) copy-start(bf16[4,16,32,512]{3,2,1,0:T(8,128)(2,1)S(1)} %shard_map.67) | copy-start | bytes 6291460
  45.5 41.2 %all-to-all-start.1 = ((bf16[4,16,32,512]{3,2,1,0:T(8,128)(2,1)}), bf16[4,16,32,512]{3,2,1,0:T(8,128)(2,1)}, u32[]{:S(2)}, u32[]{:S(2)}) async-start(bf16[4,16,32,512]{3,2,1,0:T(8,128)(2,1)} %copy-done.2), calls=%async_computation.1 | async-start | bytes 4194304 | tf_op jit(solution)/shard_map/all_to_all | solution.py:266
  52.5 13.4 %collective-permute-start = (bf16[4,16,32,256]{3,2,1,0:T(8,128)(2,1)S(1)}, bf16[4,16,32,256]{3,2,1,0:T(8,128)(2,1)S(1)}, u32[]{:S(2)}, u32[]{:S(2)}) collective-permute-start(bf16[4,16,32,256]{3,2,1,0:T(8,128)(2,1)S(1)} %all-to-all-done.wa_ref.refs_2_), channel_id=1, source_target_pairs={{0,16},{16,0},{32,48},{48,32},{64,80},{80,64},{96,112},{112,96},{1... | collective-permute-start | bytes 3145736 | tf_op jit(solution)/shard_map/ppermute | solution.py:270
  64.9 21.8 %copy-start.3 = (f32[512,128]{1,0:T(8,128)}, f32[512,128]{1,0:T(8,128)S(1)}, u32[]{:S(2)}) copy-start(f32[512,128]{1,0:T(8,128)S(1)} %get-tuple-element.8.cos_ref) | copy-start | bytes 786436
  64.9 21.8 %copy-start.4 = (f32[512,128]{1,0:T(8,128)}, f32[512,128]{1,0:T(8,128)S(1)}, u32[]{:S(2)}) copy-start(f32[512,128]{1,0:T(8,128)S(1)} %get-tuple-element.9.sin_ref) | copy-start | bytes 786436
  65.9 2.2 %copy-start.1 = (bf16[512,4096]{1,0:T(8,128)(2,1)S(1)}, bf16[512,4096]{1,0:T(8,128)(2,1)}, u32[]{:S(2)}) copy-start(bf16[512,4096]{1,0:T(8,128)(2,1)} %copy-done) | copy-start | bytes 12582916
  68.1 22.3 %copy-start.9 = (s32[1,2048]{1,0:T(1,128)S(1)}, s32[1,2048]{1,0:T(1,128)}, u32[]{:S(2)}) copy-start(s32[1,2048]{1,0:T(1,128)} %param.11) | copy-start | bytes 24580
  70.7 23.8 %copy-start.5 = (bf16[512,256]{1,0:T(8,128)(2,1)}, bf16[512,256]{1,0:T(8,128)(2,1)S(1)}, u32[]{:S(2)}) copy-start(bf16[512,256]{1,0:T(8,128)(2,1)S(1)} %shard_map.65.kv0_ref) | copy-start | bytes 786436
  70.7 12.7 %collective-permute-start.2 = (bf16[512,256]{1,0:T(8,128)(2,1)S(1)}, bf16[512,256]{1,0:T(8,128)(2,1)S(1)}, u32[]{:S(2)}, u32[]{:S(2)}) collective-permute-start(bf16[512,256]{1,0:T(8,128)(2,1)S(1)} %shard_map.65.kv0_ref), channel_id=1, source_target_pairs={{0,1},{1,2},{2,3},{4,5},{5,6},{6,7},{8,9},{9,10},{10,11},{12,13},{... | collective-permute-start | bytes 786440 | tf_op jit(solution)/shard_map/ppermute | solution.py:294
  73.5 13.1 %collective-permute-start.1 = (bf16[512,256]{1,0:T(8,128)(2,1)S(1)}, bf16[512,256]{1,0:T(8,128)(2,1)S(1)}, u32[]{:S(2)}, u32[]{:S(2)}) collective-permute-start(bf16[512,256]{1,0:T(8,128)(2,1)S(1)} %shard_map.65.kv0_ref), channel_id=1, source_target_pairs={{0,2},{1,3},{4,6},{5,7},{8,10},{9,11},{12,14},{13,15},{16,18},{17,... | collective-permute-start | bytes 786440 | tf_op jit(solution)/shard_map/ppermute | solution.py:295
  83.4 11.1 %copy-start.6 = (bf16[512,256]{1,0:T(8,128)(2,1)}, bf16[512,256]{1,0:T(8,128)(2,1)S(1)}, u32[]{:S(2)}) copy-start(bf16[512,256]{1,0:T(8,128)(2,1)S(1)} %collective-permute-done.2.refs_1_.kv1_ref) | copy-start | bytes 786436
  86.7 7.8 %copy-start.7 = (bf16[512,256]{1,0:T(8,128)(2,1)}, bf16[512,256]{1,0:T(8,128)(2,1)S(1)}, u32[]{:S(2)}) copy-start(bf16[512,256]{1,0:T(8,128)(2,1)S(1)} %collective-permute-done.1.refs_2_.kv2_ref) | copy-start | bytes 786436
  86.7 7.8 %collective-permute-start.3 = (bf16[4,16,32,512]{3,2,1,0:T(8,128)(2,1)}, bf16[4,16,32,512]{3,2,1,0:T(8,128)(2,1)}, u32[]{:S(2)}, u32[]{:S(2)}) collective-permute-start(bf16[4,16,32,512]{3,2,1,0:T(8,128)(2,1)} %shard_map.68.wa_ref), channel_id=1, source_target_pairs={{0,16},{16,0},{32,48},{48,32},{64,80},{80,64},{96,112},{112,96},{1... | collective-permute-start | bytes 6291464 | tf_op jit(solution)/shard_map/ppermute | solution.py:270
  91.0 3.5 %copy-start.11 = (s32[4,128]{1,0:T(4,128)}, s32[4,128]{1,0:T(4,128)S(1)}, u32[]{:S(2)}) copy-start(s32[4,128]{1,0:T(4,128)S(1)} %maximum_bitcast_fusion.low_ref) | copy-start | bytes 6148

commit v7 on v6

--- a/solution.py
+++ b/solution.py
@@ -260,7 +260,7 @@
         in_specs=[whole],
         out_specs=whole,
         out_shape=out,
-        compiler_params=pltpu.CompilerParams(vmem_limit_bytes=8 * 1024 * 1024),
+        compiler_params=pltpu.CompilerParams(vmem_limit_bytes=60 * 1024 * 1024),
         cost_estimate=pl.CostEstimate(flops=0, bytes_accessed=3 * out.size, transcendentals=0),
     )(x)
     return lax.all_to_all(spread, "attn", 0, 0, tiled=True)
@@ -292,8 +292,8 @@
     core = (lax.axis_index("rows") % 2).astype(jnp.int32).reshape(1)
     kv = project_kv(core, normed, kv_half, swap_cores(kv_half), cosine, sine)
     kv1 = lax.ppermute(kv, "attn", [(0, 1), (1, 2), (2, 3)])
-    kv2 = lax.ppermute(kv, "attn", [(0, 2), (1, 3)])
-    query_half = after(query_half, kv1, kv2)
+    kv2 = lax.ppermute(kv1, "attn", [(1, 2), (2, 3)])
+    query_half = after(query_half, kv1)
     other = swap_cores(query_half)
     return attend(core, first, low, normed, cosine, sine, kv2, kv1, kv, query_half, other)
 

time: 110 us -> 117 us (1.064)
  the two profiles are of different devices: /device:TPU:51 before, /device:TPU:26 now
where the time goes in v7:
time: 117 us
  blocking collectives  42.1 us (36%)
  waiting for transfers between devices  22.6 us (19%)
  Pallas kernels  20 us (17%)
  starting transfers between devices  17.6 us (15%)
  other arithmetic  8.04 us (7%)
  local copies, waits for them, and re-layouts  6.06 us (5%)
    all_gather x1, blocking collectives, gather_column(): lax.all_gather(own, 'rows', axis=0, tiled=False, axis_index_groups=same_c...  42.1 us
    pallas_call x1, Pallas kernels, attend(): pl.pallas_call(attend_kernel, in_specs=[pl.BlockSpec(memory_space=pltpu.S...  12.6 us
    all_to_all x2, starting transfers between devices, spread_attn(): return lax.all_to_all(spread, 'attn', 0, 0, tiled=True)  11.2 us
    ppermute x1, waiting for transfers between devices, on_device(): kv1 = lax.ppermute(kv, 'attn', [(0, 1), (1, 2), (2, 3)])  10.9 us
    ppermute x1, waiting for transfers between devices, on_device(): kv2 = lax.ppermute(kv1, 'attn', [(1, 2), (2, 3)])  8.66 us
    unnamed x26, local copies, waits for them, and re-layouts  5.93 us
    pallas_call x2, Pallas kernels, spread_attn(): pl.pallas_call(functools.partial(columns_kernel, first), in_specs=[whole]...  4.79 us
    ppermute x2, starting transfers between devices, swap_cores(): lax.ppermute(half, 'rows', [(i, i ^ 1) for i in range(lax.axis_size('rows...  3.83 us
  transfers between devices with their start and end apart: 6, of which 4 were waited for; matrix products, arithmetic and copies ran while one was open for 6% of the time, Pallas kernels for 2%

profile of v7, /device:TPU:26, one launch (start us, length us, event | category | flops | bytes accessed | tf_op | source)
XLA Modules:
  0.0 116.7 jit_solution(4662573002576416234)
XLA Ops:
  0.0 0.8 fusion.5
  0.8 42.1 %all-gather = bf16[512,768]{1,0:T(8,128)(2,1)} all-gather(bf16[32,768]{1,0:T(8,128)(2,1)S(1)} %fusion.5), channel_id=2, replica_groups={{0,32,64,96,128,160,192,224,256,288,320,352,384,416,448,480},{16,48,80,..., dimensions={0}, use_global_device_ids=true | all-gather | bytes 835584 | tf_op jit(solution)/shard_map/all_gather | solution.py:229
  42.9 0.0 copy-start.10
  42.9 2.2 %shard_map.64 = bf16[4,16,32,256]{3,2,1,0:T(8,128)(2,1)} custom-call(bf16[16,32,768]{2,1,0:T(8,128)(2,1)} %bitcast.6), custom_call_target="tpu_custom_call" | custom-call | bytes 1572864 | tf_op jit(solution)/shard_map/pallas_call | solution.py:258
  45.1 4.7 %all-to-all-start = ((bf16[4,16,32,256]{3,2,1,0:T(8,128)(2,1)}), bf16[4,16,32,256]{3,2,1,0:T(8,128)(2,1)S(1)}, u32[]{:S(2)}, u32[]{:S(2)}) async-start(bf16[4,16,32,256]{3,2,1,0:T(8,128)(2,1)} %shard_map.64), calls=%async_computation | async-start | bytes 2097152 | tf_op jit(solution)/shard_map/all_to_all | solution.py:266
  49.8 0.0 copy-start.8
  49.8 3.2 %fusion = f32[512]{0:T(512)S(1)} fusion(bf16[512,4096]{1,0:T(8,128)(2,1)} %param.6), kind=kLoop, calls=%fused_computation.2 | loop fusion | flops 6290944 | bytes 4196352 | tf_op jit(solution)/shard_map/reduce_sum | solution.py:218
  53.0 0.0 copy-done.10
  53.0 0.2 copy-done.8
  53.2 0.0 copy-start.2
  53.2 1.7 %fusion.2.x_ref = bf16[512,4096]{1,0:T(8,128)(2,1)S(1)} fusion(bf16[512,4096]{1,0:T(8,128)(2,1)S(1)} %copy-done.8, f32[4096]{0:T(1024)S(1)} %convert_element_type.21, f32[512]{0:T(512)S(1)} %add_rsqrt_fusion), kind=kLoop, calls=%fused_computation.4 | loop fusion | flops 8388608 | bytes 8407040 | tf_op jit(solution)/shard_map/convert_element_type | solution.py:219
  54.9 0.0 copy-start
  54.9 1.9 %copy-done = bf16[512,4096]{1,0:T(8,128)(2,1)} copy-done((bf16[512,4096]{1,0:T(8,128)(2,1)}, bf16[512,4096]{1,0:T(8,128)(2,1)S(1)}, u32[]{:S(2)}) %copy-start) | copy-done | bytes 4194328
  56.8 1.8 %all-to-all-done.wa_ref.refs_2_ = bf16[4,16,32,256]{3,2,1,0:T(8,128)(2,1)S(1)} async-done(((bf16[4,16,32,256]{3,2,1,0:T(8,128)(2,1)}), bf16[4,16,32,256]{3,2,1,0:T(8,128)(2,1)S(1)}, u32[]{:S(2)}, u32[]{:S(2)}) %all-to-all-start) | async-done | bytes 1048608 | tf_op jit(solution)/shard_map/all_to_all | solution.py:266
  58.6 0.0 copy-done.2
  58.6 0.0 copy-start.3
  58.6 0.9 copy-done.3
  59.5 2.6 %shard_map.67 = bf16[4,16,32,512]{3,2,1,0:T(8,128)(2,1)} custom-call(bf16[16,32,768]{2,1,0:T(8,128)(2,1)} %copy-done.3), custom_call_target="tpu_custom_call" | custom-call | bytes 3145728 | tf_op jit(solution)/shard_map/pallas_call | solution.py:258
  62.1 6.5 %all-to-all-start.1 = ((bf16[4,16,32,512]{3,2,1,0:T(8,128)(2,1)}), bf16[4,16,32,512]{3,2,1,0:T(8,128)(2,1)}, u32[]{:S(2)}, u32[]{:S(2)}) async-start(bf16[4,16,32,512]{3,2,1,0:T(8,128)(2,1)} %shard_map.67), calls=%async_computation.1 | async-start | bytes 4194304 | tf_op jit(solution)/shard_map/all_to_all | solution.py:266
  68.6 1.9 %collective-permute-start = (bf16[4,16,32,256]{3,2,1,0:T(8,128)(2,1)S(1)}, bf16[4,16,32,256]{3,2,1,0:T(8,128)(2,1)S(1)}, u32[]{:S(2)}, u32[]{:S(2)}) collective-permute-start(bf16[4,16,32,256]{3,2,1,0:T(8,128)(2,1)S(1)} %all-to-all-done.wa_ref.refs_2_), channel_id=1, source_target_pairs={{0,16},{16,0},{32,48},{48,32},{64,80},{80,64},{96,112},{112,96},{1... | collective-permute-start | bytes 3145736 | tf_op jit(solution)/shard_map/ppermute | solution.py:270
  70.5 1.0 fusion.3
  71.5 0.2 pad_maximum_fusion
  71.7 0.0 copy-start.4
  71.8 0.0 copy-start.5
  71.8 1.4 %collective-permute-done.wb_ref = bf16[4,16,32,256]{3,2,1,0:T(8,128)(2,1)S(1)} collective-permute-done((bf16[4,16,32,256]{3,2,1,0:T(8,128)(2,1)S(1)}, bf16[4,16,32,256]{3,2,1,0:T(8,128)(2,1)S(1)}, u32[]{:S(2)}, u32[]{:S(2)}) %collective-permute-start) | collective-permute-done | bytes 1048608 | tf_op jit(solution)/shard_map/ppermute | solution.py:270
  73.1 0.0 copy-start.1
  73.1 2.2 %copy-done.1 = bf16[512,4096]{1,0:T(8,128)(2,1)S(1)} copy-done((bf16[512,4096]{1,0:T(8,128)(2,1)S(1)}, bf16[512,4096]{1,0:T(8,128)(2,1)}, u32[]{:S(2)}) %copy-start.1) | copy-done | bytes 4194328
  75.3 0.0 copy-start.9
  75.3 2.6 %shard_map.65.kv0_ref = bf16[512,256]{1,0:T(8,128)(2,1)S(1)} custom-call(s32[1]{0:T(128)} %bitcast.core_ref, bf16[512,4096]{1,0:T(8,128)(2,1)S(1)} %copy-done.1, bf16[4,16,32,256]{3,2,1,0:T(8,128)(2,1)S(1)} %all-to-all-done.wa_ref.refs_2_, bf16[4,16,32,256]{3,2,1,0:T(8,128)(2,1)S(1)} %collective-permute-done.wb_ref, ...), custom_call_target="tpu_custom_call" | custom-call | flops 1073741824 | bytes 6553600 | tf_op jit(solution)/shard_map/pallas_call | solution.py:60
  77.9 0.0 copy-start.6
  77.9 1.3 %collective-permute-start.1 = (bf16[512,256]{1,0:T(8,128)(2,1)S(1)}, bf16[512,256]{1,0:T(8,128)(2,1)S(1)}, u32[]{:S(2)}, u32[]{:S(2)}) collective-permute-start(bf16[512,256]{1,0:T(8,128)(2,1)S(1)} %shard_map.65.kv0_ref), channel_id=1, source_target_pairs={{0,1},{1,2},{2,3},{4,5},{5,6},{6,7},{8,9},{9,10},{10,11},{12,13},{... | collective-permute-start | bytes 786440 | tf_op jit(solution)/shard_map/ppermute | solution.py:294
  79.2 10.9 %collective-permute-done.1.refs_1_.kv1_ref = bf16[512,256]{1,0:T(8,128)(2,1)S(1)} collective-permute-done((bf16[512,256]{1,0:T(8,128)(2,1)S(1)}, bf16[512,256]{1,0:T(8,128)(2,1)S(1)}, u32[]{:S(2)}, u32[]{:S(2)}) %collective-permute-start.1) | collective-permute-done | bytes 262176 | tf_op jit(solution)/shard_map/ppermute | solution.py:294
  90.1 0.0 copy-start.7
  90.1 0.0 all-to-all-done.1.refs_0_
  90.1 0.0 copy-done.4
  90.1 0.0 copy-done.5
  90.1 1.9 %collective-permute-start.3 = (bf16[4,16,32,512]{3,2,1,0:T(8,128)(2,1)}, bf16[4,16,32,512]{3,2,1,0:T(8,128)(2,1)}, u32[]{:S(2)}, u32[]{:S(2)}) collective-permute-start(bf16[4,16,32,512]{3,2,1,0:T(8,128)(2,1)} %shard_map.68.wa_ref), channel_id=1, source_target_pairs={{0,16},{16,0},{32,48},{48,32},{64,80},{80,64},{96,112},{112,96},{1... | collective-permute-start | bytes 6291464 | tf_op jit(solution)/shard_map/ppermute | solution.py:270
  92.1 0.0 copy-done.9
  92.1 0.6 convert_reduce_fusion
  92.7 0.0 copy-start.11
  92.7 1.3 %collective-permute-start.2 = (bf16[512,256]{1,0:T(8,128)(2,1)S(1)}, bf16[512,256]{1,0:T(8,128)(2,1)S(1)}, u32[]{:S(2)}, u32[]{:S(2)}) collective-permute-start(bf16[512,256]{1,0:T(8,128)(2,1)S(1)} %collective-permute-done.1.refs_1_.kv1_ref), channel_id=1, source_target_pairs={{1,2},{2,3},{5,6},{6,7},{9,10},{10,11},{13,14},{14,15},{17,18},{18... | collective-permute-start | bytes 786440 | tf_op jit(solution)/shard_map/ppermute | solution.py:295
  94.0 0.1 slice_reduce_fusion
  94.1 0.5 and_select_fusion.first_ref
  94.6 8.7 %collective-permute-done.2.kv2_ref = bf16[512,256]{1,0:T(8,128)(2,1)S(1)} collective-permute-done((bf16[512,256]{1,0:T(8,128)(2,1)S(1)}, bf16[512,256]{1,0:T(8,128)(2,1)S(1)}, u32[]{:S(2)}, u32[]{:S(2)}) %collective-permute-start.2) | collective-permute-done | bytes 262176 | tf_op jit(solution)/shard_map/ppermute | solution.py:295
  103.3 0.0 copy-start.12
  103.3 0.0 collective-permute-done.3.wb_ref
  103.3 0.0 copy-done.6
  103.3 0.0 copy-done.7
  103.3 0.0 copy-done.11
  103.3 0.7 copy-done.12
  104.0 12.6 %shard_map.69 = bf16[512,512]{1,0:T(8,128)(2,1)} custom-call(s32[1]{0:T(128)} %bitcast.core_ref, s32[4]{0:T(128)} %and_select_fusion.first_ref, s32[4,128]{1,0:T(4,128)} %copy-done.11, bf16[512,4096]{1,0:T(8,128)(2,1)} %copy-done, f32[512,128]{1,0:T(8,128)} %copy-done.4, f32[512,128]{1,0:T(8,128)} %copy-done.5, bf16[512,256]{1,0:T(8,128)(2,1)} %copy-done.12, ...), custom_call_target="tpu_custom_call" | custom-call | flops 3221225472 | bytes 8388608 | tf_op jit(solution)/shard_map/pallas_call | solution.py:187
  (9 shorter events, 0.1 us)
Async XLA Ops:
  42.9 10.1 %copy-start.10 = (bf16[4096]{0:T(1024)(128)(2,1)S(1)}, bf16[4096]{0:T(1024)(128)(2,1)}, u32[]{:S(2)}) copy-start(bf16[4096]{0:T(1024)(128)(2,1)} %param.7) | copy-start | bytes 24580
  45.1 13.5 %all-to-all-start = ((bf16[4,16,32,256]{3,2,1,0:T(8,128)(2,1)}), bf16[4,16,32,256]{3,2,1,0:T(8,128)(2,1)S(1)}, u32[]{:S(2)}, u32[]{:S(2)}) async-start(bf16[4,16,32,256]{3,2,1,0:T(8,128)(2,1)} %shard_map.64), calls=%async_computation | async-start | bytes 2097152 | tf_op jit(solution)/shard_map/all_to_all | solution.py:266
  49.8 3.4 %copy-start.8 = (bf16[512,4096]{1,0:T(8,128)(2,1)S(1)}, bf16[512,4096]{1,0:T(8,128)(2,1)}, u32[]{:S(2)}) copy-start(bf16[512,4096]{1,0:T(8,128)(2,1)} %param.6) | copy-start | bytes 12582916
  53.2 5.4 %copy-start.2 = (bf16[512,768]{1,0:T(8,128)(2,1)S(1)}, bf16[512,768]{1,0:T(8,128)(2,1)}, u32[]{:S(2)}) copy-start(bf16[512,768]{1,0:T(8,128)(2,1)} %all-gather) | copy-start | bytes 2359300
  54.9 1.9 %copy-start = (bf16[512,4096]{1,0:T(8,128)(2,1)}, bf16[512,4096]{1,0:T(8,128)(2,1)S(1)}, u32[]{:S(2)}) copy-start(bf16[512,4096]{1,0:T(8,128)(2,1)S(1)} %fusion.2.x_ref) | copy-start | bytes 12582916
  58.6 0.9 copy-start.3
  62.1 28.0 %all-to-all-start.1 = ((bf16[4,16,32,512]{3,2,1,0:T(8,128)(2,1)}), bf16[4,16,32,512]{3,2,1,0:T(8,128)(2,1)}, u32[]{:S(2)}, u32[]{:S(2)}) async-start(bf16[4,16,32,512]{3,2,1,0:T(8,128)(2,1)} %shard_map.67), calls=%async_computation.1 | async-start | bytes 4194304 | tf_op jit(solution)/shard_map/all_to_all | solution.py:266
  68.6 4.5 %collective-permute-start = (bf16[4,16,32,256]{3,2,1,0:T(8,128)(2,1)S(1)}, bf16[4,16,32,256]{3,2,1,0:T(8,128)(2,1)S(1)}, u32[]{:S(2)}, u32[]{:S(2)}) collective-permute-start(bf16[4,16,32,256]{3,2,1,0:T(8,128)(2,1)S(1)} %all-to-all-done.wa_ref.refs_2_), channel_id=1, source_target_pairs={{0,16},{16,0},{32,48},{48,32},{64,80},{80,64},{96,112},{112,96},{1... | collective-permute-start | bytes 3145736 | tf_op jit(solution)/shard_map/ppermute | solution.py:270
  71.7 18.4 %copy-start.4 = (f32[512,128]{1,0:T(8,128)}, f32[512,128]{1,0:T(8,128)S(1)}, u32[]{:S(2)}) copy-start(f32[512,128]{1,0:T(8,128)S(1)} %get-tuple-element.8.cos_ref) | copy-start | bytes 786436
  71.8 18.4 %copy-start.5 = (f32[512,128]{1,0:T(8,128)}, f32[512,128]{1,0:T(8,128)S(1)}, u32[]{:S(2)}) copy-start(f32[512,128]{1,0:T(8,128)S(1)} %get-tuple-element.9.sin_ref) | copy-start | bytes 786436
  73.1 2.2 %copy-start.1 = (bf16[512,4096]{1,0:T(8,128)(2,1)S(1)}, bf16[512,4096]{1,0:T(8,128)(2,1)}, u32[]{:S(2)}) copy-start(bf16[512,4096]{1,0:T(8,128)(2,1)} %copy-done) | copy-start | bytes 12582916
  75.3 16.7 %copy-start.9 = (s32[1,2048]{1,0:T(1,128)S(1)}, s32[1,2048]{1,0:T(1,128)}, u32[]{:S(2)}) copy-start(s32[1,2048]{1,0:T(1,128)} %param.11) | copy-start | bytes 24580
  77.9 25.4 %copy-start.6 = (bf16[512,256]{1,0:T(8,128)(2,1)}, bf16[512,256]{1,0:T(8,128)(2,1)S(1)}, u32[]{:S(2)}) copy-start(bf16[512,256]{1,0:T(8,128)(2,1)S(1)} %shard_map.65.kv0_ref) | copy-start | bytes 786436
  77.9 12.2 %collective-permute-start.1 = (bf16[512,256]{1,0:T(8,128)(2,1)S(1)}, bf16[512,256]{1,0:T(8,128)(2,1)S(1)}, u32[]{:S(2)}, u32[]{:S(2)}) collective-permute-start(bf16[512,256]{1,0:T(8,128)(2,1)S(1)} %shard_map.65.kv0_ref), channel_id=1, source_target_pairs={{0,1},{1,2},{2,3},{4,5},{5,6},{6,7},{8,9},{9,10},{10,11},{12,13},{... | collective-permute-start | bytes 786440 | tf_op jit(solution)/shard_map/ppermute | solution.py:294
  90.1 13.2 %copy-start.7 = (bf16[512,256]{1,0:T(8,128)(2,1)}, bf16[512,256]{1,0:T(8,128)(2,1)S(1)}, u32[]{:S(2)}) copy-start(bf16[512,256]{1,0:T(8,128)(2,1)S(1)} %collective-permute-done.1.refs_1_.kv1_ref) | copy-start | bytes 786436
  90.1 13.2 %collective-permute-start.3 = (bf16[4,16,32,512]{3,2,1,0:T(8,128)(2,1)}, bf16[4,16,32,512]{3,2,1,0:T(8,128)(2,1)}, u32[]{:S(2)}, u32[]{:S(2)}) collective-permute-start(bf16[4,16,32,512]{3,2,1,0:T(8,128)(2,1)} %shard_map.68.wa_ref), channel_id=1, source_target_pairs={{0,16},{16,0},{32,48},{48,32},{64,80},{80,64},{96,112},{112,96},{1... | collective-permute-start | bytes 6291464 | tf_op jit(solution)/shard_map/ppermute | solution.py:270
  92.7 10.6 %copy-start.11 = (s32[4,128]{1,0:T(4,128)}, s32[4,128]{1,0:T(4,128)S(1)}, u32[]{:S(2)}) copy-start(s32[4,128]{1,0:T(4,128)S(1)} %maximum_bitcast_fusion.low_ref) | copy-start | bytes 6148
  92.7 10.6 %collective-permute-start.2 = (bf16[512,256]{1,0:T(8,128)(2,1)S(1)}, bf16[512,256]{1,0:T(8,128)(2,1)S(1)}, u32[]{:S(2)}, u32[]{:S(2)}) collective-permute-start(bf16[512,256]{1,0:T(8,128)(2,1)S(1)} %collective-permute-done.1.refs_1_.kv1_ref), channel_id=1, source_target_pairs={{1,2},{2,3},{5,6},{6,7},{9,10},{10,11},{13,14},{14,15},{17,18},{18... | collective-permute-start | bytes 786440 | tf_op jit(solution)/shard_map/ppermute | solution.py:295
  103.3 0.7 copy-start.12

commit v8 on v6

--- a/solution.py
+++ b/solution.py
@@ -251,7 +251,7 @@
         out_ref[n] = x_ref[..., first : first + out_ref.shape[-1]]
 
 
-def spread_attn(x, first, width):
+def four_copies(x, first, width):
     parts = lax.axis_size("attn")
     whole = pl.BlockSpec(memory_space=pltpu.VMEM)
     out = jax.ShapeDtypeStruct((parts, *x.shape[:-1], width), x.dtype)
@@ -263,7 +263,11 @@
         compiler_params=pltpu.CompilerParams(vmem_limit_bytes=8 * 1024 * 1024),
         cost_estimate=pl.CostEstimate(flops=0, bytes_accessed=3 * out.size, transcendentals=0),
     )(x)
-    return lax.all_to_all(spread, "attn", 0, 0, tiled=True)
+    return spread
+
+
+def exchange_attn(copies):
+    return lax.all_to_all(copies, "attn", 0, 0, tiled=True)
 
 
 def swap_cores(half):
@@ -280,8 +284,9 @@
         jnp.concatenate([key_projection_weight, value_projection_weight, w_query], 1)
     )
     normed = normalize(tokens, norm_gain)
-    kv_half = spread_attn(column, 0, split)
-    query_half = spread_attn(after(column, normed[:16, :HEAD_SIZE], kv_half), split, w_query.shape[1])
+    kv_half = exchange_attn(four_copies(column, 0, split))
+    copies = four_copies(column, split, w_query.shape[1])
+    query_half = exchange_attn(after(copies, normed[:16, :HEAD_SIZE], kv_half))
     cosine, sine = rotary_tables(me * rows + jnp.arange(rows, dtype=jnp.int32))
     doc_ids = documents[0]
     my_docs = lax.dynamic_slice_in_dim(doc_ids, me * rows, rows)

time: 110 us -> 108 us (0.982)
  the two profiles are of different devices: /device:TPU:51 before, /device:TPU:17 now
where the time goes in v8:
time: 108 us
  blocking collectives  33.1 us (31%)
  starting transfers between devices  28.2 us (26%)
  Pallas kernels  19 us (18%)
  waiting for transfers between devices  14.7 us (14%)
  other arithmetic  8.4 us (8%)
  local copies, waits for them, and re-layouts  4.29 us (4%)
    all_gather x1, blocking collectives, gather_column(): lax.all_gather(own, 'rows', axis=0, tiled=False, axis_index_groups=same_c...  33.1 us
    ppermute x2, starting transfers between devices, swap_cores(): lax.ppermute(half, 'rows', [(i, i ^ 1) for i in range(lax.axis_size('rows...  15.2 us
    pallas_call x1, Pallas kernels, attend(): pl.pallas_call(attend_kernel, in_specs=[pl.BlockSpec(memory_space=pltpu.S...  12.6 us
    all_to_all x2, starting transfers between devices, exchange_attn(): return lax.all_to_all(copies, 'attn', 0, 0, tiled=True)  8.93 us
    ppermute x1, waiting for transfers between devices, on_device(): kv2 = lax.ppermute(kv, 'attn', [(0, 2), (1, 3)])  5.6 us
    ppermute x1, waiting for transfers between devices, on_device(): kv1 = lax.ppermute(kv, 'attn', [(0, 1), (1, 2), (2, 3)])  5.3 us
    unnamed x24, local copies, waits for them, and re-layouts  4.17 us
    pallas_call x1, Pallas kernels, project_kv(): pl.pallas_call(kv_kernel, grid=(steps,), in_specs=[pl.BlockSpec(memory_sp...  3.85 us
  transfers between devices with their start and end apart: 6, of which 4 were waited for; matrix products, arithmetic and copies ran while one was open for 7% of the time, Pallas kernels for 5%

profile of v8, /device:TPU:17, one launch (start us, length us, event | category | flops | bytes accessed | tf_op | source)
XLA Modules:
  0.0 107.8 jit_solution(1759414391926769238)
XLA Ops:
  0.0 0.8 fusion.5
  0.8 33.1 %all-gather = bf16[512,768]{1,0:T(8,128)(2,1)S(1)} all-gather(bf16[32,768]{1,0:T(8,128)(2,1)S(1)} %fusion.5), channel_id=2, replica_groups={{0,32,64,96,128,160,192,224,256,288,320,352,384,416,448,480},{16,48,80,..., dimensions={0}, use_global_device_ids=true | all-gather | bytes 835584 | tf_op jit(solution)/shard_map/all_gather | solution.py:229
  33.9 1.1 shard_map.64
  34.9 0.0 copy-start.10
  34.9 4.4 %all-to-all-start = ((bf16[4,16,32,256]{3,2,1,0:T(8,128)(2,1)}), bf16[4,16,32,256]{3,2,1,0:T(8,128)(2,1)S(1)}, u32[]{:S(2)}, u32[]{:S(2)}) async-start(bf16[4,16,32,256]{3,2,1,0:T(8,128)(2,1)} %shard_map.64), calls=%async_computation | async-start | bytes 2097152 | tf_op jit(solution)/shard_map/all_to_all | solution.py:270
  39.3 0.0 copy-start.8
  39.3 1.5 %shard_map.66.refs_0_ = bf16[4,16,32,512]{3,2,1,0:T(8,128)(2,1)} custom-call(bf16[16,32,768]{2,1,0:T(8,128)(2,1)S(1)} %bitcast.7), custom_call_target="tpu_custom_call" | custom-call | bytes 3145728 | tf_op jit(solution)/shard_map/pallas_call | solution.py:258
  40.8 3.6 %fusion = f32[512]{0:T(512)S(1)} fusion(bf16[512,4096]{1,0:T(8,128)(2,1)} %param.6), kind=kLoop, calls=%fused_computation.2 | loop fusion | flops 6290944 | bytes 4196352 | tf_op jit(solution)/shard_map/reduce_sum | solution.py:218
  44.4 0.0 copy-done.10
  44.4 0.0 copy-done.8
  44.4 1.7 %fusion.2.x_ref = bf16[512,4096]{1,0:T(8,128)(2,1)S(1)} fusion(bf16[512,4096]{1,0:T(8,128)(2,1)S(1)} %copy-done.8, f32[4096]{0:T(1024)S(1)} %convert_element_type.21, f32[512]{0:T(512)S(1)} %add_rsqrt_fusion), kind=kLoop, calls=%fused_computation.4 | loop fusion | flops 8388608 | bytes 8407040 | tf_op jit(solution)/shard_map/convert_element_type | solution.py:219
  46.1 0.0 copy-start
  46.1 1.9 %copy-done = bf16[512,4096]{1,0:T(8,128)(2,1)} copy-done((bf16[512,4096]{1,0:T(8,128)(2,1)}, bf16[512,4096]{1,0:T(8,128)(2,1)S(1)}, u32[]{:S(2)}) %copy-start) | copy-done | bytes 4194328
  48.1 0.0 all-to-all-done.wa_ref.refs_2_
  48.1 4.6 %all-to-all-start.1 = ((bf16[4,16,32,512]{3,2,1,0:T(8,128)(2,1)}), bf16[4,16,32,512]{3,2,1,0:T(8,128)(2,1)S(1)}, u32[]{:S(2)}, u32[]{:S(2)}) async-start(bf16[4,16,32,512]{3,2,1,0:T(8,128)(2,1)} %shard_map.67), calls=%async_computation.1 | async-start | bytes 4194304 | tf_op jit(solution)/shard_map/all_to_all | solution.py:270
  52.6 12.0 %collective-permute-start = (bf16[4,16,32,256]{3,2,1,0:T(8,128)(2,1)S(1)}, bf16[4,16,32,256]{3,2,1,0:T(8,128)(2,1)}, u32[]{:S(2)}, u32[]{:S(2)}) collective-permute-start(bf16[4,16,32,256]{3,2,1,0:T(8,128)(2,1)S(1)} %all-to-all-done.wa_ref.refs_2_), channel_id=1, source_target_pairs={{0,16},{16,0},{32,48},{48,32},{64,80},{80,64},{96,112},{112,96},{1... | collective-permute-start | bytes 3145736 | tf_op jit(solution)/shard_map/ppermute | solution.py:274
  64.7 1.0 fusion.3
  65.7 0.2 pad_maximum_fusion
  65.9 0.0 copy-start.4
  65.9 0.0 copy-start.3
  65.9 1.1 %collective-permute-done.wb_ref = bf16[4,16,32,256]{3,2,1,0:T(8,128)(2,1)} collective-permute-done((bf16[4,16,32,256]{3,2,1,0:T(8,128)(2,1)S(1)}, bf16[4,16,32,256]{3,2,1,0:T(8,128)(2,1)}, u32[]{:S(2)}, u32[]{:S(2)}) %collective-permute-start) | collective-permute-done | bytes 1048608 | tf_op jit(solution)/shard_map/ppermute | solution.py:274
  67.1 0.0 copy-start.1
  67.1 2.2 %copy-done.1 = bf16[512,4096]{1,0:T(8,128)(2,1)S(1)} copy-done((bf16[512,4096]{1,0:T(8,128)(2,1)S(1)}, bf16[512,4096]{1,0:T(8,128)(2,1)}, u32[]{:S(2)}) %copy-start.1) | copy-done | bytes 4194328
  69.3 0.0 copy-start.9
  69.3 3.8 %shard_map.65.kv0_ref = bf16[512,256]{1,0:T(8,128)(2,1)S(1)} custom-call(s32[1]{0:T(128)} %bitcast.core_ref, bf16[512,4096]{1,0:T(8,128)(2,1)S(1)} %copy-done.1, bf16[4,16,32,256]{3,2,1,0:T(8,128)(2,1)S(1)} %all-to-all-done.wa_ref.refs_2_, bf16[4,16,32,256]{3,2,1,0:T(8,128)(2,1)} %collective-permute-done.wb_ref, f32[512,128]{1,0:T(8,128)S(1)} %get-tuple-element.8.cos_ref, ...), custom_call_target="tpu_custom_call" | custom-call | flops 1073741824 | bytes 6553600 | tf_op jit(solution)/shard_map/pallas_call | solution.py:60
  73.1 0.0 copy-start.5
  73.1 2.8 %collective-permute-start.2 = (bf16[512,256]{1,0:T(8,128)(2,1)S(1)}, bf16[512,256]{1,0:T(8,128)(2,1)S(1)}, u32[]{:S(2)}, u32[]{:S(2)}) collective-permute-start(bf16[512,256]{1,0:T(8,128)(2,1)S(1)} %shard_map.65.kv0_ref), channel_id=1, source_target_pairs={{0,1},{1,2},{2,3},{4,5},{5,6},{6,7},{8,9},{9,10},{10,11},{12,13},{... | collective-permute-start | bytes 786440 | tf_op jit(solution)/shard_map/ppermute | solution.py:299
  75.9 1.3 %collective-permute-start.1 = (bf16[512,256]{1,0:T(8,128)(2,1)S(1)}, bf16[512,256]{1,0:T(8,128)(2,1)S(1)}, u32[]{:S(2)}, u32[]{:S(2)}) collective-permute-start(bf16[512,256]{1,0:T(8,128)(2,1)S(1)} %shard_map.65.kv0_ref), channel_id=1, source_target_pairs={{0,2},{1,3},{4,6},{5,7},{8,10},{9,11},{12,14},{13,15},{16,18},{17,... | collective-permute-start | bytes 786440 | tf_op jit(solution)/shard_map/ppermute | solution.py:300
  77.2 5.3 %collective-permute-done.2.refs_1_.kv1_ref = bf16[512,256]{1,0:T(8,128)(2,1)S(1)} collective-permute-done((bf16[512,256]{1,0:T(8,128)(2,1)S(1)}, bf16[512,256]{1,0:T(8,128)(2,1)S(1)}, u32[]{:S(2)}, u32[]{:S(2)}) %collective-permute-start.2) | collective-permute-done | bytes 262176 | tf_op jit(solution)/shard_map/ppermute | solution.py:299
  82.5 0.0 copy-done.4
  82.5 0.0 copy-done.5
  82.5 0.0 copy-start.6
  82.5 5.6 %collective-permute-done.1.refs_2_.kv2_ref = bf16[512,256]{1,0:T(8,128)(2,1)S(1)} collective-permute-done((bf16[512,256]{1,0:T(8,128)(2,1)S(1)}, bf16[512,256]{1,0:T(8,128)(2,1)S(1)}, u32[]{:S(2)}, u32[]{:S(2)}) %collective-permute-start.1) | collective-permute-done | bytes 262176 | tf_op jit(solution)/shard_map/ppermute | solution.py:300
  88.1 0.0 copy-start.7
  88.1 0.0 all-to-all-done.1.refs_0_
  88.2 0.0 copy-done.3
  88.2 0.0 copy-start.2
  88.2 3.1 %collective-permute-start.3 = (bf16[4,16,32,512]{3,2,1,0:T(8,128)(2,1)S(1)}, bf16[4,16,32,512]{3,2,1,0:T(8,128)(2,1)}, u32[]{:S(2)}, u32[]{:S(2)}) collective-permute-start(bf16[4,16,32,512]{3,2,1,0:T(8,128)(2,1)S(1)} %shard_map.68.wa_ref), channel_id=1, source_target_pairs={{0,16},{16,0},{32,48},{48,32},{64,80},{80,64},{96,112},{112,96},{1... | collective-permute-start | bytes 6291464 | tf_op jit(solution)/shard_map/ppermute | solution.py:274
  91.3 0.0 copy-done.9
  91.3 0.6 convert_reduce_fusion
  91.9 0.0 copy-start.11
  91.9 0.1 slice_reduce_fusion
  92.1 0.5 and_select_fusion.first_ref
  92.5 2.6 %collective-permute-done.3.wb_ref = bf16[4,16,32,512]{3,2,1,0:T(8,128)(2,1)} collective-permute-done((bf16[4,16,32,512]{3,2,1,0:T(8,128)(2,1)S(1)}, bf16[4,16,32,512]{3,2,1,0:T(8,128)(2,1)}, u32[]{:S(2)}, u32[]{:S(2)}) %collective-permute-start.3) | collective-permute-done | bytes 2097184 | tf_op jit(solution)/shard_map/ppermute | solution.py:274
  95.2 0.0 copy-done.6
  95.2 0.0 copy-done.7
  95.2 0.0 copy-done.2
  95.2 0.0 copy-done.11
  95.2 12.6 %shard_map.69 = bf16[512,512]{1,0:T(8,128)(2,1)} custom-call(s32[1]{0:T(128)} %bitcast.core_ref, s32[4]{0:T(128)} %and_select_fusion.first_ref, s32[4,128]{1,0:T(4,128)} %copy-done.11, bf16[512,4096]{1,0:T(8,128)(2,1)} %copy-done, f32[512,128]{1,0:T(8,128)} %copy-done.3, f32[512,128]{1,0:T(8,128)} %copy-done.4, bf16[512,256]{1,0:T(8,128)(2,1)} %copy-done.7, ...), custom_call_target="tpu_custom_call" | custom-call | flops 3221225472 | bytes 8388608 | tf_op jit(solution)/shard_map/pallas_call | solution.py:187
  (9 shorter events, 0.1 us)
Async XLA Ops:
  34.9 9.5 %copy-start.10 = (bf16[4096]{0:T(1024)(128)(2,1)S(1)}, bf16[4096]{0:T(1024)(128)(2,1)}, u32[]{:S(2)}) copy-start(bf16[4096]{0:T(1024)(128)(2,1)} %param.7) | copy-start | bytes 24580
  34.9 13.1 %all-to-all-start = ((bf16[4,16,32,256]{3,2,1,0:T(8,128)(2,1)}), bf16[4,16,32,256]{3,2,1,0:T(8,128)(2,1)S(1)}, u32[]{:S(2)}, u32[]{:S(2)}) async-start(bf16[4,16,32,256]{3,2,1,0:T(8,128)(2,1)} %shard_map.64), calls=%async_computation | async-start | bytes 2097152 | tf_op jit(solution)/shard_map/all_to_all | solution.py:270
  39.3 5.1 %copy-start.8 = (bf16[512,4096]{1,0:T(8,128)(2,1)S(1)}, bf16[512,4096]{1,0:T(8,128)(2,1)}, u32[]{:S(2)}) copy-start(bf16[512,4096]{1,0:T(8,128)(2,1)} %param.6) | copy-start | bytes 12582916
  46.1 1.9 %copy-start = (bf16[512,4096]{1,0:T(8,128)(2,1)}, bf16[512,4096]{1,0:T(8,128)(2,1)S(1)}, u32[]{:S(2)}) copy-start(bf16[512,4096]{1,0:T(8,128)(2,1)S(1)} %fusion.2.x_ref) | copy-start | bytes 12582916
  48.1 40.1 %all-to-all-start.1 = ((bf16[4,16,32,512]{3,2,1,0:T(8,128)(2,1)}), bf16[4,16,32,512]{3,2,1,0:T(8,128)(2,1)S(1)}, u32[]{:S(2)}, u32[]{:S(2)}) async-start(bf16[4,16,32,512]{3,2,1,0:T(8,128)(2,1)} %shard_map.67), calls=%async_computation.1 | async-start | bytes 4194304 | tf_op jit(solution)/shard_map/all_to_all | solution.py:270
  52.6 14.4 %collective-permute-start = (bf16[4,16,32,256]{3,2,1,0:T(8,128)(2,1)S(1)}, bf16[4,16,32,256]{3,2,1,0:T(8,128)(2,1)}, u32[]{:S(2)}, u32[]{:S(2)}) collective-permute-start(bf16[4,16,32,256]{3,2,1,0:T(8,128)(2,1)S(1)} %all-to-all-done.wa_ref.refs_2_), channel_id=1, source_target_pairs={{0,16},{16,0},{32,48},{48,32},{64,80},{80,64},{96,112},{112,96},{1... | collective-permute-start | bytes 3145736 | tf_op jit(solution)/shard_map/ppermute | solution.py:274
  65.9 16.6 %copy-start.4 = (f32[512,128]{1,0:T(8,128)}, f32[512,128]{1,0:T(8,128)S(1)}, u32[]{:S(2)}) copy-start(f32[512,128]{1,0:T(8,128)S(1)} %get-tuple-element.9.sin_ref) | copy-start | bytes 786436
  65.9 22.2 %copy-start.3 = (f32[512,128]{1,0:T(8,128)}, f32[512,128]{1,0:T(8,128)S(1)}, u32[]{:S(2)}) copy-start(f32[512,128]{1,0:T(8,128)S(1)} %get-tuple-element.8.cos_ref) | copy-start | bytes 786436
  67.1 2.2 %copy-start.1 = (bf16[512,4096]{1,0:T(8,128)(2,1)S(1)}, bf16[512,4096]{1,0:T(8,128)(2,1)}, u32[]{:S(2)}) copy-start(bf16[512,4096]{1,0:T(8,128)(2,1)} %copy-done) | copy-start | bytes 12582916
  69.3 22.0 %copy-start.9 = (s32[1,2048]{1,0:T(1,128)S(1)}, s32[1,2048]{1,0:T(1,128)}, u32[]{:S(2)}) copy-start(s32[1,2048]{1,0:T(1,128)} %param.11) | copy-start | bytes 24580
  73.1 9.4 %copy-start.5 = (bf16[512,256]{1,0:T(8,128)(2,1)}, bf16[512,256]{1,0:T(8,128)(2,1)S(1)}, u32[]{:S(2)}) copy-start(bf16[512,256]{1,0:T(8,128)(2,1)S(1)} %shard_map.65.kv0_ref) | copy-start | bytes 786436
  73.1 9.4 %collective-permute-start.2 = (bf16[512,256]{1,0:T(8,128)(2,1)S(1)}, bf16[512,256]{1,0:T(8,128)(2,1)S(1)}, u32[]{:S(2)}, u32[]{:S(2)}) collective-permute-start(bf16[512,256]{1,0:T(8,128)(2,1)S(1)} %shard_map.65.kv0_ref), channel_id=1, source_target_pairs={{0,1},{1,2},{2,3},{4,5},{5,6},{6,7},{8,9},{9,10},{10,11},{12,13},{... | collective-permute-start | bytes 786440 | tf_op jit(solution)/shard_map/ppermute | solution.py:299
  75.9 12.2 %collective-permute-start.1 = (bf16[512,256]{1,0:T(8,128)(2,1)S(1)}, bf16[512,256]{1,0:T(8,128)(2,1)S(1)}, u32[]{:S(2)}, u32[]{:S(2)}) collective-permute-start(bf16[512,256]{1,0:T(8,128)(2,1)S(1)} %shard_map.65.kv0_ref), channel_id=1, source_target_pairs={{0,2},{1,3},{4,6},{5,7},{8,10},{9,11},{12,14},{13,15},{16,18},{17,... | collective-permute-start | bytes 786440 | tf_op jit(solution)/shard_map/ppermute | solution.py:300
  82.5 12.7 %copy-start.6 = (bf16[512,256]{1,0:T(8,128)(2,1)}, bf16[512,256]{1,0:T(8,128)(2,1)S(1)}, u32[]{:S(2)}) copy-start(bf16[512,256]{1,0:T(8,128)(2,1)S(1)} %collective-permute-done.2.refs_1_.kv1_ref) | copy-start | bytes 786436
  88.1 7.1 %copy-start.7 = (bf16[512,256]{1,0:T(8,128)(2,1)}, bf16[512,256]{1,0:T(8,128)(2,1)S(1)}, u32[]{:S(2)}) copy-start(bf16[512,256]{1,0:T(8,128)(2,1)S(1)} %collective-permute-done.1.refs_2_.kv2_ref) | copy-start | bytes 786436
  88.2 7.0 %copy-start.2 = (bf16[4,16,32,512]{3,2,1,0:T(8,128)(2,1)}, bf16[4,16,32,512]{3,2,1,0:T(8,128)(2,1)S(1)}, u32[]{:S(2)}) copy-start(bf16[4,16,32,512]{3,2,1,0:T(8,128)(2,1)S(1)} %shard_map.68.wa_ref) | copy-start | bytes 6291460
  88.2 7.0 %collective-permute-start.3 = (bf16[4,16,32,512]{3,2,1,0:T(8,128)(2,1)S(1)}, bf16[4,16,32,512]{3,2,1,0:T(8,128)(2,1)}, u32[]{:S(2)}, u32[]{:S(2)}) collective-permute-start(bf16[4,16,32,512]{3,2,1,0:T(8,128)(2,1)S(1)} %shard_map.68.wa_ref), channel_id=1, source_target_pairs={{0,16},{16,0},{32,48},{48,32},{64,80},{80,64},{96,112},{112,96},{1... | collective-permute-start | bytes 6291464 | tf_op jit(solution)/shard_map/ppermute | solution.py:274
  91.9 3.3 %copy-start.11 = (s32[4,128]{1,0:T(4,128)}, s32[4,128]{1,0:T(4,128)S(1)}, u32[]{:S(2)}) copy-start(s32[4,128]{1,0:T(4,128)S(1)} %maximum_bitcast_fusion.low_ref) | copy-start | bytes 6148

commit v9 on v8

--- a/solution.py
+++ b/solution.py
@@ -27,51 +27,71 @@
     return u * cosine + pltpu.roll(u, HEAD_SIZE // 2, 1) * sine
 
 
-def kv_kernel(core_ref, x_ref, wa_ref, wb_ref, cos_ref, sin_ref, out_ref, acc_ref):
-    step = pl.program_id(0)
-    first = core_ref[0] == 0
-    rows = []
-    for chip in range(wa_ref.shape[1]):
-        own = jnp.concatenate([wa_ref[k, chip] for k in range(wa_ref.shape[0])], axis=0)
-        other = jnp.concatenate([wb_ref[k, chip] for k in range(wb_ref.shape[0])], axis=0)
-        rows += [jnp.where(first, own, other), jnp.where(first, other, own)]
-    part = jnp.dot(x_ref[...], jnp.concatenate(rows, axis=0), preferred_element_type=jnp.float32)
-
-    @pl.when(step == 0)
-    def _():
-        acc_ref[...] = part
-
-    @pl.when(step > 0)
-    def _():
-        acc_ref[...] += part
-
-    @pl.when(step == pl.num_programs(0) - 1)
-    def _():
-        keys = rotate(acc_ref[:, :HEAD_SIZE], cos_ref[...], sin_ref[...])
-        out_ref[:, :HEAD_SIZE] = keys.astype(jnp.bfloat16)
-        out_ref[:, HEAD_SIZE:] = acc_ref[:, HEAD_SIZE:].astype(jnp.bfloat16)
-
-
-def project_kv(core, x, wa, wb, cosine, sine, steps=4):
+def bring_weights(bring, core, chips, own, other, w):
+    for k in range(own.shape[0]):
+        bring(own.at[k, chips], w.at[chips, core, k])
+        bring(other.at[k, chips], w.at[chips, 1 - core, k])
+
+
+def kv_kernel(
+    core_ref, x_ref, wa_ref, wb_ref, cos_ref, sin_ref, out_ref, x, w, cos, sin, sums, sems
+):
+    rows, depth = x_ref.shape
+    width = out_ref.shape[1]
+    pieces = 4
+    count = wa_ref.shape[1] // pieces
+    piece = depth // pieces
+    copies = []
+
+    def bring(src, dst):
+        copies.append(pltpu.make_async_copy(src, dst, sems.at[len(copies)]))
+        copies[-1].start()
+
+    ready = []
+    for n in range(pieces):
+        begin = len(copies)
+        bring_weights(bring, core_ref[0], pl.ds(n * count, count), wa_ref, wb_ref, w)
+        take = pl.ds(n * piece, piece)
+        bring(x_ref.at[:, take], x.at[:, take])
+        ready.append(copies[begin:])
+    bring(cos_ref, cos)
+    bring(sin_ref, sin)
+    for n in range(pieces):
+        for copy in ready[n]:
+            copy.wait()
+        weights = w[n * count : (n + 1) * count].reshape(piece, width)
+        part = jnp.dot(
+            x[:, n * piece : (n + 1) * piece], weights, preferred_element_type=jnp.float32
+        )
+        if n == 0:
+            sums[...] = part
+        else:
+            sums[...] += part
+    copies[-2].wait()
+    copies[-1].wait()
+    keys = rotate(sums[:, :HEAD_SIZE], cos[...], sin[...])
+    out_ref[:, :HEAD_SIZE] = keys.astype(jnp.bfloat16)
+    out_ref[:, HEAD_SIZE:] = sums[:, HEAD_SIZE:].astype(jnp.bfloat16)
+
+
+def project_kv(core, x, wa, wb, cosine, sine):
     rows, depth = x.shape
     quarters, chips, part, width = wa.shape
-    w_spec = pl.BlockSpec((quarters, chips // steps, part, width), lambda s: (0, s, 0, 0))
-    table = pl.BlockSpec((rows, HEAD_SIZE), lambda s: (0, 0))
     return pl.pallas_call(
         kv_kernel,
-        grid=(steps,),
-        in_specs=[
-            pl.BlockSpec(memory_space=pltpu.SMEM),
-            pl.BlockSpec((rows, depth // steps), lambda s: (0, s)),
-            w_spec,
-            w_spec,
-            table,
-            table,
+        in_specs=[pl.BlockSpec(memory_space=pltpu.SMEM)]
+        + [pl.BlockSpec(memory_space=pl.ANY)] * 5,
+        out_specs=pl.BlockSpec(memory_space=pltpu.VMEM),
+        out_shape=jax.ShapeDtypeStruct((rows, width), jnp.bfloat16),
+        scratch_shapes=[
+            pltpu.VMEM((rows, depth), jnp.bfloat16),
+            pltpu.VMEM((chips, 2, quarters, part, width), jnp.bfloat16),
+            pltpu.VMEM((rows, HEAD_SIZE), jnp.float32),
+            pltpu.VMEM((rows, HEAD_SIZE), jnp.float32),
+            pltpu.VMEM((rows, width), jnp.float32),
+            pltpu.SemaphoreType.DMA((4 * (2 * quarters + 1) + 2,)),
         ],
-        out_specs=pl.BlockSpec((rows, width), lambda s: (0, 0)),
-        out_shape=jax.ShapeDtypeStruct((rows, width), jnp.bfloat16),
-        scratch_shapes=[pltpu.VMEM((rows, width), jnp.float32)],
-        compiler_params=pltpu.CompilerParams(vmem_limit_bytes=20 * 1024 * 1024),
+        compiler_params=pltpu.CompilerParams(vmem_limit_bytes=60 * 1024 * 1024),
         cost_estimate=pl.CostEstimate(
             flops=2 * rows * depth * width,
             bytes_accessed=2 * (rows * depth + depth * width + rows * width),
@@ -101,9 +121,7 @@
     for n in range(pieces):
         begin = len(copies)
         some = pl.ds(n * count, count)
-        for k in range(quarters):
-            bring(wa_ref.at[k, some], w.at[some, core_ref[0], k])
-            bring(wb_ref.at[k, some], w.at[some, 1 - core_ref[0], k])
+        bring_weights(bring, core_ref[0], some, wa_ref, wb_ref, w)
         take = pl.ds(n * piece, piece)
         bring(x_ref.at[:, take], x.at[:, take])
         ready.append(copies[begin:])

time: 108 us -> 108 us (level)
  the two profiles are of different devices: /device:TPU:17 before, /device:TPU:22 now
where the time goes in v9:
time: 108 us; the launch traced here: 107 us
  blocking collectives  40.1 us (37%)
  Pallas kernels  20.5 us (19%)
  starting transfers between devices  19.5 us (18%)
  waiting for transfers between devices  15.7 us (15%)
  other arithmetic  9.36 us (9%)
  local copies, waits for them, and re-layouts  2.1 us (2%)
    all_gather x1, blocking collectives, gather_column(): lax.all_gather(own, 'rows', axis=0, tiled=False, axis_index_groups=same_c...  40.1 us
    pallas_call x1, Pallas kernels, attend(): pl.pallas_call(attend_kernel, in_specs=[pl.BlockSpec(memory_space=pltpu.S...  12.6 us
    ppermute x1, waiting for transfers between devices, on_device(): kv1 = lax.ppermute(kv, 'attn', [(0, 1), (1, 2), (2, 3)])  12.1 us
    all_to_all x2, starting transfers between devices, exchange_attn(): return lax.all_to_all(copies, 'attn', 0, 0, tiled=True)  11.3 us
    pallas_call x1, Pallas kernels, project_kv(): pl.pallas_call(kv_kernel, in_specs=[pl.BlockSpec(memory_space=pltpu.SMEM)...  5.27 us
    ppermute x2, starting transfers between devices, swap_cores(): lax.ppermute(half, 'rows', [(i, i ^ 1) for i in range(lax.axis_size('rows...  3.83 us
    reduce_sum x1, other arithmetic, normalize(): mean_sq = jnp.mean(widened * widened, axis=-1, keepdims=True)  3.63 us
    ppermute x2, waiting for transfers between devices, swap_cores(): lax.ppermute(half, 'rows', [(i, i ^ 1) for i in range(lax.axis_size('rows...  3.57 us
  transfers between devices with their start and end apart: 6, of which 3 were waited for; matrix products, arithmetic and copies ran while one was open for 8% of the time, Pallas kernels for 6%

profile of v9, /device:TPU:22, one launch (start us, length us, event | category | flops | bytes accessed | tf_op | source)
XLA Modules:
  0.0 107.4 jit_solution(17939519931553224943)
XLA Ops:
  0.0 0.8 fusion.5
  0.8 40.1 %all-gather = bf16[512,768]{1,0:T(8,128)(2,1)S(1)} all-gather(bf16[32,768]{1,0:T(8,128)(2,1)S(1)} %fusion.5), channel_id=2, replica_groups={{0,32,64,96,128,160,192,224,256,288,320,352,384,416,448,480},{16,48,80,..., dimensions={0}, use_global_device_ids=true | all-gather | bytes 835584 | tf_op jit(solution)/shard_map/all_gather | solution.py:247
  40.9 1.1 shard_map.64
  42.0 0.0 copy-start.7
  42.0 4.9 %all-to-all-start = ((bf16[4,16,32,256]{3,2,1,0:T(8,128)(2,1)}), bf16[4,16,32,256]{3,2,1,0:T(8,128)(2,1)S(1)}, u32[]{:S(2)}, u32[]{:S(2)}) async-start(bf16[4,16,32,256]{3,2,1,0:T(8,128)(2,1)} %shard_map.64), calls=%async_computation | async-start | bytes 2097152 | tf_op jit(solution)/shard_map/all_to_all | solution.py:288
  46.9 0.0 copy-start.5
  46.9 1.5 %shard_map.66.refs_0_ = bf16[4,16,32,512]{3,2,1,0:T(8,128)(2,1)} custom-call(bf16[16,32,768]{2,1,0:T(8,128)(2,1)S(1)} %bitcast.7), custom_call_target="tpu_custom_call" | custom-call | bytes 3145728 | tf_op jit(solution)/shard_map/pallas_call | solution.py:276
  48.4 3.6 %fusion = f32[512]{0:T(512)S(1)} fusion(bf16[512,4096]{1,0:T(8,128)(2,1)} %param.6), kind=kLoop, calls=%fused_computation.2 | loop fusion | flops 6290944 | bytes 4196352 | tf_op jit(solution)/shard_map/reduce_sum | solution.py:236
  52.0 0.0 copy-done.7
  52.0 0.0 copy-done.5
  52.0 1.7 %fusion.2.x_ref = bf16[512,4096]{1,0:T(8,128)(2,1)S(1)} fusion(bf16[512,4096]{1,0:T(8,128)(2,1)S(1)} %copy-done.5, f32[4096]{0:T(1024)S(1)} %convert_element_type.21, f32[512]{0:T(512)S(1)} %add_rsqrt_fusion), kind=kLoop, calls=%fused_computation.4 | loop fusion | flops 8388608 | bytes 8407040 | tf_op jit(solution)/shard_map/convert_element_type | solution.py:237
  53.7 0.0 copy-start.4
  53.7 1.9 %copy-done.4 = bf16[512,4096]{1,0:T(8,128)(2,1)} copy-done((bf16[512,4096]{1,0:T(8,128)(2,1)}, bf16[512,4096]{1,0:T(8,128)(2,1)S(1)}, u32[]{:S(2)}) %copy-start.4) | copy-done | bytes 4194328
  55.7 0.0 all-to-all-done.wa_ref.refs_2_
  55.7 0.0 copy-start
  55.7 6.4 %all-to-all-start.1 = ((bf16[4,16,32,512]{3,2,1,0:T(8,128)(2,1)}), bf16[4,16,32,512]{3,2,1,0:T(8,128)(2,1)S(1)}, u32[]{:S(2)}, u32[]{:S(2)}) async-start(bf16[4,16,32,512]{3,2,1,0:T(8,128)(2,1)} %shard_map.67), calls=%async_computation.1 | async-start | bytes 4194304 | tf_op jit(solution)/shard_map/all_to_all | solution.py:288
  62.1 0.0 copy-done
  62.1 1.9 %collective-permute-start = (bf16[4,16,32,256]{3,2,1,0:T(8,128)(2,1)S(1)}, bf16[4,16,32,256]{3,2,1,0:T(8,128)(2,1)}, u32[]{:S(2)}, u32[]{:S(2)}) collective-permute-start(bf16[4,16,32,256]{3,2,1,0:T(8,128)(2,1)S(1)} %all-to-all-done.wa_ref.refs_2_), channel_id=1, source_target_pairs={{0,16},{16,0},{32,48},{48,32},{64,80},{80,64},{96,112},{112,96},{1... | collective-permute-start | bytes 3145736 | tf_op jit(solution)/shard_map/ppermute | solution.py:292
  64.1 1.0 fusion.3
  65.0 1.1 pad_maximum_fusion
  66.1 0.7 collective-permute-done.wb_ref
  66.8 0.0 copy-start.6
  66.8 5.3 %shard_map.65.kv0_ref = bf16[512,256]{1,0:T(8,128)(2,1)} custom-call(s32[1]{0:T(128)} %bitcast.core_ref, bf16[512,4096]{1,0:T(8,128)(2,1)} %copy-done.4, bf16[4,16,32,256]{3,2,1,0:T(8,128)(2,1)} %copy-done, bf16[4,16,32,256]{3,2,1,0:T(8,128)(2,1)} %collective-permute-done.wb_ref, f32[512,128]{1,0:T(8,128)} %get-tuple-element.8.cos_ref, ...), custom_call_target="tpu_custom_call" | custom-call | flops 1073741824 | bytes 6553600 | tf_op jit(solution)/shard_map/pallas_call | solution.py:80
  72.1 3.1 %collective-permute-start.2 = (bf16[512,256]{1,0:T(8,128)(2,1)}, bf16[512,256]{1,0:T(8,128)(2,1)S(1)}, u32[]{:S(2)}, u32[]{:S(2)}) collective-permute-start(bf16[512,256]{1,0:T(8,128)(2,1)} %shard_map.65.kv0_ref), channel_id=1, source_target_pairs={{0,1},{1,2},{2,3},{4,5},{5,6},{6,7},{8,9},{9,10},{10,11},{12,13},{... | collective-permute-start | bytes 786440 | tf_op jit(solution)/shard_map/ppermute | solution.py:317
  75.1 1.3 %collective-permute-start.1 = (bf16[512,256]{1,0:T(8,128)(2,1)}, bf16[512,256]{1,0:T(8,128)(2,1)S(1)}, u32[]{:S(2)}, u32[]{:S(2)}) collective-permute-start(bf16[512,256]{1,0:T(8,128)(2,1)} %shard_map.65.kv0_ref), channel_id=1, source_target_pairs={{0,2},{1,3},{4,6},{5,7},{8,10},{9,11},{12,14},{13,15},{16,18},{17,... | collective-permute-start | bytes 786440 | tf_op jit(solution)/shard_map/ppermute | solution.py:318
  76.4 12.1 %collective-permute-done.2.refs_1_.kv1_ref = bf16[512,256]{1,0:T(8,128)(2,1)S(1)} collective-permute-done((bf16[512,256]{1,0:T(8,128)(2,1)}, bf16[512,256]{1,0:T(8,128)(2,1)S(1)}, u32[]{:S(2)}, u32[]{:S(2)}) %collective-permute-start.2) | collective-permute-done | bytes 262176 | tf_op jit(solution)/shard_map/ppermute | solution.py:317
  88.5 0.0 copy-start.2
  88.5 0.0 collective-permute-done.1.refs_2_.kv2_ref
  88.6 0.0 copy-start.3
  88.6 0.0 all-to-all-done.1.refs_0_
  88.6 0.0 copy-start.1
  88.6 1.9 %collective-permute-start.3 = (bf16[4,16,32,512]{3,2,1,0:T(8,128)(2,1)S(1)}, bf16[4,16,32,512]{3,2,1,0:T(8,128)(2,1)}, u32[]{:S(2)}, u32[]{:S(2)}) collective-permute-start(bf16[4,16,32,512]{3,2,1,0:T(8,128)(2,1)S(1)} %shard_map.68.wa_ref), channel_id=1, source_target_pairs={{0,16},{16,0},{32,48},{48,32},{64,80},{80,64},{96,112},{112,96},{1... | collective-permute-start | bytes 6291464 | tf_op jit(solution)/shard_map/ppermute | solution.py:292
  90.5 0.0 copy-done.6
  90.5 0.6 convert_reduce_fusion
  91.1 0.0 copy-start.8
  91.2 0.1 slice_reduce_fusion
  91.3 0.6 and_select_fusion.first_ref
  91.9 2.9 %collective-permute-done.3.wb_ref = bf16[4,16,32,512]{3,2,1,0:T(8,128)(2,1)} collective-permute-done((bf16[4,16,32,512]{3,2,1,0:T(8,128)(2,1)S(1)}, bf16[4,16,32,512]{3,2,1,0:T(8,128)(2,1)}, u32[]{:S(2)}, u32[]{:S(2)}) %collective-permute-start.3) | collective-permute-done | bytes 2097184 | tf_op jit(solution)/shard_map/ppermute | solution.py:292
  94.8 0.0 copy-done.2
  94.8 0.0 copy-done.3
  94.8 0.0 copy-done.1
  94.8 0.0 copy-done.8
  94.8 12.6 %shard_map.69 = bf16[512,512]{1,0:T(8,128)(2,1)} custom-call(s32[1]{0:T(128)} %bitcast.core_ref, s32[4]{0:T(128)} %and_select_fusion.first_ref, s32[4,128]{1,0:T(4,128)} %copy-done.8, bf16[512,4096]{1,0:T(8,128)(2,1)} %copy-done.4, f32[512,128]{1,0:T(8,128)} %get-tuple-element.8.cos_ref, f32[512,128]{1,0:T(8,128)} %get-tuple-element.9.sin_ref, ...), custom_call_target="tpu_custom_call" | custom-call | flops 3221225472 | bytes 8388608 | tf_op jit(solution)/shard_map/pallas_call | solution.py:205
  (9 shorter events, 0.1 us)
Async XLA Ops:
  42.0 10.0 %copy-start.7 = (bf16[4096]{0:T(1024)(128)(2,1)S(1)}, bf16[4096]{0:T(1024)(128)(2,1)}, u32[]{:S(2)}) copy-start(bf16[4096]{0:T(1024)(128)(2,1)} %param.7) | copy-start | bytes 24580
  42.0 13.7 %all-to-all-start = ((bf16[4,16,32,256]{3,2,1,0:T(8,128)(2,1)}), bf16[4,16,32,256]{3,2,1,0:T(8,128)(2,1)S(1)}, u32[]{:S(2)}, u32[]{:S(2)}) async-start(bf16[4,16,32,256]{3,2,1,0:T(8,128)(2,1)} %shard_map.64), calls=%async_computation | async-start | bytes 2097152 | tf_op jit(solution)/shard_map/all_to_all | solution.py:288
  46.9 5.1 %copy-start.5 = (bf16[512,4096]{1,0:T(8,128)(2,1)S(1)}, bf16[512,4096]{1,0:T(8,128)(2,1)}, u32[]{:S(2)}) copy-start(bf16[512,4096]{1,0:T(8,128)(2,1)} %param.6) | copy-start | bytes 12582916
  53.7 1.9 %copy-start.4 = (bf16[512,4096]{1,0:T(8,128)(2,1)}, bf16[512,4096]{1,0:T(8,128)(2,1)S(1)}, u32[]{:S(2)}) copy-start(bf16[512,4096]{1,0:T(8,128)(2,1)S(1)} %fusion.2.x_ref) | copy-start | bytes 12582916
  55.7 6.4 %copy-start = (bf16[4,16,32,256]{3,2,1,0:T(8,128)(2,1)}, bf16[4,16,32,256]{3,2,1,0:T(8,128)(2,1)S(1)}, u32[]{:S(2)}) copy-start(bf16[4,16,32,256]{3,2,1,0:T(8,128)(2,1)S(1)} %all-to-all-done.wa_ref.refs_2_) | copy-start | bytes 3145732
  55.7 32.9 %all-to-all-start.1 = ((bf16[4,16,32,512]{3,2,1,0:T(8,128)(2,1)}), bf16[4,16,32,512]{3,2,1,0:T(8,128)(2,1)S(1)}, u32[]{:S(2)}, u32[]{:S(2)}) async-start(bf16[4,16,32,512]{3,2,1,0:T(8,128)(2,1)} %shard_map.67), calls=%async_computation.1 | async-start | bytes 4194304 | tf_op jit(solution)/shard_map/all_to_all | solution.py:288
  62.1 4.7 %collective-permute-start = (bf16[4,16,32,256]{3,2,1,0:T(8,128)(2,1)S(1)}, bf16[4,16,32,256]{3,2,1,0:T(8,128)(2,1)}, u32[]{:S(2)}, u32[]{:S(2)}) collective-permute-start(bf16[4,16,32,256]{3,2,1,0:T(8,128)(2,1)S(1)} %all-to-all-done.wa_ref.refs_2_), channel_id=1, source_target_pairs={{0,16},{16,0},{32,48},{48,32},{64,80},{80,64},{96,112},{112,96},{1... | collective-permute-start | bytes 3145736 | tf_op jit(solution)/shard_map/ppermute | solution.py:292
  66.8 23.7 %copy-start.6 = (s32[1,2048]{1,0:T(1,128)S(1)}, s32[1,2048]{1,0:T(1,128)}, u32[]{:S(2)}) copy-start(s32[1,2048]{1,0:T(1,128)} %param.11) | copy-start | bytes 24580
  72.1 16.5 %collective-permute-start.2 = (bf16[512,256]{1,0:T(8,128)(2,1)}, bf16[512,256]{1,0:T(8,128)(2,1)S(1)}, u32[]{:S(2)}, u32[]{:S(2)}) collective-permute-start(bf16[512,256]{1,0:T(8,128)(2,1)} %shard_map.65.kv0_ref), channel_id=1, source_target_pairs={{0,1},{1,2},{2,3},{4,5},{5,6},{6,7},{8,9},{9,10},{10,11},{12,13},{... | collective-permute-start | bytes 786440 | tf_op jit(solution)/shard_map/ppermute | solution.py:317
  75.1 13.4 %collective-permute-start.1 = (bf16[512,256]{1,0:T(8,128)(2,1)}, bf16[512,256]{1,0:T(8,128)(2,1)S(1)}, u32[]{:S(2)}, u32[]{:S(2)}) collective-permute-start(bf16[512,256]{1,0:T(8,128)(2,1)} %shard_map.65.kv0_ref), channel_id=1, source_target_pairs={{0,2},{1,3},{4,6},{5,7},{8,10},{9,11},{12,14},{13,15},{16,18},{17,... | collective-permute-start | bytes 786440 | tf_op jit(solution)/shard_map/ppermute | solution.py:318
  88.5 6.2 %copy-start.2 = (bf16[512,256]{1,0:T(8,128)(2,1)}, bf16[512,256]{1,0:T(8,128)(2,1)S(1)}, u32[]{:S(2)}) copy-start(bf16[512,256]{1,0:T(8,128)(2,1)S(1)} %collective-permute-done.2.refs_1_.kv1_ref) | copy-start | bytes 786436
  88.6 6.2 %copy-start.3 = (bf16[512,256]{1,0:T(8,128)(2,1)}, bf16[512,256]{1,0:T(8,128)(2,1)S(1)}, u32[]{:S(2)}) copy-start(bf16[512,256]{1,0:T(8,128)(2,1)S(1)} %collective-permute-done.1.refs_2_.kv2_ref) | copy-start | bytes 786436
  88.6 6.2 %copy-start.1 = (bf16[4,16,32,512]{3,2,1,0:T(8,128)(2,1)}, bf16[4,16,32,512]{3,2,1,0:T(8,128)(2,1)S(1)}, u32[]{:S(2)}) copy-start(bf16[4,16,32,512]{3,2,1,0:T(8,128)(2,1)S(1)} %shard_map.68.wa_ref) | copy-start | bytes 6291460
  88.6 6.2 %collective-permute-start.3 = (bf16[4,16,32,512]{3,2,1,0:T(8,128)(2,1)S(1)}, bf16[4,16,32,512]{3,2,1,0:T(8,128)(2,1)}, u32[]{:S(2)}, u32[]{:S(2)}) collective-permute-start(bf16[4,16,32,512]{3,2,1,0:T(8,128)(2,1)S(1)} %shard_map.68.wa_ref), channel_id=1, source_target_pairs={{0,16},{16,0},{32,48},{48,32},{64,80},{80,64},{96,112},{112,96},{1... | collective-permute-start | bytes 6291464 | tf_op jit(solution)/shard_map/ppermute | solution.py:292
  91.1 3.6 %copy-start.8 = (s32[4,128]{1,0:T(4,128)}, s32[4,128]{1,0:T(4,128)S(1)}, u32[]{:S(2)}) copy-start(s32[4,128]{1,0:T(4,128)S(1)} %maximum_bitcast_fusion.low_ref) | copy-start | bytes 6148

commit v10 on v9

--- a/solution.py
+++ b/solution.py
@@ -154,8 +154,6 @@
         lanes = slice(h * HEAD_SIZE, (h + 1) * HEAD_SIZE)
         q[h] = rotate(sums[:, lanes], cos[...], sin[...]).T.astype(jnp.bfloat16)
 
-    key_lane = lax.broadcasted_iota(jnp.int32, (KEY_BLOCK, QUERY_BLOCK), 0)
-    query_lane = lax.broadcasted_iota(jnp.int32, (KEY_BLOCK, QUERY_BLOCK), 1)
     to_log2 = math.log2(math.e) / math.sqrt(HEAD_SIZE)
     for step in range(rows // QUERY_BLOCK):
         block = slice(step * QUERY_BLOCK, (step + 1) * QUERY_BLOCK)
@@ -166,13 +164,14 @@
         first_query = 2 * rows + step * QUERY_BLOCK
         acc[...] = jnp.zeros_like(acc)
 
-        def visit(n, carry):
+        def visit(start, size, carry):
             run_max, run_sum = carry
-            start = pl.multiple_of(n * KEY_BLOCK, KEY_BLOCK)
             scores = jnp.dot(
-                keys[pl.ds(start, KEY_BLOCK)], queries, preferred_element_type=jnp.float32
+                keys[pl.ds(start, size)], queries, preferred_element_type=jnp.float32
             )
-            visible = (start + key_lane >= low) & (start + key_lane <= first_query + query_lane)
+            key_at = start + lax.broadcasted_iota(jnp.int32, (size, QUERY_BLOCK), 0)
+            query_at = first_query + lax.broadcasted_iota(jnp.int32, (size, QUERY_BLOCK), 1)
+            visible = (key_at >= low) & (key_at <= query_at)
             visible = jnp.concatenate([visible] * heads, axis=1)
             scores = jnp.where(visible, scores, -1e30)
             new_max = jnp.maximum(run_max, jnp.max(scores, axis=0, keepdims=True))
@@ -180,18 +179,21 @@
             weights = jnp.exp2((scores - new_max) * to_log2)
             run_sum = run_sum * factor + jnp.sum(weights, axis=0, keepdims=True)
             acc[...] = acc[...] * factor + jnp.dot(
-                values[:, pl.ds(start, KEY_BLOCK)],
+                values[:, pl.ds(start, size)],
                 weights.astype(jnp.bfloat16),
                 preferred_element_type=jnp.float32,
             )
             return new_max, run_sum
 
+        def visit_earlier(n, carry):
+            return visit(pl.multiple_of(n * KEY_BLOCK, KEY_BLOCK), KEY_BLOCK, carry)
+
         initial = (
             jnp.full((1, width), -1e30, jnp.float32),
             jnp.zeros((1, width), jnp.float32),
         )
-        last = (first_query + QUERY_BLOCK - 1) // KEY_BLOCK + 1
-        _, run_sum = lax.fori_loop(first_ref[step], last, visit, initial)
+        carry = lax.fori_loop(first_ref[step], 2 * rows // KEY_BLOCK, visit_earlier, initial)
+        _, run_sum = visit(2 * rows, (step + 1) * QUERY_BLOCK, carry)
         mixed = acc[...] / run_sum
         for h in range(heads):
             lanes = slice(h * HEAD_SIZE, (h + 1) * HEAD_SIZE)

time: 108 us -> 108 us (level)
  the two profiles are of different devices: /device:TPU:22 before, /device:TPU:17 now
where the time goes in v10:
time: 108 us; the launch traced here: 107 us
  blocking collectives  33.1 us (31%)
  starting transfers between devices  28.6 us (26%)
  Pallas kernels  19.8 us (18%)
  waiting for transfers between devices  14 us (13%)
  other arithmetic  9.36 us (9%)
  local copies, waits for them, and re-layouts  2.1 us (2%)
    all_gather x1, blocking collectives, gather_column(): lax.all_gather(own, 'rows', axis=0, tiled=False, axis_index_groups=same_c...  33.1 us
    ppermute x2, starting transfers between devices, swap_cores(): lax.ppermute(half, 'rows', [(i, i ^ 1) for i in range(lax.axis_size('rows...  15.6 us
    pallas_call x1, Pallas kernels, attend(): pl.pallas_call(attend_kernel, in_specs=[pl.BlockSpec(memory_space=pltpu.S...  12 us
    all_to_all x2, starting transfers between devices, exchange_attn(): return lax.all_to_all(copies, 'attn', 0, 0, tiled=True)  8.93 us
    ppermute x1, waiting for transfers between devices, on_device(): kv1 = lax.ppermute(kv, 'attn', [(0, 1), (1, 2), (2, 3)])  7.18 us
    pallas_call x1, Pallas kernels, project_kv(): pl.pallas_call(kv_kernel, in_specs=[pl.BlockSpec(memory_space=pltpu.SMEM)...  5.27 us
    ppermute x1, waiting for transfers between devices, on_device(): kv2 = lax.ppermute(kv, 'attn', [(0, 2), (1, 3)])  4 us
    reduce_sum x1, other arithmetic, normalize(): mean_sq = jnp.mean(widened * widened, axis=-1, keepdims=True)  3.63 us
  transfers between devices with their start and end apart: 6, of which 4 were waited for; matrix products, arithmetic and copies ran while one was open for 8% of the time, Pallas kernels for 6%

profile of v10, /device:TPU:17, one launch (start us, length us, event | category | flops | bytes accessed | tf_op | source)
XLA Modules:
  0.0 107.1 jit_solution(7564773891167159827)
XLA Ops:
  0.0 0.8 fusion.5
  0.8 33.1 %all-gather = bf16[512,768]{1,0:T(8,128)(2,1)S(1)} all-gather(bf16[32,768]{1,0:T(8,128)(2,1)S(1)} %fusion.5), channel_id=2, replica_groups={{0,32,64,96,128,160,192,224,256,288,320,352,384,416,448,480},{16,48,80,..., dimensions={0}, use_global_device_ids=true | all-gather | bytes 835584 | tf_op jit(solution)/shard_map/all_gather | solution.py:249
  33.9 1.1 shard_map.64
  34.9 0.0 copy-start.7
  34.9 4.4 %all-to-all-start = ((bf16[4,16,32,256]{3,2,1,0:T(8,128)(2,1)}), bf16[4,16,32,256]{3,2,1,0:T(8,128)(2,1)S(1)}, u32[]{:S(2)}, u32[]{:S(2)}) async-start(bf16[4,16,32,256]{3,2,1,0:T(8,128)(2,1)} %shard_map.64), calls=%async_computation | async-start | bytes 2097152 | tf_op jit(solution)/shard_map/all_to_all | solution.py:290
  39.3 0.0 copy-start.5
  39.3 1.5 %shard_map.66.refs_0_ = bf16[4,16,32,512]{3,2,1,0:T(8,128)(2,1)} custom-call(bf16[16,32,768]{2,1,0:T(8,128)(2,1)S(1)} %bitcast.7), custom_call_target="tpu_custom_call" | custom-call | bytes 3145728 | tf_op jit(solution)/shard_map/pallas_call | solution.py:278
  40.8 3.6 %fusion = f32[512]{0:T(512)S(1)} fusion(bf16[512,4096]{1,0:T(8,128)(2,1)} %param.6), kind=kLoop, calls=%fused_computation.2 | loop fusion | flops 6290944 | bytes 4196352 | tf_op jit(solution)/shard_map/reduce_sum | solution.py:238
  44.4 0.0 copy-done.7
  44.4 0.0 copy-done.5
  44.4 1.7 %fusion.2.x_ref = bf16[512,4096]{1,0:T(8,128)(2,1)S(1)} fusion(bf16[512,4096]{1,0:T(8,128)(2,1)S(1)} %copy-done.5, f32[4096]{0:T(1024)S(1)} %convert_element_type.21, f32[512]{0:T(512)S(1)} %add_rsqrt_fusion), kind=kLoop, calls=%fused_computation.4 | loop fusion | flops 8388608 | bytes 8407040 | tf_op jit(solution)/shard_map/convert_element_type | solution.py:239
  46.1 0.0 copy-start.4
  46.1 1.9 %copy-done.4 = bf16[512,4096]{1,0:T(8,128)(2,1)} copy-done((bf16[512,4096]{1,0:T(8,128)(2,1)}, bf16[512,4096]{1,0:T(8,128)(2,1)S(1)}, u32[]{:S(2)}) %copy-start.4) | copy-done | bytes 4194328
  48.0 0.0 all-to-all-done.wa_ref.refs_2_
  48.0 0.0 copy-start
  48.1 4.6 %all-to-all-start.1 = ((bf16[4,16,32,512]{3,2,1,0:T(8,128)(2,1)}), bf16[4,16,32,512]{3,2,1,0:T(8,128)(2,1)S(1)}, u32[]{:S(2)}, u32[]{:S(2)}) async-start(bf16[4,16,32,512]{3,2,1,0:T(8,128)(2,1)} %shard_map.67), calls=%async_computation.1 | async-start | bytes 4194304 | tf_op jit(solution)/shard_map/all_to_all | solution.py:290
  52.6 0.0 copy-done
  52.6 12.0 %collective-permute-start = (bf16[4,16,32,256]{3,2,1,0:T(8,128)(2,1)S(1)}, bf16[4,16,32,256]{3,2,1,0:T(8,128)(2,1)}, u32[]{:S(2)}, u32[]{:S(2)}) collective-permute-start(bf16[4,16,32,256]{3,2,1,0:T(8,128)(2,1)S(1)} %all-to-all-done.wa_ref.refs_2_), channel_id=1, source_target_pairs={{0,16},{16,0},{32,48},{48,32},{64,80},{80,64},{96,112},{112,96},{1... | collective-permute-start | bytes 3145736 | tf_op jit(solution)/shard_map/ppermute | solution.py:294
  64.7 1.0 fusion.3
  65.7 1.1 pad_maximum_fusion
  66.8 0.3 collective-permute-done.wb_ref
  67.1 0.0 copy-start.6
  67.1 5.3 %shard_map.65.kv0_ref = bf16[512,256]{1,0:T(8,128)(2,1)} custom-call(s32[1]{0:T(128)} %bitcast.core_ref, bf16[512,4096]{1,0:T(8,128)(2,1)} %copy-done.4, bf16[4,16,32,256]{3,2,1,0:T(8,128)(2,1)} %copy-done, bf16[4,16,32,256]{3,2,1,0:T(8,128)(2,1)} %collective-permute-done.wb_ref, f32[512,128]{1,0:T(8,128)} %get-tuple-element.8.cos_ref, ...), custom_call_target="tpu_custom_call" | custom-call | flops 1073741824 | bytes 6553600 | tf_op jit(solution)/shard_map/pallas_call | solution.py:80
  72.4 2.8 %collective-permute-start.2 = (bf16[512,256]{1,0:T(8,128)(2,1)}, bf16[512,256]{1,0:T(8,128)(2,1)S(1)}, u32[]{:S(2)}, u32[]{:S(2)}) collective-permute-start(bf16[512,256]{1,0:T(8,128)(2,1)} %shard_map.65.kv0_ref), channel_id=1, source_target_pairs={{0,1},{1,2},{2,3},{4,5},{5,6},{6,7},{8,9},{9,10},{10,11},{12,13},{... | collective-permute-start | bytes 786440 | tf_op jit(solution)/shard_map/ppermute | solution.py:319
  75.2 1.3 %collective-permute-start.1 = (bf16[512,256]{1,0:T(8,128)(2,1)}, bf16[512,256]{1,0:T(8,128)(2,1)S(1)}, u32[]{:S(2)}, u32[]{:S(2)}) collective-permute-start(bf16[512,256]{1,0:T(8,128)(2,1)} %shard_map.65.kv0_ref), channel_id=1, source_target_pairs={{0,2},{1,3},{4,6},{5,7},{8,10},{9,11},{12,14},{13,15},{16,18},{17,... | collective-permute-start | bytes 786440 | tf_op jit(solution)/shard_map/ppermute | solution.py:320
  76.5 7.2 %collective-permute-done.2.refs_1_.kv1_ref = bf16[512,256]{1,0:T(8,128)(2,1)S(1)} collective-permute-done((bf16[512,256]{1,0:T(8,128)(2,1)}, bf16[512,256]{1,0:T(8,128)(2,1)S(1)}, u32[]{:S(2)}, u32[]{:S(2)}) %collective-permute-start.2) | collective-permute-done | bytes 262176 | tf_op jit(solution)/shard_map/ppermute | solution.py:319
  83.6 0.0 copy-start.2
  83.6 4.0 %collective-permute-done.1.refs_2_.kv2_ref = bf16[512,256]{1,0:T(8,128)(2,1)S(1)} collective-permute-done((bf16[512,256]{1,0:T(8,128)(2,1)}, bf16[512,256]{1,0:T(8,128)(2,1)S(1)}, u32[]{:S(2)}, u32[]{:S(2)}) %collective-permute-start.1) | collective-permute-done | bytes 262176 | tf_op jit(solution)/shard_map/ppermute | solution.py:320
  87.6 0.0 copy-start.3
  87.6 0.0 all-to-all-done.1.refs_0_
  87.6 0.0 copy-start.1
  87.6 3.5 %collective-permute-start.3 = (bf16[4,16,32,512]{3,2,1,0:T(8,128)(2,1)S(1)}, bf16[4,16,32,512]{3,2,1,0:T(8,128)(2,1)}, u32[]{:S(2)}, u32[]{:S(2)}) collective-permute-start(bf16[4,16,32,512]{3,2,1,0:T(8,128)(2,1)S(1)} %shard_map.68.wa_ref), channel_id=1, source_target_pairs={{0,16},{16,0},{32,48},{48,32},{64,80},{80,64},{96,112},{112,96},{1... | collective-permute-start | bytes 6291464 | tf_op jit(solution)/shard_map/ppermute | solution.py:294
  91.2 0.0 copy-done.6
  91.2 0.6 convert_reduce_fusion
  91.8 0.0 copy-start.8
  91.8 0.1 slice_reduce_fusion
  91.9 0.6 and_select_fusion.first_ref
  92.5 2.5 %collective-permute-done.3.wb_ref = bf16[4,16,32,512]{3,2,1,0:T(8,128)(2,1)} collective-permute-done((bf16[4,16,32,512]{3,2,1,0:T(8,128)(2,1)S(1)}, bf16[4,16,32,512]{3,2,1,0:T(8,128)(2,1)}, u32[]{:S(2)}, u32[]{:S(2)}) %collective-permute-start.3) | collective-permute-done | bytes 2097184 | tf_op jit(solution)/shard_map/ppermute | solution.py:294
  95.1 0.0 copy-done.2
  95.1 0.0 copy-done.3
  95.1 0.0 copy-done.1
  95.1 0.0 copy-done.8
  95.1 12.0 %shard_map.69 = bf16[512,512]{1,0:T(8,128)(2,1)} custom-call(s32[1]{0:T(128)} %bitcast.core_ref, s32[4]{0:T(128)} %and_select_fusion.first_ref, s32[4,128]{1,0:T(4,128)} %copy-done.8, bf16[512,4096]{1,0:T(8,128)(2,1)} %copy-done.4, f32[512,128]{1,0:T(8,128)} %get-tuple-element.8.cos_ref, f32[512,128]{1,0:T(8,128)} %get-tuple-element.9.sin_ref, ...), custom_call_target="tpu_custom_call" | custom-call | flops 3221225472 | bytes 8388608 | tf_op jit(solution)/shard_map/pallas_call | solution.py:207
  (9 shorter events, 0.0 us)
Async XLA Ops:
  34.9 9.5 %copy-start.7 = (bf16[4096]{0:T(1024)(128)(2,1)S(1)}, bf16[4096]{0:T(1024)(128)(2,1)}, u32[]{:S(2)}) copy-start(bf16[4096]{0:T(1024)(128)(2,1)} %param.7) | copy-start | bytes 24580
  34.9 13.1 %all-to-all-start = ((bf16[4,16,32,256]{3,2,1,0:T(8,128)(2,1)}), bf16[4,16,32,256]{3,2,1,0:T(8,128)(2,1)S(1)}, u32[]{:S(2)}, u32[]{:S(2)}) async-start(bf16[4,16,32,256]{3,2,1,0:T(8,128)(2,1)} %shard_map.64), calls=%async_computation | async-start | bytes 2097152 | tf_op jit(solution)/shard_map/all_to_all | solution.py:290
  39.3 5.1 %copy-start.5 = (bf16[512,4096]{1,0:T(8,128)(2,1)S(1)}, bf16[512,4096]{1,0:T(8,128)(2,1)}, u32[]{:S(2)}) copy-start(bf16[512,4096]{1,0:T(8,128)(2,1)} %param.6) | copy-start | bytes 12582916
  46.1 1.9 %copy-start.4 = (bf16[512,4096]{1,0:T(8,128)(2,1)}, bf16[512,4096]{1,0:T(8,128)(2,1)S(1)}, u32[]{:S(2)}) copy-start(bf16[512,4096]{1,0:T(8,128)(2,1)S(1)} %fusion.2.x_ref) | copy-start | bytes 12582916
  48.0 4.6 %copy-start = (bf16[4,16,32,256]{3,2,1,0:T(8,128)(2,1)}, bf16[4,16,32,256]{3,2,1,0:T(8,128)(2,1)S(1)}, u32[]{:S(2)}) copy-start(bf16[4,16,32,256]{3,2,1,0:T(8,128)(2,1)S(1)} %all-to-all-done.wa_ref.refs_2_) | copy-start | bytes 3145732
  48.1 39.6 %all-to-all-start.1 = ((bf16[4,16,32,512]{3,2,1,0:T(8,128)(2,1)}), bf16[4,16,32,512]{3,2,1,0:T(8,128)(2,1)S(1)}, u32[]{:S(2)}, u32[]{:S(2)}) async-start(bf16[4,16,32,512]{3,2,1,0:T(8,128)(2,1)} %shard_map.67), calls=%async_computation.1 | async-start | bytes 4194304 | tf_op jit(solution)/shard_map/all_to_all | solution.py:290
  52.6 14.4 %collective-permute-start = (bf16[4,16,32,256]{3,2,1,0:T(8,128)(2,1)S(1)}, bf16[4,16,32,256]{3,2,1,0:T(8,128)(2,1)}, u32[]{:S(2)}, u32[]{:S(2)}) collective-permute-start(bf16[4,16,32,256]{3,2,1,0:T(8,128)(2,1)S(1)} %all-to-all-done.wa_ref.refs_2_), channel_id=1, source_target_pairs={{0,16},{16,0},{32,48},{48,32},{64,80},{80,64},{96,112},{112,96},{1... | collective-permute-start | bytes 3145736 | tf_op jit(solution)/shard_map/ppermute | solution.py:294
  67.1 24.1 %copy-start.6 = (s32[1,2048]{1,0:T(1,128)S(1)}, s32[1,2048]{1,0:T(1,128)}, u32[]{:S(2)}) copy-start(s32[1,2048]{1,0:T(1,128)} %param.11) | copy-start | bytes 24580
  72.4 11.3 %collective-permute-start.2 = (bf16[512,256]{1,0:T(8,128)(2,1)}, bf16[512,256]{1,0:T(8,128)(2,1)S(1)}, u32[]{:S(2)}, u32[]{:S(2)}) collective-permute-start(bf16[512,256]{1,0:T(8,128)(2,1)} %shard_map.65.kv0_ref), channel_id=1, source_target_pairs={{0,1},{1,2},{2,3},{4,5},{5,6},{6,7},{8,9},{9,10},{10,11},{12,13},{... | collective-permute-start | bytes 786440 | tf_op jit(solution)/shard_map/ppermute | solution.py:319
  75.2 12.5 %collective-permute-start.1 = (bf16[512,256]{1,0:T(8,128)(2,1)}, bf16[512,256]{1,0:T(8,128)(2,1)S(1)}, u32[]{:S(2)}, u32[]{:S(2)}) collective-permute-start(bf16[512,256]{1,0:T(8,128)(2,1)} %shard_map.65.kv0_ref), channel_id=1, source_target_pairs={{0,2},{1,3},{4,6},{5,7},{8,10},{9,11},{12,14},{13,15},{16,18},{17,... | collective-permute-start | bytes 786440 | tf_op jit(solution)/shard_map/ppermute | solution.py:320
  83.6 11.4 %copy-start.2 = (bf16[512,256]{1,0:T(8,128)(2,1)}, bf16[512,256]{1,0:T(8,128)(2,1)S(1)}, u32[]{:S(2)}) copy-start(bf16[512,256]{1,0:T(8,128)(2,1)S(1)} %collective-permute-done.2.refs_1_.kv1_ref) | copy-start | bytes 786436
  87.6 7.4 %copy-start.3 = (bf16[512,256]{1,0:T(8,128)(2,1)}, bf16[512,256]{1,0:T(8,128)(2,1)S(1)}, u32[]{:S(2)}) copy-start(bf16[512,256]{1,0:T(8,128)(2,1)S(1)} %collective-permute-done.1.refs_2_.kv2_ref) | copy-start | bytes 786436
  87.6 7.4 %copy-start.1 = (bf16[4,16,32,512]{3,2,1,0:T(8,128)(2,1)}, bf16[4,16,32,512]{3,2,1,0:T(8,128)(2,1)S(1)}, u32[]{:S(2)}) copy-start(bf16[4,16,32,512]{3,2,1,0:T(8,128)(2,1)S(1)} %shard_map.68.wa_ref) | copy-start | bytes 6291460
  87.6 7.4 %collective-permute-start.3 = (bf16[4,16,32,512]{3,2,1,0:T(8,128)(2,1)S(1)}, bf16[4,16,32,512]{3,2,1,0:T(8,128)(2,1)}, u32[]{:S(2)}, u32[]{:S(2)}) collective-permute-start(bf16[4,16,32,512]{3,2,1,0:T(8,128)(2,1)S(1)} %shard_map.68.wa_ref), channel_id=1, source_target_pairs={{0,16},{16,0},{32,48},{48,32},{64,80},{80,64},{96,112},{112,96},{1... | collective-permute-start | bytes 6291464 | tf_op jit(solution)/shard_map/ppermute | solution.py:294
  91.8 3.3 %copy-start.8 = (s32[4,128]{1,0:T(4,128)}, s32[4,128]{1,0:T(4,128)S(1)}, u32[]{:S(2)}) copy-start(s32[4,128]{1,0:T(4,128)S(1)} %maximum_bitcast_fusion.low_ref) | copy-start | bytes 6148

commit v11 on v10

--- a/solution.py
+++ b/solution.py
@@ -192,7 +192,14 @@
             jnp.full((1, width), -1e30, jnp.float32),
             jnp.zeros((1, width), jnp.float32),
         )
-        carry = lax.fori_loop(first_ref[step], 2 * rows // KEY_BLOCK, visit_earlier, initial)
+        half = KEY_BLOCK // 2
+        first = jnp.minimum(first_ref[step], 2 * rows // half)
+
+        def visit_half(n, carry):
+            return visit(pl.multiple_of((first + n) * half, half), half, carry)
+
+        carry = lax.fori_loop(0, first % 2, visit_half, initial)
+        carry = lax.fori_loop((first + 1) // 2, 2 * rows // KEY_BLOCK, visit_earlier, carry)
         _, run_sum = visit(2 * rows, (step + 1) * QUERY_BLOCK, carry)
         mixed = acc[...] / run_sum
         for h in range(heads):
@@ -312,7 +319,7 @@
     my_docs = lax.dynamic_slice_in_dim(doc_ids, me * rows, rows)
     begin = jnp.sum((doc_ids[None, :] < my_docs[:, None]).astype(jnp.int32), axis=1)
     low = jnp.maximum(begin - (me - 2) * rows, 0).reshape(-1, QUERY_BLOCK)
-    first = low[:, 0] // KEY_BLOCK
+    first = low[:, 0] // (KEY_BLOCK // 2)
 
     core = (lax.axis_index("rows") % 2).astype(jnp.int32).reshape(1)
     kv = project_kv(core, normed, kv_half, swap_cores(kv_half), cosine, sine)

time: 108 us -> 107 us (level)
  the two profiles are of different devices: /device:TPU:17 before, /device:TPU:9 now
where the time goes in v11:
time: 107 us; the launch traced here: 106 us
  starting transfers between devices  33.4 us (31%)
  blocking collectives  33.1 us (31%)
  Pallas kernels  19.1 us (18%)
  other arithmetic  9.36 us (9%)
  waiting for transfers between devices  8.45 us (8%)
  local copies, waits for them, and re-layouts  2.1 us (2%)
    all_gather x1, blocking collectives, gather_column(): lax.all_gather(own, 'rows', axis=0, tiled=False, axis_index_groups=same_c...  33.1 us
    ppermute x2, starting transfers between devices, swap_cores(): lax.ppermute(half, 'rows', [(i, i ^ 1) for i in range(lax.axis_size('rows...  19.3 us
    pallas_call x1, Pallas kernels, attend(): pl.pallas_call(attend_kernel, in_specs=[pl.BlockSpec(memory_space=pltpu.S...  11.3 us
    all_to_all x2, starting transfers between devices, exchange_attn(): return lax.all_to_all(copies, 'attn', 0, 0, tiled=True)  9.04 us
    pallas_call x1, Pallas kernels, project_kv(): pl.pallas_call(kv_kernel, in_specs=[pl.BlockSpec(memory_space=pltpu.SMEM)...  5.27 us
    ppermute x1, waiting for transfers between devices, on_device(): kv1 = lax.ppermute(kv, 'attn', [(0, 1), (1, 2), (2, 3)])  4.89 us
    reduce_sum x1, other arithmetic, normalize(): mean_sq = jnp.mean(widened * widened, axis=-1, keepdims=True)  3.63 us
    ppermute x1, starting transfers between devices, on_device(): kv1 = lax.ppermute(kv, 'attn', [(0, 1), (1, 2), (2, 3)])  3.09 us
  transfers between devices with their start and end apart: 6, of which 4 were waited for; matrix products, arithmetic and copies ran while one was open for 8% of the time, Pallas kernels for 6%

profile of v11, /device:TPU:9, one launch (start us, length us, event | category | flops | bytes accessed | tf_op | source)
XLA Modules:
  0.0 105.6 jit_solution(1846591177100769381)
XLA Ops:
  0.0 0.8 fusion.5
  0.8 33.1 %all-gather = bf16[512,768]{1,0:T(8,128)(2,1)S(1)} all-gather(bf16[32,768]{1,0:T(8,128)(2,1)S(1)} %fusion.5), channel_id=2, replica_groups={{0,32,64,96,128,160,192,224,256,288,320,352,384,416,448,480},{16,48,80,..., dimensions={0}, use_global_device_ids=true | all-gather | bytes 835584 | tf_op jit(solution)/shard_map/all_gather | solution.py:256
  33.9 1.1 %shard_map.64 = bf16[4,16,32,256]{3,2,1,0:T(8,128)(2,1)} custom-call(bf16[16,32,768]{2,1,0:T(8,128)(2,1)S(1)} %bitcast.6), custom_call_target="tpu_custom_call" | custom-call | bytes 1572864 | tf_op jit(solution)/shard_map/pallas_call | solution.py:285
  34.9 0.0 copy-start.7
  34.9 4.5 %all-to-all-start = ((bf16[4,16,32,256]{3,2,1,0:T(8,128)(2,1)}), bf16[4,16,32,256]{3,2,1,0:T(8,128)(2,1)S(1)}, u32[]{:S(2)}, u32[]{:S(2)}) async-start(bf16[4,16,32,256]{3,2,1,0:T(8,128)(2,1)} %shard_map.64), calls=%async_computation | async-start | bytes 2097152 | tf_op jit(solution)/shard_map/all_to_all | solution.py:297
  39.4 0.0 copy-start.5
  39.4 1.5 %shard_map.66.refs_0_ = bf16[4,16,32,512]{3,2,1,0:T(8,128)(2,1)} custom-call(bf16[16,32,768]{2,1,0:T(8,128)(2,1)S(1)} %bitcast.7), custom_call_target="tpu_custom_call" | custom-call | bytes 3145728 | tf_op jit(solution)/shard_map/pallas_call | solution.py:285
  40.9 3.6 %fusion = f32[512]{0:T(512)S(1)} fusion(bf16[512,4096]{1,0:T(8,128)(2,1)} %param.6), kind=kLoop, calls=%fused_computation.2 | loop fusion | flops 6290944 | bytes 4196352 | tf_op jit(solution)/shard_map/reduce_sum | solution.py:245
  44.5 0.0 copy-done.7
  44.5 0.0 copy-done.5
  44.5 1.7 %fusion.2.x_ref = bf16[512,4096]{1,0:T(8,128)(2,1)S(1)} fusion(bf16[512,4096]{1,0:T(8,128)(2,1)S(1)} %copy-done.5, f32[4096]{0:T(1024)S(1)} %convert_element_type.21, f32[512]{0:T(512)S(1)} %add_rsqrt_fusion), kind=kLoop, calls=%fused_computation.4 | loop fusion | flops 8388608 | bytes 8407040 | tf_op jit(solution)/shard_map/convert_element_type | solution.py:246
  46.2 0.0 copy-start.4
  46.2 1.9 %copy-done.4 = bf16[512,4096]{1,0:T(8,128)(2,1)} copy-done((bf16[512,4096]{1,0:T(8,128)(2,1)}, bf16[512,4096]{1,0:T(8,128)(2,1)S(1)}, u32[]{:S(2)}) %copy-start.4) | copy-done | bytes 4194328
  48.2 0.0 all-to-all-done.wa_ref.refs_2_
  48.2 0.0 copy-start
  48.2 4.6 %all-to-all-start.1 = ((bf16[4,16,32,512]{3,2,1,0:T(8,128)(2,1)}), bf16[4,16,32,512]{3,2,1,0:T(8,128)(2,1)S(1)}, u32[]{:S(2)}, u32[]{:S(2)}) async-start(bf16[4,16,32,512]{3,2,1,0:T(8,128)(2,1)} %shard_map.67), calls=%async_computation.1 | async-start | bytes 4194304 | tf_op jit(solution)/shard_map/all_to_all | solution.py:297
  52.7 0.0 copy-done
  52.7 12.0 %collective-permute-start = (bf16[4,16,32,256]{3,2,1,0:T(8,128)(2,1)S(1)}, bf16[4,16,32,256]{3,2,1,0:T(8,128)(2,1)}, u32[]{:S(2)}, u32[]{:S(2)}) collective-permute-start(bf16[4,16,32,256]{3,2,1,0:T(8,128)(2,1)S(1)} %all-to-all-done.wa_ref.refs_2_), channel_id=1, source_target_pairs={{0,16},{16,0},{32,48},{48,32},{64,80},{80,64},{96,112},{112,96},{1... | collective-permute-start | bytes 3145736 | tf_op jit(solution)/shard_map/ppermute | solution.py:301
  64.8 1.0 fusion.3
  65.8 1.1 pad_maximum_fusion
  66.9 0.3 collective-permute-done.wb_ref
  67.2 0.0 copy-start.6
  67.2 5.3 %shard_map.65.kv0_ref = bf16[512,256]{1,0:T(8,128)(2,1)} custom-call(s32[1]{0:T(128)} %bitcast.core_ref, bf16[512,4096]{1,0:T(8,128)(2,1)} %copy-done.4, bf16[4,16,32,256]{3,2,1,0:T(8,128)(2,1)} %copy-done, bf16[4,16,32,256]{3,2,1,0:T(8,128)(2,1)} %collective-permute-done.wb_ref, f32[512,128]{1,0:T(8,128)} %get-tuple-element.8.cos_ref, ...), custom_call_target="tpu_custom_call" | custom-call | flops 1073741824 | bytes 6553600 | tf_op jit(solution)/shard_map/pallas_call | solution.py:80
  72.5 3.1 %collective-permute-start.2 = (bf16[512,256]{1,0:T(8,128)(2,1)}, bf16[512,256]{1,0:T(8,128)(2,1)S(1)}, u32[]{:S(2)}, u32[]{:S(2)}) collective-permute-start(bf16[512,256]{1,0:T(8,128)(2,1)} %shard_map.65.kv0_ref), channel_id=1, source_target_pairs={{0,1},{1,2},{2,3},{4,5},{5,6},{6,7},{8,9},{9,10},{10,11},{12,13},{... | collective-permute-start | bytes 786440 | tf_op jit(solution)/shard_map/ppermute | solution.py:326
  75.6 1.9 %collective-permute-start.1 = (bf16[512,256]{1,0:T(8,128)(2,1)}, bf16[512,256]{1,0:T(8,128)(2,1)S(1)}, u32[]{:S(2)}, u32[]{:S(2)}) collective-permute-start(bf16[512,256]{1,0:T(8,128)(2,1)} %shard_map.65.kv0_ref), channel_id=1, source_target_pairs={{0,2},{1,3},{4,6},{5,7},{8,10},{9,11},{12,14},{13,15},{16,18},{17,... | collective-permute-start | bytes 786440 | tf_op jit(solution)/shard_map/ppermute | solution.py:327
  77.5 4.9 %collective-permute-done.2.refs_1_.kv1_ref = bf16[512,256]{1,0:T(8,128)(2,1)S(1)} collective-permute-done((bf16[512,256]{1,0:T(8,128)(2,1)}, bf16[512,256]{1,0:T(8,128)(2,1)S(1)}, u32[]{:S(2)}, u32[]{:S(2)}) %collective-permute-start.2) | collective-permute-done | bytes 262176 | tf_op jit(solution)/shard_map/ppermute | solution.py:326
  82.4 0.0 copy-start.2
  82.4 0.7 collective-permute-done.1.refs_2_.kv2_ref
  83.1 0.0 copy-start.3
  83.1 0.0 all-to-all-done.1.refs_0_
  83.1 0.0 copy-start.1
  83.1 7.3 %collective-permute-start.3 = (bf16[4,16,32,512]{3,2,1,0:T(8,128)(2,1)S(1)}, bf16[4,16,32,512]{3,2,1,0:T(8,128)(2,1)}, u32[]{:S(2)}, u32[]{:S(2)}) collective-permute-start(bf16[4,16,32,512]{3,2,1,0:T(8,128)(2,1)S(1)} %shard_map.68.wa_ref), channel_id=1, source_target_pairs={{0,16},{16,0},{32,48},{48,32},{64,80},{80,64},{96,112},{112,96},{1... | collective-permute-start | bytes 6291464 | tf_op jit(solution)/shard_map/ppermute | solution.py:301
  90.4 0.0 copy-done.6
  90.4 0.6 convert_reduce_fusion
  91.0 0.0 copy-start.8
  91.0 0.1 slice_reduce_fusion
  91.2 0.6 and_select_fusion.first_ref
  91.8 2.5 %collective-permute-done.3.wb_ref = bf16[4,16,32,512]{3,2,1,0:T(8,128)(2,1)} collective-permute-done((bf16[4,16,32,512]{3,2,1,0:T(8,128)(2,1)S(1)}, bf16[4,16,32,512]{3,2,1,0:T(8,128)(2,1)}, u32[]{:S(2)}, u32[]{:S(2)}) %collective-permute-start.3) | collective-permute-done | bytes 2097184 | tf_op jit(solution)/shard_map/ppermute | solution.py:301
  94.3 0.0 copy-done.2
  94.3 0.0 copy-done.3
  94.3 0.0 copy-done.1
  94.3 0.0 copy-done.8
  94.3 11.3 %shard_map.69 = bf16[512,512]{1,0:T(8,128)(2,1)} custom-call(s32[1]{0:T(128)} %bitcast.core_ref, s32[4]{0:T(128)} %and_select_fusion.first_ref, s32[4,128]{1,0:T(4,128)} %copy-done.8, bf16[512,4096]{1,0:T(8,128)(2,1)} %copy-done.4, f32[512,128]{1,0:T(8,128)} %get-tuple-element.8.cos_ref, f32[512,128]{1,0:T(8,128)} %get-tuple-element.9.sin_ref, ...), custom_call_target="tpu_custom_call" | custom-call | flops 3221225472 | bytes 8388608 | tf_op jit(solution)/shard_map/pallas_call | solution.py:214
  (9 shorter events, 0.0 us)
Async XLA Ops:
  34.9 9.6 %copy-start.7 = (bf16[4096]{0:T(1024)(128)(2,1)S(1)}, bf16[4096]{0:T(1024)(128)(2,1)}, u32[]{:S(2)}) copy-start(bf16[4096]{0:T(1024)(128)(2,1)} %param.7) | copy-start | bytes 24580
  34.9 13.2 %all-to-all-start = ((bf16[4,16,32,256]{3,2,1,0:T(8,128)(2,1)}), bf16[4,16,32,256]{3,2,1,0:T(8,128)(2,1)S(1)}, u32[]{:S(2)}, u32[]{:S(2)}) async-start(bf16[4,16,32,256]{3,2,1,0:T(8,128)(2,1)} %shard_map.64), calls=%async_computation | async-start | bytes 2097152 | tf_op jit(solution)/shard_map/all_to_all | solution.py:297
  39.4 5.1 %copy-start.5 = (bf16[512,4096]{1,0:T(8,128)(2,1)S(1)}, bf16[512,4096]{1,0:T(8,128)(2,1)}, u32[]{:S(2)}) copy-start(bf16[512,4096]{1,0:T(8,128)(2,1)} %param.6) | copy-start | bytes 12582916
  46.2 1.9 %copy-start.4 = (bf16[512,4096]{1,0:T(8,128)(2,1)}, bf16[512,4096]{1,0:T(8,128)(2,1)S(1)}, u32[]{:S(2)}) copy-start(bf16[512,4096]{1,0:T(8,128)(2,1)S(1)} %fusion.2.x_ref) | copy-start | bytes 12582916
  48.2 4.6 %copy-start = (bf16[4,16,32,256]{3,2,1,0:T(8,128)(2,1)}, bf16[4,16,32,256]{3,2,1,0:T(8,128)(2,1)S(1)}, u32[]{:S(2)}) copy-start(bf16[4,16,32,256]{3,2,1,0:T(8,128)(2,1)S(1)} %all-to-all-done.wa_ref.refs_2_) | copy-start | bytes 3145732
  48.2 34.9 %all-to-all-start.1 = ((bf16[4,16,32,512]{3,2,1,0:T(8,128)(2,1)}), bf16[4,16,32,512]{3,2,1,0:T(8,128)(2,1)S(1)}, u32[]{:S(2)}, u32[]{:S(2)}) async-start(bf16[4,16,32,512]{3,2,1,0:T(8,128)(2,1)} %shard_map.67), calls=%async_computation.1 | async-start | bytes 4194304 | tf_op jit(solution)/shard_map/all_to_all | solution.py:297
  52.7 14.4 %collective-permute-start = (bf16[4,16,32,256]{3,2,1,0:T(8,128)(2,1)S(1)}, bf16[4,16,32,256]{3,2,1,0:T(8,128)(2,1)}, u32[]{:S(2)}, u32[]{:S(2)}) collective-permute-start(bf16[4,16,32,256]{3,2,1,0:T(8,128)(2,1)S(1)} %all-to-all-done.wa_ref.refs_2_), channel_id=1, source_target_pairs={{0,16},{16,0},{32,48},{48,32},{64,80},{80,64},{96,112},{112,96},{1... | collective-permute-start | bytes 3145736 | tf_op jit(solution)/shard_map/ppermute | solution.py:301
  67.2 23.2 %copy-start.6 = (s32[1,2048]{1,0:T(1,128)S(1)}, s32[1,2048]{1,0:T(1,128)}, u32[]{:S(2)}) copy-start(s32[1,2048]{1,0:T(1,128)} %param.11) | copy-start | bytes 24580
  72.5 9.9 %collective-permute-start.2 = (bf16[512,256]{1,0:T(8,128)(2,1)}, bf16[512,256]{1,0:T(8,128)(2,1)S(1)}, u32[]{:S(2)}, u32[]{:S(2)}) collective-permute-start(bf16[512,256]{1,0:T(8,128)(2,1)} %shard_map.65.kv0_ref), channel_id=1, source_target_pairs={{0,1},{1,2},{2,3},{4,5},{5,6},{6,7},{8,9},{9,10},{10,11},{12,13},{... | collective-permute-start | bytes 786440 | tf_op jit(solution)/shard_map/ppermute | solution.py:326
  75.6 7.5 %collective-permute-start.1 = (bf16[512,256]{1,0:T(8,128)(2,1)}, bf16[512,256]{1,0:T(8,128)(2,1)S(1)}, u32[]{:S(2)}, u32[]{:S(2)}) collective-permute-start(bf16[512,256]{1,0:T(8,128)(2,1)} %shard_map.65.kv0_ref), channel_id=1, source_target_pairs={{0,2},{1,3},{4,6},{5,7},{8,10},{9,11},{12,14},{13,15},{16,18},{17,... | collective-permute-start | bytes 786440 | tf_op jit(solution)/shard_map/ppermute | solution.py:327
  82.4 11.9 %copy-start.2 = (bf16[512,256]{1,0:T(8,128)(2,1)}, bf16[512,256]{1,0:T(8,128)(2,1)S(1)}, u32[]{:S(2)}) copy-start(bf16[512,256]{1,0:T(8,128)(2,1)S(1)} %collective-permute-done.2.refs_1_.kv1_ref) | copy-start | bytes 786436
  83.1 11.2 %copy-start.3 = (bf16[512,256]{1,0:T(8,128)(2,1)}, bf16[512,256]{1,0:T(8,128)(2,1)S(1)}, u32[]{:S(2)}) copy-start(bf16[512,256]{1,0:T(8,128)(2,1)S(1)} %collective-permute-done.1.refs_2_.kv2_ref) | copy-start | bytes 786436
  83.1 11.2 %copy-start.1 = (bf16[4,16,32,512]{3,2,1,0:T(8,128)(2,1)}, bf16[4,16,32,512]{3,2,1,0:T(8,128)(2,1)S(1)}, u32[]{:S(2)}) copy-start(bf16[4,16,32,512]{3,2,1,0:T(8,128)(2,1)S(1)} %shard_map.68.wa_ref) | copy-start | bytes 6291460
  83.1 11.2 %collective-permute-start.3 = (bf16[4,16,32,512]{3,2,1,0:T(8,128)(2,1)S(1)}, bf16[4,16,32,512]{3,2,1,0:T(8,128)(2,1)}, u32[]{:S(2)}, u32[]{:S(2)}) collective-permute-start(bf16[4,16,32,512]{3,2,1,0:T(8,128)(2,1)S(1)} %shard_map.68.wa_ref), channel_id=1, source_target_pairs={{0,16},{16,0},{32,48},{48,32},{64,80},{80,64},{96,112},{112,96},{1... | collective-permute-start | bytes 6291464 | tf_op jit(solution)/shard_map/ppermute | solution.py:301
  91.0 3.3 %copy-start.8 = (s32[4,128]{1,0:T(4,128)}, s32[4,128]{1,0:T(4,128)S(1)}, u32[]{:S(2)}) copy-start(s32[4,128]{1,0:T(4,128)S(1)} %maximum_bitcast_fusion.low_ref) | copy-start | bytes 6148
